TPU v7x, 128 devices: a whole 4x4x4 slice. The times are simulated.
128 devices in a mesh: rep: 2 (over z_hi), fsdp: 64 (over z_lo, x, y, core).
Axes of the slice: x: 4, y: 4, z: 4 (z_hi: 2, z_lo: 2; z = z_hi * 2 + z_lo), core: 2. Of those that a mesh axis runs over, the one named last changes fastest.
Arguments:
- tokens: bfloat16 [32768, 1024], P(('rep', 'fsdp')), may hold values from -6 to 6
- gain_first: bfloat16 [1024], P('fsdp'), may hold values from 0.099609375 to 1.8984375
- w_in: bfloat16 [1024, 3072], P('fsdp'), may hold values from -0.1875 to 0.1875
- conv_weight: bfloat16 [1024, 3], P('fsdp'), may hold values from -3.5 to 3.5
- w_out: bfloat16 [1024, 1024], P('fsdp'), may hold values from -0.1875 to 0.1875
- gain_second: bfloat16 [1024], P('fsdp'), may hold values from 0.099609375 to 1.8984375
- w_gate: bfloat16 [1024, 4608], P('fsdp'), may hold values from -0.1875 to 0.1875
- w_up: bfloat16 [1024, 4608], P('fsdp'), may hold values from -0.1875 to 0.1875
- w_down: bfloat16 [4608, 1024], P('fsdp'), may hold values from -0.09375 to 0.09375
- cotangent: bfloat16 [32768, 1024], P(('rep', 'fsdp')), may hold values from -6 to 6
Outputs:
- result: bfloat16 [32768, 1024], P(('rep', 'fsdp'))
- grad_tokens: float32 [32768, 1024], P(('rep', 'fsdp'))
- grad_gain_first: float32 [1024], P('fsdp')
- grad_w_in: float32 [1024, 3072], P('fsdp')
- grad_conv_weight: float32 [1024, 3], P('fsdp')
- grad_w_out: float32 [1024, 1024], P('fsdp')
- grad_gain_second: float32 [1024], P('fsdp')
- grad_w_gate: float32 [1024, 4608], P('fsdp')
- grad_w_up: float32 [1024, 4608], P('fsdp')
- grad_w_down: float32 [4608, 1024], P('fsdp')
All inputs are finite; a program needn't handle non-finite values.
Results may differ from a plain program's by a relative error of at most 0.012.
Values may be sent and summed in bfloat16 or wider, within the bound.
No kernel may reach another device: no remote copies, remote signals or barrier semaphores. Data moves between devices by JAX's collectives and lax.ppermute only.
A program may use at most 256 MiB of HBM per device.

v0:
```python
import jax
import jax.numpy as jnp
from jax import lax
from jax.experimental import pallas as pl
from jax.experimental.pallas import tpu as pltpu
from jax.sharding import PartitionSpec as P

epsilon = 1e-05

SIDE = 4
PLANE = SIDE * SIDE
HALF = PLANE * 2
SPARE = 128
CHUNK = 256
VMEM_BYTES = 56 * 1024 * 1024


def place(z, plane, core):
    return (z * PLANE + plane) * 2 + core


def moves(target):
    return [
        (place(z, plane, core), place(*target(z, plane, core)))
        for z in range(2)
        for plane in range(PLANE)
        for core in range(2)
    ]


TO_CORE = moves(lambda z, plane, core: (z, plane, 1 - core))
TO_Z = moves(lambda z, plane, core: (1 - z, plane, core))
TO_NEXT = moves(lambda z, plane, core: (z, (plane + 1) % PLANE, core))
TO_PREVIOUS = moves(lambda z, plane, core: (z, (plane - 1) % PLANE, core))
TEAMS = [
    [place(z, plane, core) for z in range(2) for core in range(2)] for plane in range(PLANE)
]
PLANES = [
    [place(z, plane, core) for plane in range(PLANE)] for z in range(2) for core in range(2)
]
BOTH_TEAMS = [[rep * 2 * HALF + member for rep in range(2) for member in team] for team in TEAMS]


def to_core(value):
    return lax.ppermute(value, "fsdp", TO_CORE)


def to_z(value):
    return lax.ppermute(value, "fsdp", TO_Z)


def norm_scale(values):
    return lax.rsqrt(jnp.mean(values * values, axis=-1, keepdims=True) + epsilon)


def norm_back(grad_normed, values, scale):
    inner = jnp.mean(grad_normed * values, axis=-1, keepdims=True)
    return scale * (grad_normed - values * scale * scale * inner)


def contract_rows(left, right):
    return lax.dot_general(
        left, right, (((0,), (0,)), ((), ())), preferred_element_type=jnp.float32
    )


def contract_cols(left, right):
    return lax.dot_general(
        left, right, (((1,), (1,)), ((), ())), preferred_element_type=jnp.float32
    )


def by_member(shard, parts):
    rows, columns = shard.shape
    split = shard.reshape(rows, parts, 2, PLANE, 2, -1)
    return split.transpose(2, 4, 0, 1, 3, 5).reshape(4, rows, columns // 4)


def from_members(blocks, parts):
    members, rows, columns = blocks.shape
    split = blocks.reshape(2, 2, rows, parts, PLANE, -1)
    return split.transpose(2, 3, 0, 4, 1, 5).reshape(rows, 4 * columns)


def team_swap(blocks):
    return lax.all_to_all(blocks, "fsdp", 0, 0, tiled=True, axis_index_groups=TEAMS)


def plane_swap(blocks):
    return lax.all_to_all(blocks, "fsdp", 0, 0, tiled=True, axis_index_groups=PLANES)


def gather_rows(blocks):
    members, rows, columns = blocks.shape
    return lax.all_gather(
        blocks.reshape(2, 2 * rows, columns),
        "fsdp",
        axis=1,
        tiled=True,
        axis_index_groups=PLANES,
    ).reshape(-1, columns)


def scatter_rows(value):
    total, columns = value.shape
    return lax.psum_scatter(
        value.reshape(2, total // 2, columns),
        "fsdp",
        scatter_dimension=1,
        tiled=True,
        axis_index_groups=PLANES,
    ).reshape(4, -1, columns)


def slots_of(pair, other):
    return jnp.stack([pair[0], other[0], pair[1], other[1]])


def core_sum(keep, sent):
    return keep + to_core(sent).astype(jnp.float32)


def own_sum(keep, sent):
    pair = core_sum(keep, sent)
    return pair[0] + to_z(pair[1].astype(jnp.bfloat16)).astype(jnp.float32)


def whole(*shape):
    return pl.BlockSpec(shape, lambda *_: (0,) * len(shape))


def per_slot(length, width, column=0):
    return pl.BlockSpec((1, length, width), lambda slot: (slot, 0, column))


def per_pair(length, width):
    return pl.BlockSpec((1, length, width), lambda slot: (slot // 2, 0, 0))


def pair_of_values(length, width, which):
    return pl.BlockSpec((1, 1, length, width), lambda slot: (slot // 2, which, 0, 0))


def run(kernel, grid, in_specs, out_specs, out_shape, scratch, flops, values):
    moved = 0 if flops == 0 else sum(value.size * value.dtype.itemsize for value in values)
    moved += 0 if flops == 0 else sum(value.size * value.dtype.itemsize for value in out_shape)
    return pl.pallas_call(
        kernel,
        grid=grid,
        in_specs=in_specs,
        out_specs=out_specs,
        out_shape=out_shape,
        scratch_shapes=scratch,
        compiler_params=pltpu.CompilerParams(vmem_limit_bytes=VMEM_BYTES),
        cost_estimate=pl.CostEstimate(flops=flops, bytes_accessed=moved, transcendentals=0),
    )(*values)


def array(shape, kind):
    return jax.ShapeDtypeStruct(shape, kind)


def pick(slot, even, odd):
    return jnp.where(slot % 2 == 0, even, odd)


def shifted_in(values, first_rows, steps):
    moved = pltpu.roll(values, steps, 0)
    row = lax.broadcasted_iota(jnp.int32, values.shape, 0)
    for index in range(steps):
        moved = jnp.where(row == index, first_rows[2 - steps + index :][:1], moved)
    return moved


def shifted_out(values, next_rows, steps):
    length = values.shape[0]
    moved = pltpu.roll(values, length - steps, 0)
    row = lax.broadcasted_iota(jnp.int32, values.shape, 0)
    for index in range(steps):
        moved = jnp.where(row == length - steps + index, next_rows[index : index + 1], moved)
    return moved


def store_pair(slot, value, keep_ref, sent_ref):
    @pl.when(slot % 2 == 0)
    def _():
        keep_ref[0] = value

    @pl.when(slot % 2 == 1)
    def _():
        sent_ref[0] = value.astype(sent_ref.dtype)


def project_kernel(
    pair_ref, other_ref, first_ref,
    normed_ref, proj_ref, mixed_ref, in_ref, out_ref, gains_ref, taps_ref,
    column, taps_column,
):
    slot = pl.program_id(0)
    width = in_ref.shape[1]
    channels = width // 3
    rows = channels // PLANE

    @pl.when(slot == 0)
    def _():
        for plane in range(PLANE):
            for z in range(2):
                at = pl.ds((z * PLANE + plane) * 2 * rows, 2 * rows)
                source = pl.ds(z * 2 * rows, 2 * rows)
                in_ref[at, :] = first_ref[plane, source, :width]
                column[at, :] = first_ref[plane, source, width + channels :].astype(jnp.float32)
            at = pl.ds(plane * rows, rows)
            for part in range(4):
                out_ref[at, part * channels : (part + 1) * channels] = first_ref[
                    plane, pl.ds(part * rows, rows), width : width + channels
                ]
            taps_column[at, :] = first_ref[plane, :rows, width + channels :].astype(jnp.float32)
        gains_ref[...] = column[...].T[:8]
        taps_ref[...] = taps_column[...].T[:8]

    values = pick(slot, pair_ref[0, 0], other_ref[0, 0]).astype(jnp.float32)
    normed = (values * norm_scale(values) * gains_ref[0:1]).astype(jnp.bfloat16)
    normed_ref[0] = normed
    projected = jnp.dot(normed, in_ref[...], preferred_element_type=jnp.float32)
    proj_ref[0] = projected
    mixed = projected[:, :channels] * projected[:, 2 * channels :]
    mixed_ref[0] = mixed.astype(jnp.bfloat16)


def branch_kernel(
    mixed_ref, earlier_ref, out_gate_ref, taps_ref, out_ref,
    convolved_ref, gated_ref, keep_ref, sent_ref,
):
    slot = pl.program_id(0)
    mixed = mixed_ref[0].astype(jnp.float32)
    earlier = earlier_ref[0]
    convolved = (
        taps_ref[2:3] * mixed
        + taps_ref[3:4] * shifted_in(mixed, earlier, 1)
        + taps_ref[4:5] * shifted_in(mixed, earlier, 2)
    )
    convolved_ref[0] = convolved
    gated = (out_gate_ref[0] * convolved).astype(jnp.bfloat16)
    gated_ref[0] = gated
    branch = jnp.dot(gated, out_ref[...], preferred_element_type=jnp.float32)
    store_pair(slot, branch, keep_ref, sent_ref)


def ff_kernel(
    own_ref, swap_ref, pair_ref, other_ref, weights_ref, down_ref,
    hidden_ref, grad_gate_ref, grad_up_ref, keep_ref, sent_ref,
):
    slot = pl.program_id(0)
    units = down_ref.shape[0]
    normed = pick(slot, own_ref[0], swap_ref[0])
    outer = pick(slot, pair_ref[0, 0], other_ref[0, 0])
    for start in range(0, units, CHUNK):
        lanes = slice(start, min(start + CHUNK, units))
        up_lanes = slice(units + lanes.start, units + lanes.stop)
        gate = jnp.dot(normed, weights_ref[:, lanes], preferred_element_type=jnp.float32)
        up = jnp.dot(normed, weights_ref[:, up_lanes], preferred_element_type=jnp.float32)
        grad = contract_cols(outer, down_ref[lanes, :])
        sigmoid = jax.nn.sigmoid(gate)
        silu = gate * sigmoid
        hidden_ref[0, :, lanes] = (silu * up).astype(jnp.bfloat16)
        grad_gate = grad * up * sigmoid * (1.0 + gate * (1.0 - sigmoid))
        grad_gate_ref[0, :, lanes] = grad_gate.astype(jnp.bfloat16)
        grad_up_ref[0, :, lanes] = (grad * silu).astype(jnp.bfloat16)
    term = contract_cols(grad_gate_ref[0], weights_ref[:, :units])
    term += contract_cols(grad_up_ref[0], weights_ref[:, units : 2 * units])
    store_pair(slot, term, keep_ref, sent_ref)


def ff_grads_kernel(
    own_ref, swap_ref, pair_ref, other_ref, hidden_ref, grad_gate_ref, grad_up_ref, down_ref,
    pack_ref, keep_ref, sent_ref,
    gate_total, up_total, down_total,
):
    slot = pl.program_id(0)
    width, units = gate_total.shape
    each = units // PLANE
    block = width // PLANE
    rest = each - block
    normed = pick(slot, own_ref[0], swap_ref[0])
    outer = pick(slot, pair_ref[0, 0], other_ref[0, 0])

    @pl.when(slot == 0)
    def _():
        gate_total[...] = jnp.zeros_like(gate_total)
        up_total[...] = jnp.zeros_like(up_total)
        down_total[...] = jnp.zeros_like(down_total)

    gate_total[...] += contract_rows(normed, grad_gate_ref[0])
    up_total[...] += contract_rows(normed, grad_up_ref[0])
    down_total[...] += contract_rows(hidden_ref[0], outer)
    term = jnp.dot(hidden_ref[0], down_ref[...], preferred_element_type=jnp.float32)
    store_pair(slot, term, keep_ref, sent_ref)

    @pl.when(slot == 3)
    def _():
        pack_ref[:, :units] = gate_total[...].astype(jnp.bfloat16)
        pack_ref[:, units : 2 * units] = up_total[...].astype(jnp.bfloat16)
        for plane in range(PLANE):
            start = plane * each
            for half in range(2):
                to = half * width // 2 + plane * block // 2
                pack_ref[to : to + block // 2, 2 * units : 2 * units + width] = down_total[
                    start + half * block // 2 : start + (half + 1) * block // 2
                ].astype(jnp.bfloat16)
                parts = block // rest // 2
                lanes = width * rest // block
                last = down_total[start + block : start + each]
                pieces = [
                    last[:, (half * parts + part) * lanes : (half * parts + part + 1) * lanes]
                    for part in range(parts)
                ]
                pack_ref[to : to + block // 2, 2 * units + width :] = jnp.concatenate(
                    pieces, 0
                ).astype(jnp.bfloat16)


def gated_back_kernel(
    own_ref, swap_ref, out_ref, convolved_ref, out_gate_ref, grad_out_ref, grad_conv_ref
):
    slot = pl.program_id(0)
    grad_gated = contract_cols(pick(slot, own_ref[0], swap_ref[0]), out_ref[...])
    grad_out_ref[0] = (grad_gated * convolved_ref[0]).astype(jnp.bfloat16)
    grad_conv_ref[0] = grad_gated * out_gate_ref[0]


def out_grads_kernel(
    own_ref, swap_ref, gated_ref, grad_conv_ref, mixed_ref, earlier_ref, gain_ref,
    part_ref, spare_ref,
    total, taps_rows, gain_rows,
):
    slot = pl.program_id(0)
    rows = spare_ref.shape[1] // 4
    channels = gated_ref.shape[2]

    @pl.when(slot == 0)
    def _():
        total[...] = jnp.zeros_like(total)
        taps_rows[...] = jnp.zeros_like(taps_rows)
        gain_rows[...] = jnp.zeros_like(gain_rows)
        gain_rows[1:2] = gain_ref[...]

    total[...] += contract_rows(gated_ref[0], pick(slot, own_ref[0], swap_ref[0]))
    grad_conv = grad_conv_ref[0]
    mixed = mixed_ref[0].astype(jnp.float32)
    earlier = earlier_ref[0]
    lagged = (mixed, shifted_in(mixed, earlier, 1), shifted_in(mixed, earlier, 2))
    for lag, value in enumerate(lagged):
        taps_rows[2 + lag : 3 + lag] += jnp.sum(grad_conv * value, axis=0, keepdims=True)

    @pl.when(slot == 3)
    def _():
        gain_column = gain_rows[...].T
        taps_column = taps_rows[...].T
        for plane in range(PLANE):
            at = slice(plane * rows, (plane + 1) * rows)
            for part in range(4):
                part_ref[plane, part * rows : (part + 1) * rows, :] = total[
                    at, part * channels : (part + 1) * channels
                ].astype(jnp.bfloat16)
            for z in range(2):
                start = (z * PLANE + plane) * 2 * rows
                spare_ref[plane, z * 2 * rows : (z + 1) * 2 * rows, :] = gain_column[
                    start : start + 2 * rows
                ]
            spare_ref[plane, :rows, :] += taps_column[at]


def project_back_kernel(
    grad_conv_ref, later_ref, proj_ref, grad_out_ref, normed_ref, in_ref, taps_ref,
    pair_ref, other_ref, part_ref, spare_ref,
    pack_ref, keep_ref, sent_ref,
    total, gain_rows,
):
    slot = pl.program_id(0)
    width = in_ref.shape[1]
    channels = width // 3
    rows = channels // PLANE

    @pl.when(slot == 0)
    def _():
        total[...] = jnp.zeros_like(total)
        gain_rows[...] = jnp.zeros_like(gain_rows)

    grad_conv, later = grad_conv_ref[0], later_ref[0]
    grad_mixed = (
        taps_ref[2:3] * grad_conv
        + taps_ref[3:4] * shifted_out(grad_conv, later, 1)
        + taps_ref[4:5] * shifted_out(grad_conv, later, 2)
    )
    grad_projected = jnp.concatenate(
        [
            (grad_mixed * proj_ref[0, :, 2 * channels :]).astype(jnp.bfloat16),
            grad_out_ref[0],
            (grad_mixed * proj_ref[0, :, :channels]).astype(jnp.bfloat16),
        ],
        1,
    )
    total[...] += contract_rows(normed_ref[0], grad_projected)
    grad_normed = contract_cols(grad_projected, in_ref[...])
    store_pair(slot, grad_normed, keep_ref, sent_ref)
    values = pick(slot, pair_ref[0, 0], other_ref[0, 0]).astype(jnp.float32)
    gain_rows[0:1] += jnp.sum(grad_normed * values * norm_scale(values), axis=0, keepdims=True)

    @pl.when(slot == 3)
    def _():
        gain_column = gain_rows[...].T
        for plane in range(PLANE):
            for z in range(2):
                start = (z * PLANE + plane) * 2 * rows
                to = slice(z * 2 * rows, (z + 1) * 2 * rows)
                pack_ref[plane, to, :width] = total[start : start + 2 * rows].astype(jnp.bfloat16)
                pack_ref[plane, to, width + channels :] = (
                    spare_ref[plane, to] + gain_column[start : start + 2 * rows]
                ).astype(jnp.bfloat16)
            pack_ref[plane, :, width : width + channels] = part_ref[plane]


def in_total_kernel(blocks_ref, total_ref, spare_ref):
    members, rows, width = blocks_ref.shape
    channels = total_ref.shape[1] // 12
    first = width - SPARE - 3 * channels
    unit = channels // PLANE
    source = lax.broadcasted_iota(jnp.int32, (channels, 2 * channels), 0)
    target = lax.broadcasted_iota(jnp.int32, (channels, 2 * channels), 1)
    for z in range(2):
        for part in range(3):
            total = jnp.zeros((rows, 2 * channels), jnp.float32)
            for core in range(2):
                placed = source // unit * (2 * unit) + core * unit + source % unit == target
                placed = placed.astype(jnp.float32).astype(jnp.bfloat16)
                for rep in range(2):
                    block = blocks_ref[rep * 4 + z * 2 + core]
                    total += jnp.dot(
                        block[:, first + part * channels : first + (part + 1) * channels],
                        placed,
                        preferred_element_type=jnp.float32,
                    )
            start = (part * 2 + z) * 2 * channels
            total_ref[:, start : start + 2 * channels] = total
    spare = jnp.zeros((rows, SPARE), jnp.float32)
    for member in range(members):
        spare += blocks_ref[member, :, width - SPARE :].astype(jnp.float32)
    spare_ref[...] = spare


def body(
    tokens, gain_first, w_in, conv_weight, w_out, gain_second, w_gate, w_up, w_down, cotangent
):
    low, wide = jnp.bfloat16, jnp.float32
    length, model_width = tokens.shape
    position = lax.axis_index("fsdp")
    core, plane, z = position % 2, position // 2 % PLANE, position // HALF
    rows = w_in.shape[0]
    channels = model_width // 4

    block = 4 * rows
    rest = w_down.shape[0] - block
    units = w_down.shape[0] * PLANE
    gains = jnp.pad(jnp.stack([gain_first, gain_second], 1), ((0, 0), (0, SPARE - 2)))
    gains = jnp.broadcast_to(gains, (4, rows, SPARE))
    swapped = team_swap(
        jnp.concatenate(
            [by_member(w_gate, 1), by_member(w_up, 1), by_member(w_in, 3), gains], 2
        )
    )
    down_main = w_down[:block].reshape(4, rows, model_width)
    down_rest = w_down[block:].reshape(rest, block // rest, -1).transpose(1, 0, 2)
    ff_all = gather_rows(
        jnp.concatenate(
            [swapped[:, :, : 2 * units], down_main, down_rest.reshape(4, rows, -1)], 2
        )
    )

    in_width = 3 * channels
    conv_lanes = jnp.pad(conv_weight, ((0, 0), (2, SPARE - 5)))
    first_pack = jnp.concatenate(
        [
            swapped[:, :, 2 * units : 2 * units + in_width],
            w_out.reshape(rows, 4, channels).transpose(1, 0, 2),
            swapped[:, :, 2 * units + in_width :] + conv_lanes,
        ],
        2,
    )
    first_all = plane_swap(jnp.broadcast_to(first_pack, (PLANE,) + first_pack.shape))
    first_all = first_all.reshape(PLANE, 4 * rows, -1)

    main_rows = ff_all[:, 2 * units : 2 * units + model_width].reshape(2, PLANE, 2 * rows, -1)
    main_rows = main_rows.transpose(1, 0, 2, 3).reshape(PLANE, block, model_width)
    rest_rows = ff_all[:, 2 * units + model_width :].reshape(2, PLANE, 2 * rows, -1)
    rest_rows = rest_rows.transpose(1, 0, 2, 3).reshape(PLANE, block // rest, rest, -1)
    rest_rows = rest_rows.transpose(0, 2, 1, 3).reshape(PLANE, rest, model_width)
    down_full = jnp.concatenate([main_rows, rest_rows], 1).reshape(units, model_width)

    pair = jnp.stack([tokens, cotangent])
    pair = jnp.stack([pair, to_z(pair)])
    other = to_core(pair)
    team_pairs = [pair_of_values(length, model_width, 0)] * 2
    slot_wide, slot_narrow = (4, length, model_width), (4, length, channels)
    pair_wide = (2, length, model_width)
    pairs = [per_pair(length, model_width)] * 2
    narrow = per_slot(length, channels)
    out_gate = per_slot(length, channels, 1)
    edge = per_slot(8, channels)
    out_matrix, in_matrix = whole(channels, model_width), whole(model_width, in_width)
    taps = whole(8, channels)
    unit = 2 * 4 * length * model_width * channels

    normed, projected, mixed, in_full, out_full, gains, kernel = run(
        project_kernel,
        (4,),
        team_pairs + [whole(*first_all.shape)],
        [
            per_slot(length, model_width),
            per_slot(length, in_width),
            narrow,
            in_matrix,
            out_matrix,
            whole(8, model_width),
            taps,
        ],
        [
            array(slot_wide, low),
            array((4, length, in_width), wide),
            array(slot_narrow, low),
            array((model_width, in_width), low),
            array((channels, model_width), low),
            array((8, model_width), wide),
            array((8, channels), wide),
        ],
        [pltpu.VMEM((model_width, SPARE), wide), pltpu.VMEM((channels, SPARE), wide)],
        3 * unit,
        [pair, other, first_all],
    )
    gain_one, gain_two = gains[0], gains[1]

    def by_core(first, second):
        return jnp.where(core == 0, first, second)

    tails = mixed[:, length - 2 :]
    sent = by_core(tails[1::2], tails[0::2])
    received = lax.ppermute(sent, "fsdp", TO_NEXT)
    nothing = jnp.zeros_like(received[0])
    shifted = jnp.where(
        z == 0, jnp.stack([nothing, received[0]]), jnp.stack([received[1], nothing])
    )
    before = jnp.where(plane == 0, shifted, received)
    own_before = by_core(before, tails[1::2])
    other_before = by_core(tails[0::2], before)
    earlier = jnp.stack([own_before[0], other_before[0], own_before[1], other_before[1]])
    earlier = jnp.pad(earlier.astype(wide), ((0, 0), (0, 6), (0, 0)))
    convolved, gated, branch_keep, branch_sent = run(
        branch_kernel,
        (4,),
        [narrow, edge, out_gate, taps, out_matrix],
        [narrow, narrow] + pairs,
        [
            array(slot_narrow, wide),
            array(slot_narrow, low),
            array(pair_wide, wide),
            array(pair_wide, low),
        ],
        [],
        unit,
        [mixed, earlier, projected, kernel, out_full],
    )
    branch_pair = core_sum(branch_keep, branch_sent)
    branch_other = to_z(branch_pair.astype(low))
    branch_other, down_full = lax.optimization_barrier((branch_other, down_full))
    inputs = pair[:, 0].astype(wide)
    middle = inputs + branch_pair + branch_other.astype(wide)[::-1]
    scale_two = norm_scale(middle)
    normed_two = (middle * scale_two * gain_two).astype(low)
    normed_swap = to_core(normed_two)

    outer_pairs = [pair_of_values(length, model_width, 1)] * 2
    unit_slot = per_slot(length, units)
    unit_shape = array((4, length, units), low)
    hidden, grad_gate, grad_upper, grad_keep, grad_sent = run(
        ff_kernel,
        (4,),
        pairs
        + outer_pairs
        + [whole(*ff_all.shape), whole(units, model_width)],
        [unit_slot] * 3 + pairs,
        [unit_shape] * 3 + [array(pair_wide, wide), array(pair_wide, low)],
        [],
        5 * 2 * 4 * length * model_width * units,
        [normed_two, normed_swap, pair, other, ff_all, down_full],
    )
    grad_pair = core_sum(grad_keep, grad_sent)
    grad_sent = grad_pair.astype(low)
    grad_other = to_z(grad_sent)

    grad_sent, hidden, grad_gate, grad_upper = lax.optimization_barrier(
        (grad_sent, hidden, grad_gate, grad_upper)
    )
    ff_grads, down_keep, down_sent = run(
        ff_grads_kernel,
        (4,),
        pairs + outer_pairs + [unit_slot] * 3 + [whole(units, model_width)],
        [whole(*ff_all.shape)] + pairs,
        [array(ff_all.shape, low), array(pair_wide, wide), array(pair_wide, low)],
        [
            pltpu.VMEM((model_width, units), wide),
            pltpu.VMEM((model_width, units), wide),
            pltpu.VMEM((units, model_width), wide),
        ],
        0,
        [normed_two, normed_swap, pair, other, hidden, grad_gate, grad_upper, down_full],
    )
    ff_share = scatter_rows(ff_grads)
    grad_other, down_keep = lax.optimization_barrier((grad_other, down_keep))
    grad_normed_two = grad_pair + grad_other.astype(wide)[::-1]
    grad_gain_two = jnp.sum(grad_normed_two[0] * middle[0] * scale_two[0], axis=0)
    outer = pair[:, 1].astype(wide)
    grad_middle = outer + norm_back(grad_normed_two * gain_two, middle, scale_two)
    grad_branch = grad_middle.astype(low)
    grad_swap = to_core(grad_branch)

    grad_out, grad_conv = run(
        gated_back_kernel,
        (4,),
        pairs + [out_matrix, narrow, out_gate],
        [narrow, narrow],
        [array(slot_narrow, low), array(slot_narrow, wide)],
        [],
        unit,
        [grad_branch, grad_swap, out_full, convolved, projected],
    )
    heads = grad_conv[:, :2]
    sent = by_core(heads[0::2], heads[1::2])
    received = lax.ppermute(sent, "fsdp", TO_PREVIOUS)
    nothing = jnp.zeros_like(received[0])
    shifted = jnp.where(
        z == 0, jnp.stack([received[1], nothing]), jnp.stack([nothing, received[0]])
    )
    after = jnp.where(plane == PLANE - 1, shifted, received)
    own_after = by_core(heads[1::2], after)
    other_after = by_core(after, heads[0::2])
    later = jnp.stack([own_after[0], other_after[0], own_after[1], other_after[1]])
    later = jnp.pad(later, ((0, 0), (0, 6), (0, 0)))
    part_shape, spare_shape = (PLANE, 4 * rows, channels), (PLANE, 4 * rows, SPARE)
    out_part, spare_part = run(
        out_grads_kernel,
        (4,),
        pairs + [narrow, narrow, narrow, edge, whole(1, model_width)],
        [whole(*part_shape), whole(*spare_shape)],
        [array(part_shape, low), array(spare_shape, wide)],
        [
            pltpu.VMEM((channels, model_width), wide),
            pltpu.VMEM((SPARE, channels), wide),
            pltpu.VMEM((SPARE, model_width), wide),
        ],
        unit,
        [grad_branch, grad_swap, gated, grad_conv, mixed, earlier, grad_gain_two[None]],
    )
    first_grads, normed_keep, normed_sent = run(
        project_back_kernel,
        (4,),
        [
            narrow,
            edge,
            per_slot(length, in_width),
            narrow,
            per_slot(length, model_width),
            in_matrix,
            taps,
        ]
        + team_pairs
        + [whole(*part_shape), whole(*spare_shape)],
        [whole(*first_all.shape)] + pairs,
        [array(first_all.shape, low), array(pair_wide, wide), array(pair_wide, low)],
        [pltpu.VMEM((model_width, in_width), wide), pltpu.VMEM((SPARE, model_width), wide)],
        6 * unit,
        [
            grad_conv,
            later,
            projected,
            grad_out,
            normed,
            in_full,
            kernel,
            pair,
            other,
            out_part,
            spare_part,
        ],
    )
    first_grads = first_grads.reshape(PLANE, 4, rows, -1)
    first_arrived = plane_swap(first_grads)

    down_sent, normed_sent = lax.optimization_barrier((down_sent, normed_sent))
    result = middle[0] + own_sum(down_keep, down_sent)
    grad_normed_own = own_sum(normed_keep, normed_sent)
    grad_inputs = grad_middle[0] + norm_back(
        grad_normed_own * gain_one, inputs[0], norm_scale(inputs[0])
    )
    result, grad_inputs, first_arrived = lax.optimization_barrier(
        (result.astype(low), grad_inputs, first_arrived)
    )
    first_share = jnp.sum(first_arrived.astype(wide), axis=0).astype(low)

    def both_reps(value):
        other = lax.ppermute(value, "rep", [(0, 1), (1, 0)])
        return value.astype(wide) + other.astype(wide)

    down_total = both_reps(ff_share[:, :, 2 * units :])
    down_rest = down_total[:, :, model_width:].reshape(block // rest, rest, -1)
    down_rest = down_rest.transpose(1, 0, 2).reshape(rest, model_width)
    down_total = jnp.concatenate(
        [down_total[:, :, :model_width].reshape(block, model_width), down_rest], 0
    )
    out_total = both_reps(first_share[:, :, in_width:])
    conv_total = out_total[0, :, channels + 2 : channels + 5]
    out_total = out_total[:, :, :channels].transpose(1, 0, 2).reshape(rows, model_width)
    blocks = jnp.concatenate(
        [
            ff_share[:, :, : 2 * units],
            first_share[:, :, :in_width],
            first_share[:, :, in_width + channels :],
        ],
        2,
    )
    blocks = lax.all_to_all(
        jnp.concatenate([blocks, blocks]),
        ("rep", "fsdp"),
        0,
        0,
        tiled=True,
        axis_index_groups=BOTH_TEAMS,
    )
    in_total, gain_total = run(
        in_total_kernel,
        (1,),
        [whole(*blocks.shape)],
        [whole(rows, w_in.shape[1]), whole(rows, SPARE)],
        [array((rows, w_in.shape[1]), wide), array((rows, SPARE), wide)],
        [],
        unit,
        [blocks],
    )
    ff_total = blocks[:, :, : 2 * units].astype(wide)
    ff_total = ff_total[:4] + ff_total[4:]

    return (
        result,
        grad_inputs,
        gain_total[:, 0],
        in_total,
        conv_total,
        out_total,
        gain_total[:, 1],
        from_members(ff_total[:, :, :units], 1),
        from_members(ff_total[:, :, units:], 1),
        down_total,
    )


def solution(mesh):
    return jax.shard_map(
        body,
        mesh=mesh,
        in_specs=(
            P(("rep", "fsdp"), None),
            P("fsdp"),
            P("fsdp", None),
            P("fsdp", None),
            P("fsdp", None),
            P("fsdp"),
            P("fsdp", None),
            P("fsdp", None),
            P("fsdp", None),
            P(("rep", "fsdp"), None),
        ),
        out_specs=(
            P(("rep", "fsdp"), None),
            P(("rep", "fsdp"), None),
            P("fsdp"),
            P("fsdp", None),
            P("fsdp", None),
            P("fsdp", None),
            P("fsdp"),
            P("fsdp", None),
            P("fsdp", None),
            P("fsdp", None),
        ),
        check_vma=False,
    )
```

profile of v0, /device:TPU:1, one launch (start us, length us, event | category | flops | bytes accessed | tf_op | source)
XLA Modules:
  0.0 332.8 jit_solution(4882543948325885872)
XLA Ops:
  7.2 1.5 reshape.162
  11.4 0.8 pad_maximum_fusion.4
  12.2 4.8 %all-to-all-start = ((bf16[4,16,3200]{2,1,0:T(8,128)(2,1)}), bf16[4,16,3200]{2,1,0:T(8,128)(2,1)S(1)}, u32[]{:S(2)}, u32[]{:S(2)}) async-start(bf16[4,16,3200]{2,1,0:T(8,128)(2,1)} %pad_maximum_fusion.4), calls=%async_computation | async-start | bytes 819200 | tf_op jit(solution)/shard_map/all_to_all | solution.py:86
  17.1 6.7 %all-to-all-done = bf16[4,16,3200]{2,1,0:T(8,128)(2,1)S(1)} async-done(((bf16[4,16,3200]{2,1,0:T(8,128)(2,1)}), bf16[4,16,3200]{2,1,0:T(8,128)(2,1)S(1)}, u32[]{:S(2)}, u32[]{:S(2)}) %all-to-all-start) | async-done | bytes 409632 | tf_op jit(solution)/shard_map/all_to_all | solution.py:86
  25.3 1.4 copy.51
  28.2 1.7 broadcast_in_dim.7
  29.9 6.9 %all-to-all-start.1 = ((bf16[16,4,16,1152]{3,2,1,0:T(8,128)(2,1)}), bf16[16,4,16,1152]{3,2,1,0:T(8,128)(2,1)}, u32[]{:S(2)}, u32[]{:S(2)}) async-start(bf16[16,4,16,1152]{3,2,1,0:T(8,128)(2,1)} %broadcast_in_dim.7), calls=%async_computation.1 | async-start | bytes 4718592 | tf_op jit(solution)/shard_map/all_to_all | solution.py:90
  36.9 12.0 %collective-permute-done = bf16[2,256,1024]{2,1,0:T(8,128)(2,1)S(1)} collective-permute-done((bf16[2,256,1024]{2,1,0:T(8,128)(2,1)S(1)}, bf16[2,256,1024]{2,1,0:T(8,128)(2,1)S(1)}, u32[]{:S(2)}, u32[]{:S(2)}) %collective-permute-start) | collective-permute-done | bytes 1048608 | tf_op jit(solution)/shard_map/ppermute | solution.py:49
  48.8 1.0 copy-done.1
  49.8 1.4 pad_maximum_fusion.pair_ref
  51.2 1.7 collective-permute-start.1
  53.0 23.5 %all-to-all-done.1 = bf16[16,4,16,1152]{3,2,1,0:T(8,128)(2,1)} async-done(((bf16[16,4,16,1152]{3,2,1,0:T(8,128)(2,1)}), bf16[16,4,16,1152]{3,2,1,0:T(8,128)(2,1)}, u32[]{:S(2)}, u32[]{:S(2)}) %all-to-all-start.1) | async-done | bytes 2359328 | tf_op jit(solution)/shard_map/all_to_all | solution.py:90
  76.5 7.7 %shard_map.177 = (bf16[4,256,1024]{2,1,0:T(8,128)(2,1)}, f32[4,256,768]{2,1,0:T(8,128)}, bf16[4,256,256]{2,1,0:T(8,128)(2,1)}, bf16[1024,768]{1,0:T(8,128)(2,1)}...) custom-call(bf16[2,2,256,1024]{3,2,1,0:T(8,128)(2,1)} %copy-done, ...), custom_call_target="tpu_custom_call" | custom-call | flops 1610612736 | bytes 14458880 | tf_op jit(solution)/shard_map/pallas_call | solution.py:147
  85.3 5.5 %collective-permute-done.2 = bf16[2,2,256]{2,1,0:T(2,128)(2,1)S(1)} collective-permute-done((bf16[2,2,256]{2,1,0:T(2,128)(2,1)S(1)}, bf16[2,2,256]{2,1,0:T(2,128)(2,1)S(1)}, u32[]{:S(2)}, u32[]{:S(2)}) %collective-permute-start.2) | collective-permute-done | bytes 2080 | tf_op jit(solution)/shard_map/ppermute | solution.py:546
  91.5 5.6 %shard_map.178 = (f32[4,256,256]{2,1,0:T(8,128)}, bf16[4,256,256]{2,1,0:T(8,128)(2,1)}, f32[2,256,1024]{2,1,0:T(8,128)}, bf16[2,256,1024]{2,1,0:T(8,128)(2,1)}) custom-call(bf16[4,256,256]{2,1,0:T(8,128)(2,1)} %get-tuple-element.50.mixed_ref, f32[4,8,256]{2,1,0:T(8,128)} %fusion.25.earlier_ref, f32[4,256,768]{2,1,0:T(8,128)} %get-tuple-element.51.out_gate_ref.proj_ref, ...), custom_call_target="tpu_custom_call" | custom-call | flops 536870912 | bytes 8953856 | tf_op jit(solution)/shard_map/pallas_call | solution.py:147
  97.1 3.3 collective-permute-start.3
  100.4 2.5 collective-permute-done.3
  102.9 2.4 fusion.1
  105.3 1.5 collective-permute-start.4
  106.9 0.8 fusion.30
  107.7 10.0 %all-gather.2.cloned.1.call-done = bf16[2,512,3456]{2,1,0:T(8,128)(2,1)} async-done(((bf16[2,32,3456]{2,1,0:T(8,128)(2,1)}), bf16[2,512,3456]{2,1,0:T(8,128)(2,1)}) %all-gather.2.cloned.1.call-update) | async-done | bytes 7077904 | tf_op jit(solution)/shard_map/all_gather | solution.py:95
  117.6 1.8 slice.237
  119.4 1.0 slice.238
  120.7 1.7 pad_maximum_fusion.1
  122.4 7.4 %collective-permute-done.4 = bf16[2,256,1024]{2,1,0:T(8,128)(2,1)S(1)} collective-permute-done((bf16[2,256,1024]{2,1,0:T(8,128)(2,1)S(1)}, bf16[2,256,1024]{2,1,0:T(8,128)(2,1)S(1)}, u32[]{:S(2)}, u32[]{:S(2)}) %collective-permute-start.4) | collective-permute-done | bytes 1048608 | tf_op jit(solution)/shard_map/ppermute | solution.py:49
  131.0 1.4 collective-permute-start.5
  132.3 2.3 collective-permute-done.5.swap_ref
  134.6 1.0 copy-done.17
  135.6 21.2 %shard_map.179 = (bf16[4,256,1152]{2,1,0:T(8,128)(2,1)}, bf16[4,256,1152]{2,1,0:T(8,128)(2,1)}, bf16[4,256,1152]{2,1,0:T(8,128)(2,1)}, f32[2,256,1024]{2,1,0:T(8,128)}, bf16[2,256,1024]{2,1,0:T(8,128)(2,1)}) custom-call(bf16[2,256,1024]{2,1,0:T(8,128)(2,1)} %copy-done.14, bf16[2,256,1024]{2,1,0:T(8,128)(2,1)} %copy-done.17, ...), custom_call_target="tpu_custom_call" | custom-call | flops 12079595520 | bytes 25952256 | tf_op jit(solution)/shard_map/pallas_call | solution.py:147
  157.2 2.5 collective-permute-done.6
  159.7 3.3 %fusion.2 = bf16[2,256,1024]{2,1,0:T(8,128)(2,1)} fusion(f32[2,256,1024]{2,1,0:T(8,128)} %get-tuple-element.59, bf16[2,256,1024]{2,1,0:T(8,128)(2,1)S(1)} %collective-permute-done.6), kind=kLoop, calls=%fused_computation.18 | loop fusion | flops 1572864 | bytes 4194304 | tf_op jit(solution)/shard_map/convert_element_type | solution.py:596
  163.0 20.3 %shard_map.180 = (bf16[1024,3456]{1,0:T(8,128)(2,1)}, f32[2,256,1024]{2,1,0:T(8,128)}, bf16[2,256,1024]{2,1,0:T(8,128)(2,1)}) custom-call(bf16[2,256,1024]{2,1,0:T(8,128)(2,1)} %copy-done.14, bf16[2,256,1024]{2,1,0:T(8,128)(2,1)} %copy-done.17, bf16[2,2,256,1024]{3,2,1,0:T(8,128)(2,1)} %copy-done, ...), custom_call_target="tpu_custom_call" | custom-call | tf_op jit(solution)/shard_map/pallas_call | solution.py:147
  183.4 1.5 collective-permute-start.7
  184.9 23.2 %collective-permute-done.7 = bf16[2,256,1024]{2,1,0:T(8,128)(2,1)S(1)} collective-permute-done((bf16[2,256,1024]{2,1,0:T(8,128)(2,1)}, bf16[2,256,1024]{2,1,0:T(8,128)(2,1)S(1)}, u32[]{:S(2)}, u32[]{:S(2)}) %collective-permute-start.7) | collective-permute-done | bytes 1048608 | tf_op jit(solution)/shard_map/ppermute | solution.py:49
  209.7 2.4 fusion.27
  212.0 1.1 collective-permute-start.8
  213.1 2.1 fusion.15
  215.8 5.1 %shard_map.181 = (bf16[4,256,256]{2,1,0:T(8,128)(2,1)}, f32[4,256,256]{2,1,0:T(8,128)}) custom-call(bf16[2,256,1024]{2,1,0:T(8,128)(2,1)} %get-tuple-element.94.own_ref, bf16[2,256,1024]{2,1,0:T(8,128)(2,1)} %collective-permute-done.8.swap_ref, bf16[256,1024]{1,0:T(8,128)(2,1)} %get-tuple-element.53.out_ref, f32[4,256,256]{2,1,0:T(8,128)} %get-tuple-element.71.convolved_ref, ...), custom_call_target="tpu_custom_call" | custom-call | flops 536870912 | bytes 8388608 | tf_op jit(solution)/shard_map/pallas_call | solution.py:147
  221.7 5.4 %shard_map.182 = (bf16[16,64,256]{2,1,0:T(8,128)(2,1)}, f32[16,64,128]{2,1,0:T(8,128)}) custom-call(bf16[2,256,1024]{2,1,0:T(8,128)(2,1)} %get-tuple-element.94.own_ref, bf16[2,256,1024]{2,1,0:T(8,128)(2,1)} %collective-permute-done.8.swap_ref, bf16[4,256,256]{2,1,0:T(8,128)(2,1)} %get-tuple-element.76.gated_ref, ...), custom_call_target="tpu_custom_call" | custom-call | flops 536870912 | bytes 5279744 | tf_op jit(solution)/shard_map/pallas_call | solution.py:147
  227.8 11.8 %shard_map.183 = (bf16[16,64,1152]{2,1,0:T(8,128)(2,1)}, f32[2,256,1024]{2,1,0:T(8,128)}, bf16[2,256,1024]{2,1,0:T(8,128)(2,1)}) custom-call(f32[4,256,256]{2,1,0:T(8,128)} %get-tuple-element.72.grad_conv_ref, f32[4,8,256]{2,1,0:T(8,128)} %select_maximum_fusion.later_ref, f32[4,256,768]{2,1,0:T(8,128)} %get-tuple-element.51.out_gate_ref.proj_ref, ...), custom_call_target="tpu_custom_call" | custom-call | flops 3221225472 | bytes 19177472 | tf_op jit(solution)/shard_map/pallas_call | solution.py:147
  240.4 1.5 fusion.4
  241.9 4.5 %all-to-all-start.2 = ((bf16[16,4,16,1152]{3,2,1,0:T(8,128)(2,1)}), bf16[16,4,16,1152]{3,2,1,0:T(8,128)(2,1)}, u32[]{:S(2)}, u32[]{:S(2)}) async-start(bf16[16,4,16,1152]{3,2,1,0:T(8,128)(2,1)} %bitcast.148), calls=%async_computation.2 | async-start | bytes 4718592 | tf_op jit(solution)/shard_map/all_to_all | solution.py:90
  246.4 2.3 convert_add_fusion.1
  248.8 1.5 collective-permute-start.13
  250.3 1.7 convert_add_fusion.2
  252.3 9.7 %collective-permute-done.13 = bf16[256,1024]{1,0:T(8,128)(2,1)S(1)} collective-permute-done((bf16[256,1024]{1,0:T(8,128)(2,1)S(1)}, bf16[256,1024]{1,0:T(8,128)(2,1)S(1)}, u32[]{:S(2)}, u32[]{:S(2)}) %collective-permute-start.13) | collective-permute-done | bytes 524320 | tf_op jit(solution)/shard_map/ppermute | solution.py:49
  262.5 10.8 %collective-permute-done.11 = bf16[256,1024]{1,0:T(8,128)(2,1)S(1)} collective-permute-done((bf16[256,1024]{1,0:T(8,128)(2,1)S(1)}, bf16[256,1024]{1,0:T(8,128)(2,1)S(1)}, u32[]{:S(2)}, u32[]{:S(2)}) %collective-permute-start.11) | collective-permute-done | bytes 524320 | tf_op jit(solution)/shard_map/ppermute | solution.py:49
  273.3 1.1 fusion.12
  274.4 1.3 fusion.9
  275.7 6.8 %all-to-all-done.2 = bf16[16,4,16,1152]{3,2,1,0:T(8,128)(2,1)} async-done(((bf16[16,4,16,1152]{3,2,1,0:T(8,128)(2,1)}), bf16[16,4,16,1152]{3,2,1,0:T(8,128)(2,1)}, u32[]{:S(2)}, u32[]{:S(2)}) %all-to-all-start.2) | async-done | bytes 2359328 | tf_op jit(solution)/shard_map/all_to_all | solution.py:90
  282.5 2.0 reduce_sum.62
  284.6 3.1 collective-permute-start.14
  287.7 1.5 collective-permute-done.14
  289.3 0.9 slice.267
  290.2 1.0 slice.256
  291.2 3.0 collective-permute-start.15
  294.2 1.0 maximum_maximum_fusion
  295.2 8.3 %all-to-all-start.3 = ((bf16[8,16,3200]{2,1,0:T(8,128)(2,1)}), bf16[8,16,3200]{2,1,0:T(8,128)(2,1)S(1)}, u32[]{:S(2)}, u32[]{:S(2)}) async-start(bf16[8,16,3200]{2,1,0:T(8,128)(2,1)} %maximum_maximum_fusion), calls=%async_computation.4 | async-start | bytes 1638400 | tf_op jit(solution)/shard_map/all_to_all | solution.py:729
  304.8 0.9 convert_add_fusion.5
  306.5 9.6 %all-to-all-done.3.blocks_ref = bf16[8,16,3200]{2,1,0:T(8,128)(2,1)S(1)} async-done(((bf16[8,16,3200]{2,1,0:T(8,128)(2,1)}), bf16[8,16,3200]{2,1,0:T(8,128)(2,1)S(1)}, u32[]{:S(2)}, u32[]{:S(2)}) %all-to-all-start.3) | async-done | bytes 819232 | tf_op jit(solution)/shard_map/all_to_all | solution.py:729
  317.9 1.4 reshape.179
  320.2 1.4 reshape.181
  321.7 2.8 shard_map.184
  324.5 1.5 slice_reduce_fusion
  (135 shorter events, 19.0 us)
Async XLA Ops:
  7.2 2.4 copy-start.20
  8.7 1.7 copy-start.21
  8.8 2.5 copy-start.22
  8.8 2.5 copy-start.23
  10.1 13.8 %slice-start = ((bf16[72,1024]{1,0:T(8,128)(2,1)}), bf16[64,1024]{1,0:T(8,128)(2,1)S(1)}, s32[]{:S(2)}) async-start(bf16[72,1024]{1,0:T(8,128)(2,1)} %param.18), calls=%async_computation.7 | async-start | bytes 262144 | tf_op jit(solution)/shard_map/slice | solution.py:471
  10.1 13.7 %slice-start.1 = ((bf16[72,1024]{1,0:T(8,128)(2,1)}), bf16[8,1024]{1,0:T(8,128)(2,1)S(1)}, s32[]{:S(2)}) async-start(bf16[72,1024]{1,0:T(8,128)(2,1)} %param.18), calls=%async_computation.8 | async-start | bytes 32768 | tf_op jit(solution)/shard_map/slice | solution.py:472
  11.0 13.7 %copy-start.18 = (bf16[256,1024]{1,0:T(8,128)(2,1)S(1)}, bf16[256,1024]{1,0:T(8,128)(2,1)}, u32[]{:S(2)}) copy-start(bf16[256,1024]{1,0:T(8,128)(2,1)} %param.19) | copy-start | bytes 1572868
  11.0 13.7 %copy-start.19 = (bf16[256,1024]{1,0:T(8,128)(2,1)S(1)}, bf16[256,1024]{1,0:T(8,128)(2,1)}, u32[]{:S(2)}) copy-start(bf16[256,1024]{1,0:T(8,128)(2,1)} %param.10) | copy-start | bytes 1572868
  12.2 11.6 %all-to-all-start = ((bf16[4,16,3200]{2,1,0:T(8,128)(2,1)}), bf16[4,16,3200]{2,1,0:T(8,128)(2,1)S(1)}, u32[]{:S(2)}, u32[]{:S(2)}) async-start(bf16[4,16,3200]{2,1,0:T(8,128)(2,1)} %pad_maximum_fusion.4), calls=%async_computation | async-start | bytes 819200 | tf_op jit(solution)/shard_map/all_to_all | solution.py:86
  17.1 100.6 %all-gather.2.cloned.1.call-start = ((), (), s32[]{:S(2)}) async-start(), calls=%async_computation.5 | async-start | bytes 7520256 | tf_op jit(solution)/shard_map/all_gather | solution.py:95
  24.9 24.0 %collective-permute-start = (bf16[2,256,1024]{2,1,0:T(8,128)(2,1)S(1)}, bf16[2,256,1024]{2,1,0:T(8,128)(2,1)S(1)}, u32[]{:S(2)}, u32[]{:S(2)}) collective-permute-start(bf16[2,256,1024]{2,1,0:T(8,128)(2,1)S(1)} %get-tuple-element.103), channel_id=1, source_target_pairs={{0,32},{1,33},{2,34},{3,35},{4,36},{5,37},{6,38},{7,39},{8,40},{9,... | collective-permute-start | bytes 3145736 | tf_op jit(solution)/shard_map/ppermute | solution.py:49
  29.9 46.5 %all-to-all-start.1 = ((bf16[16,4,16,1152]{3,2,1,0:T(8,128)(2,1)}), bf16[16,4,16,1152]{3,2,1,0:T(8,128)(2,1)}, u32[]{:S(2)}, u32[]{:S(2)}) async-start(bf16[16,4,16,1152]{3,2,1,0:T(8,128)(2,1)} %broadcast_in_dim.7), calls=%async_computation.1 | async-start | bytes 4718592 | tf_op jit(solution)/shard_map/all_to_all | solution.py:90
  36.8 252.4 %reduce-scatter.2.cloned.1.call-start = ((), (), s32[]{:S(2)}) async-start(), calls=%async_computation.6 | async-start | bytes 7520256 | tf_op jit(solution)/shard_map/reduce_scatter | solution.py:106
  48.8 1.0 copy-start.1
  51.2 25.3 %copy-start = (bf16[2,2,256,1024]{3,2,1,0:T(8,128)(2,1)}, bf16[2,2,256,1024]{3,2,1,0:T(8,128)(2,1)S(1)}, u32[]{:S(2)}) copy-start(bf16[2,2,256,1024]{3,2,1,0:T(8,128)(2,1)S(1)} %pad_maximum_fusion.pair_ref) | copy-start | bytes 6291460
  51.2 25.2 %collective-permute-start.1 = (bf16[2,2,256,1024]{3,2,1,0:T(8,128)(2,1)S(1)}, bf16[2,2,256,1024]{3,2,1,0:T(8,128)(2,1)}, u32[]{:S(2)}, u32[]{:S(2)}) collective-permute-start(bf16[2,2,256,1024]{3,2,1,0:T(8,128)(2,1)S(1)} %pad_maximum_fusion.pair_ref), channel_id=1, source_target_pairs={{0,1},{1,0},{2,3},{3,2},{4,5},{5,4},{6,7},{7,6},{8,9},{9,8},{10,11... | collective-permute-start | bytes 6291464 | tf_op jit(solution)/shard_map/ppermute | solution.py:45
  84.9 5.9 %collective-permute-start.2 = (bf16[2,2,256]{2,1,0:T(2,128)(2,1)S(1)}, bf16[2,2,256]{2,1,0:T(2,128)(2,1)S(1)}, u32[]{:S(2)}, u32[]{:S(2)}) collective-permute-start(bf16[2,2,256]{2,1,0:T(2,128)(2,1)S(1)} %broadcast_select_fusion.7), channel_id=1, source_target_pairs={{0,2},{1,3},{2,4},{3,5},{4,6},{5,7},{6,8},{7,9},{8,10},{9,11},{10,... | collective-permute-start | bytes 6152 | tf_op jit(solution)/shard_map/ppermute | solution.py:546
  97.1 5.8 %collective-permute-start.3 = (bf16[2,256,1024]{2,1,0:T(8,128)(2,1)}, bf16[2,256,1024]{2,1,0:T(8,128)(2,1)S(1)}, u32[]{:S(2)}, u32[]{:S(2)}) collective-permute-start(bf16[2,256,1024]{2,1,0:T(8,128)(2,1)} %get-tuple-element.55), channel_id=1, source_target_pairs={{0,1},{1,0},{2,3},{3,2},{4,5},{5,4},{6,7},{7,6},{8,9},{9,8},{10,11... | collective-permute-start | bytes 3145736 | tf_op jit(solution)/shard_map/ppermute | solution.py:45
  102.9 2.4 copy-start.12
  105.3 24.5 %collective-permute-start.4 = (bf16[2,256,1024]{2,1,0:T(8,128)(2,1)S(1)}, bf16[2,256,1024]{2,1,0:T(8,128)(2,1)S(1)}, u32[]{:S(2)}, u32[]{:S(2)}) collective-permute-start(bf16[2,256,1024]{2,1,0:T(8,128)(2,1)S(1)} %fusion.1), channel_id=1, source_target_pairs={{0,32},{1,33},{2,34},{3,35},{4,36},{5,37},{6,38},{7,39},{8,40},{9,... | collective-permute-start | bytes 3145736 | tf_op jit(solution)/shard_map/ppermute | solution.py:49
  120.7 9.4 %copy-start.13 = (bf16[2,256,1024]{2,1,0:T(8,128)(2,1)S(1)}, bf16[2,256,1024]{2,1,0:T(8,128)(2,1)}, u32[]{:S(2)}) copy-start(bf16[2,256,1024]{2,1,0:T(8,128)(2,1)} %copy-done.12) | copy-start | bytes 3145732
  122.4 7.7 %copy-start.2 = (bf16[2,256,1024]{2,1,0:T(8,128)(2,1)S(1)}, bf16[2,256,1024]{2,1,0:T(8,128)(2,1)}, u32[]{:S(2)}) copy-start(bf16[2,256,1024]{2,1,0:T(8,128)(2,1)} %copy-done.1) | copy-start | bytes 3145732
  122.4 7.7 %copy-start.6 = (f32[2,256,1024]{2,1,0:T(8,128)S(1)}, f32[2,256,1024]{2,1,0:T(8,128)}, u32[]{:S(2)}) copy-start(f32[2,256,1024]{2,1,0:T(8,128)} %get-tuple-element.54) | copy-start | bytes 6291460
  130.9 3.7 %copy-start.14 = (bf16[2,256,1024]{2,1,0:T(8,128)(2,1)}, bf16[2,256,1024]{2,1,0:T(8,128)(2,1)S(1)}, u32[]{:S(2)}) copy-start(bf16[2,256,1024]{2,1,0:T(8,128)(2,1)S(1)} %multiply_convert_fusion.own_ref) | copy-start | bytes 3145732
  131.0 3.7 %collective-permute-start.5 = (bf16[2,256,1024]{2,1,0:T(8,128)(2,1)S(1)}, bf16[2,256,1024]{2,1,0:T(8,128)(2,1)S(1)}, u32[]{:S(2)}, u32[]{:S(2)}) collective-permute-start(bf16[2,256,1024]{2,1,0:T(8,128)(2,1)S(1)} %multiply_convert_fusion.own_ref), channel_id=1, source_target_pairs={{0,1},{1,0},{2,3},{3,2},{4,5},{5,4},{6,7},{7,6},{8,9},{9,8},{10,11... | collective-permute-start | bytes 3145736 | tf_op jit(solution)/shard_map/ppermute | solution.py:45
  134.6 1.0 copy-start.17
  156.8 2.9 collective-permute-start.6
  159.7 3.3 %copy-start.10 = (bf16[2,256,1024]{2,1,0:T(8,128)(2,1)}, bf16[2,256,1024]{2,1,0:T(8,128)(2,1)S(1)}, u32[]{:S(2)}) copy-start(bf16[2,256,1024]{2,1,0:T(8,128)(2,1)S(1)} %collective-permute-done.6) | copy-start | bytes 3145732
  183.4 25.0 %copy-start.7 = (f32[2,256,1024]{2,1,0:T(8,128)S(1)}, f32[2,256,1024]{2,1,0:T(8,128)}, u32[]{:S(2)}) copy-start(f32[2,256,1024]{2,1,0:T(8,128)} %get-tuple-element.59) | copy-start | bytes 6291460
  183.4 25.0 %copy-start.11 = (bf16[2,256,1024]{2,1,0:T(8,128)(2,1)S(1)}, bf16[2,256,1024]{2,1,0:T(8,128)(2,1)}, u32[]{:S(2)}) copy-start(bf16[2,256,1024]{2,1,0:T(8,128)(2,1)} %copy-done.10) | copy-start | bytes 3145732
  183.4 24.8 %collective-permute-start.7 = (bf16[2,256,1024]{2,1,0:T(8,128)(2,1)}, bf16[2,256,1024]{2,1,0:T(8,128)(2,1)S(1)}, u32[]{:S(2)}, u32[]{:S(2)}) collective-permute-start(bf16[2,256,1024]{2,1,0:T(8,128)(2,1)} %fusion.2), channel_id=1, source_target_pairs={{0,32},{1,33},{2,34},{3,35},{4,36},{5,37},{6,38},{7,39},{8,40},{9,... | collective-permute-start | bytes 3145736 | tf_op jit(solution)/shard_map/ppermute | solution.py:49
  208.4 1.2 copy-start.3
  209.0 3.0 copy-start.5
  212.0 3.7 %collective-permute-start.8 = (bf16[2,256,1024]{2,1,0:T(8,128)(2,1)}, bf16[2,256,1024]{2,1,0:T(8,128)(2,1)}, u32[]{:S(2)}, u32[]{:S(2)}) collective-permute-start(bf16[2,256,1024]{2,1,0:T(8,128)(2,1)} %get-tuple-element.94.own_ref), channel_id=1, source_target_pairs={{0,1},{1,0},{2,3},{3,2},{4,5},{5,4},{6,7},{7,6},{8,9},{9,8},{10,11... | collective-permute-start | bytes 3145736 | tf_op jit(solution)/shard_map/ppermute | solution.py:45
  221.7 5.4 %collective-permute-start.9 = (f32[2,2,256]{2,1,0:T(2,128)S(1)}, f32[2,2,256]{2,1,0:T(2,128)S(1)}, u32[]{:S(2)}, u32[]{:S(2)}) collective-permute-start(f32[2,2,256]{2,1,0:T(2,128)S(1)} %broadcast_select_fusion.4), channel_id=1, source_target_pairs={{0,30},{1,31},{2,0},{3,1},{4,2},{5,3},{6,4},{7,5},{8,6},{9,7},{10,... | collective-permute-start | bytes 12296 | tf_op jit(solution)/shard_map/ppermute | solution.py:637
  227.8 12.7 %copy-start.4 = (bf16[2,256,1024]{2,1,0:T(8,128)(2,1)S(1)}, bf16[2,256,1024]{2,1,0:T(8,128)(2,1)}, u32[]{:S(2)}) copy-start(bf16[2,256,1024]{2,1,0:T(8,128)(2,1)} %copy-done.1) | copy-start | bytes 3145732
  239.6 6.8 %collective-permute-start.12 = (bf16[2,256,1024]{2,1,0:T(8,128)(2,1)}, bf16[2,256,1024]{2,1,0:T(8,128)(2,1)}, u32[]{:S(2)}, u32[]{:S(2)}) collective-permute-start(bf16[2,256,1024]{2,1,0:T(8,128)(2,1)} %get-tuple-element.82), channel_id=1, source_target_pairs={{0,1},{1,0},{2,3},{3,2},{4,5},{5,4},{6,7},{7,6},{8,9},{9,8},{10,11... | collective-permute-start | bytes 3145736 | tf_op jit(solution)/shard_map/ppermute | solution.py:45
  240.4 9.9 %collective-permute-start.10 = (bf16[2,256,1024]{2,1,0:T(8,128)(2,1)}, bf16[2,256,1024]{2,1,0:T(8,128)(2,1)}, u32[]{:S(2)}, u32[]{:S(2)}) collective-permute-start(bf16[2,256,1024]{2,1,0:T(8,128)(2,1)} %get-tuple-element.80), channel_id=1, source_target_pairs={{0,1},{1,0},{2,3},{3,2},{4,5},{5,4},{6,7},{7,6},{8,9},{9,8},{10,11... | collective-permute-start | bytes 3145736 | tf_op jit(solution)/shard_map/ppermute | solution.py:45
  241.9 40.6 %all-to-all-start.2 = ((bf16[16,4,16,1152]{3,2,1,0:T(8,128)(2,1)}), bf16[16,4,16,1152]{3,2,1,0:T(8,128)(2,1)}, u32[]{:S(2)}, u32[]{:S(2)}) async-start(bf16[16,4,16,1152]{3,2,1,0:T(8,128)(2,1)} %bitcast.148), calls=%async_computation.2 | async-start | bytes 4718592 | tf_op jit(solution)/shard_map/all_to_all | solution.py:90
  246.4 3.9 %copy-start.16 = (f32[2,256,1024]{2,1,0:T(8,128)S(1)}, f32[2,256,1024]{2,1,0:T(8,128)}, u32[]{:S(2)}) copy-start(f32[2,256,1024]{2,1,0:T(8,128)} %get-tuple-element.68) | copy-start | bytes 6291460
  248.8 13.3 %copy-start.8 = (f32[2,1,256,1024]{3,2,1,0:T(8,128)S(1)}, f32[2,1,256,1024]{3,2,1,0:T(8,128)}, u32[]{:S(2)}) copy-start(f32[2,1,256,1024]{3,2,1,0:T(8,128)} %fusion.4) | copy-start | bytes 6291460
  248.8 13.3 %collective-permute-start.13 = (bf16[256,1024]{1,0:T(8,128)(2,1)S(1)}, bf16[256,1024]{1,0:T(8,128)(2,1)S(1)}, u32[]{:S(2)}, u32[]{:S(2)}) collective-permute-start(bf16[256,1024]{1,0:T(8,128)(2,1)S(1)} %fusion.17), channel_id=1, source_target_pairs={{0,32},{1,33},{2,34},{3,35},{4,36},{5,37},{6,38},{7,39},{8,40},{9,... | collective-permute-start | bytes 1572872 | tf_op jit(solution)/shard_map/ppermute | solution.py:49
  252.0 21.3 %collective-permute-start.11 = (bf16[256,1024]{1,0:T(8,128)(2,1)S(1)}, bf16[256,1024]{1,0:T(8,128)(2,1)S(1)}, u32[]{:S(2)}, u32[]{:S(2)}) collective-permute-start(bf16[256,1024]{1,0:T(8,128)(2,1)S(1)} %fusion.16), channel_id=1, source_target_pairs={{0,32},{1,33},{2,34},{3,35},{4,36},{5,37},{6,38},{7,39},{8,40},{9,... | collective-permute-start | bytes 1572872 | tf_op jit(solution)/shard_map/ppermute | solution.py:49
  262.4 11.9 %copy-start.9 = (f32[2,256,1024]{2,1,0:T(8,128)S(1)}, f32[2,256,1024]{2,1,0:T(8,128)}, u32[]{:S(2)}) copy-start(f32[2,256,1024]{2,1,0:T(8,128)} %get-tuple-element.95) | copy-start | bytes 6291460
  284.6 4.6 %collective-permute-start.14 = (bf16[4,16,384]{2,1,0:T(8,128)(2,1)S(1)}, bf16[4,16,384]{2,1,0:T(8,128)(2,1)S(1)}, u32[]{:S(2)}, u32[]{:S(2)}) collective-permute-start(bf16[4,16,384]{2,1,0:T(8,128)(2,1)S(1)} %slice.259), channel_id=1, source_target_pairs={{0,64},{64,0},{1,65},{65,1},{2,66},{66,2},{3,67},{67,3},{4,68},{68... | collective-permute-start | bytes 147464 | tf_op jit(solution)/shard_map/ppermute | solution.py:709
  291.2 13.6 %collective-permute-start.15 = (bf16[4,16,1152]{2,1,0:T(8,128)(2,1)S(1)}, bf16[4,16,1152]{2,1,0:T(8,128)(2,1)S(1)}, u32[]{:S(2)}, u32[]{:S(2)}) collective-permute-start(bf16[4,16,1152]{2,1,0:T(8,128)(2,1)S(1)} %slice.267), channel_id=1, source_target_pairs={{0,64},{64,0},{1,65},{65,1},{2,66},{66,2},{3,67},{67,3},{4,68},{68... | collective-permute-start | bytes 442376 | tf_op jit(solution)/shard_map/ppermute | solution.py:709
  295.2 21.0 %all-to-all-start.3 = ((bf16[8,16,3200]{2,1,0:T(8,128)(2,1)}), bf16[8,16,3200]{2,1,0:T(8,128)(2,1)S(1)}, u32[]{:S(2)}, u32[]{:S(2)}) async-start(bf16[8,16,3200]{2,1,0:T(8,128)(2,1)} %maximum_maximum_fusion), calls=%async_computation.4 | async-start | bytes 1638400 | tf_op jit(solution)/shard_map/all_to_all | solution.py:729
  316.2 0.9 copy-start.15
Sparse Core Ops, SparseCore 0:
  24.8 92.7 all-gather.1
  183.5 102.9 reduce-scatter.1
where the time goes:
time: 334 us; the launch traced here: 333 us
  waiting for transfers between devices  135 us (40%)
  Pallas kernels  79.9 us (24%)
  starting transfers between devices  45.1 us (14%)
  other arithmetic  31.3 us (9%)
  local copies, waits for them, and re-layouts  27 us (8%)
  between operations  14.7 us (4%)
    pallas_call x8, Pallas kernels, run(): pl.pallas_call(kernel, grid=grid, in_specs=in_specs, out_specs=out_specs,...  79.9 us
    ppermute x5, waiting for transfers between devices, to_z(): return lax.ppermute(value, 'fsdp', TO_Z)  63.2 us
    all_to_all x2, waiting for transfers between devices, plane_swap(): lax.all_to_all(blocks, 'fsdp', 0, 0, tiled=True, axis_index_groups=PLANES)  30.3 us
    all_to_all x2, starting transfers between devices, plane_swap(): lax.all_to_all(blocks, 'fsdp', 0, 0, tiled=True, axis_index_groups=PLANES)  11.3 us
    all_gather x1, waiting for transfers between devices, gather_rows(): lax.all_gather(blocks.reshape(2, 2 * rows, columns), 'fsdp', axis=1, tile...  9.95 us
    all_to_all x1, waiting for transfers between devices, body(): lax.all_to_all(jnp.concatenate([blocks, blocks]), ('rep', 'fsdp'), 0, 0,...  9.64 us
    ppermute x7, starting transfers between devices, to_core(): return lax.ppermute(value, 'fsdp', TO_CORE)  8.78 us
    all_to_all x1, starting transfers between devices, body(): lax.all_to_all(jnp.concatenate([blocks, blocks]), ('rep', 'fsdp'), 0, 0,...  8.34 us
  transfers between devices with their start and end apart: 22, of which 16 were waited for; matrix products, arithmetic and copies ran while one was open for 11% of the time, Pallas kernels for 11%

commit v1 on v0

--- a/solution.py
+++ b/solution.py
@@ -11,8 +11,9 @@
 PLANE = SIDE * SIDE
 HALF = PLANE * 2
 SPARE = 128
+EDGE = 16
 CHUNK = 256
-VMEM_BYTES = 56 * 1024 * 1024
+MIB = 1024 * 1024
 
 
 def place(z, plane, core):
@@ -30,7 +31,7 @@
 
 TO_CORE = moves(lambda z, plane, core: (z, plane, 1 - core))
 TO_Z = moves(lambda z, plane, core: (1 - z, plane, core))
-TO_NEXT = moves(lambda z, plane, core: (z, (plane + 1) % PLANE, core))
+TO_FOLLOWING = [(index, index + 1) for index in range(2 * HALF - 1)]
 TO_PREVIOUS = moves(lambda z, plane, core: (z, (plane - 1) % PLANE, core))
 TEAMS = [
     [place(z, plane, core) for z in range(2) for core in range(2)] for plane in range(PLANE)
@@ -141,9 +142,7 @@
     return pl.BlockSpec((1, 1, length, width), lambda slot: (slot // 2, which, 0, 0))
 
 
-def run(kernel, grid, in_specs, out_specs, out_shape, scratch, flops, values):
-    moved = 0 if flops == 0 else sum(value.size * value.dtype.itemsize for value in values)
-    moved += 0 if flops == 0 else sum(value.size * value.dtype.itemsize for value in out_shape)
+def run(kernel, grid, in_specs, out_specs, out_shape, scratch, room, busy, values):
     return pl.pallas_call(
         kernel,
         grid=grid,
@@ -151,8 +150,10 @@
         out_specs=out_specs,
         out_shape=out_shape,
         scratch_shapes=scratch,
-        compiler_params=pltpu.CompilerParams(vmem_limit_bytes=VMEM_BYTES),
-        cost_estimate=pl.CostEstimate(flops=flops, bytes_accessed=moved, transcendentals=0),
+        compiler_params=pltpu.CompilerParams(vmem_limit_bytes=room * MIB),
+        cost_estimate=pl.CostEstimate(
+            flops=int(busy * 1.15e9), bytes_accessed=0, transcendentals=0
+        ),
     )(*values)
 
 
@@ -164,11 +165,12 @@
     return jnp.where(slot % 2 == 0, even, odd)
 
 
-def shifted_in(values, first_rows, steps):
+def shifted_in(values, rows_before, steps):
     moved = pltpu.roll(values, steps, 0)
     row = lax.broadcasted_iota(jnp.int32, values.shape, 0)
     for index in range(steps):
-        moved = jnp.where(row == index, first_rows[2 - steps + index :][:1], moved)
+        at = EDGE - steps + index
+        moved = jnp.where(row == index, rows_before[at : at + 1], moved)
     return moved
 
 
@@ -192,8 +194,8 @@
 
 
 def project_kernel(
-    pair_ref, other_ref, first_ref,
-    normed_ref, proj_ref, mixed_ref, in_ref, out_ref, gains_ref, taps_ref,
+    pair_ref, other_ref, pair_edge_ref, other_edge_ref, first_ref,
+    normed_ref, proj_ref, mixed_ref, earlier_ref, in_ref, out_ref, gains_ref, taps_ref,
     column, taps_column,
 ):
     slot = pl.program_id(0)
@@ -218,13 +220,16 @@
         gains_ref[...] = column[...].T[:8]
         taps_ref[...] = taps_column[...].T[:8]
 
-    values = pick(slot, pair_ref[0, 0], other_ref[0, 0]).astype(jnp.float32)
-    normed = (values * norm_scale(values) * gains_ref[0:1]).astype(jnp.bfloat16)
-    normed_ref[0] = normed
-    projected = jnp.dot(normed, in_ref[...], preferred_element_type=jnp.float32)
-    proj_ref[0] = projected
-    mixed = projected[:, :channels] * projected[:, 2 * channels :]
-    mixed_ref[0] = mixed.astype(jnp.bfloat16)
+    def project(values):
+        values = values.astype(jnp.float32)
+        normed = (values * norm_scale(values) * gains_ref[0:1]).astype(jnp.bfloat16)
+        projected = jnp.dot(normed, in_ref[...], preferred_element_type=jnp.float32)
+        mixed = (projected[:, :channels] * projected[:, 2 * channels :]).astype(jnp.bfloat16)
+        return normed, projected, mixed
+
+    normed_ref[0], proj_ref[0], mixed_ref[0] = project(pick(slot, pair_ref[0, 0], other_ref[0, 0]))
+    edge = project(pick(slot, pair_edge_ref[0, 0], other_edge_ref[0, 0]))[2]
+    earlier_ref[0] = edge.astype(jnp.float32)
 
 
 def branch_kernel(
@@ -272,8 +277,8 @@
 
 
 def ff_grads_kernel(
-    own_ref, swap_ref, pair_ref, other_ref, hidden_ref, grad_gate_ref, grad_up_ref, down_ref,
-    pack_ref, keep_ref, sent_ref,
+    own_ref, swap_ref, pair_ref, other_ref, hidden_ref, grad_gate_ref, grad_up_ref,
+    pack_ref,
     gate_total, up_total, down_total,
 ):
     slot = pl.program_id(0)
@@ -293,8 +298,6 @@
     gate_total[...] += contract_rows(normed, grad_gate_ref[0])
     up_total[...] += contract_rows(normed, grad_up_ref[0])
     down_total[...] += contract_rows(hidden_ref[0], outer)
-    term = jnp.dot(hidden_ref[0], down_ref[...], preferred_element_type=jnp.float32)
-    store_pair(slot, term, keep_ref, sent_ref)
 
     @pl.when(slot == 3)
     def _():
@@ -496,7 +499,13 @@
     rest_rows = rest_rows.transpose(0, 2, 1, 3).reshape(PLANE, rest, model_width)
     down_full = jnp.concatenate([main_rows, rest_rows], 1).reshape(units, model_width)
 
-    pair = jnp.stack([tokens, cotangent])
+    before = lax.ppermute(tokens[length - EDGE :], "fsdp", TO_FOLLOWING)
+    pair = jnp.stack(
+        [
+            jnp.concatenate([tokens, before], 0),
+            jnp.concatenate([cotangent, jnp.zeros_like(before)], 0),
+        ]
+    )
     pair = jnp.stack([pair, to_z(pair)])
     other = to_core(pair)
     team_pairs = [pair_of_values(length, model_width, 0)] * 2
@@ -505,19 +514,22 @@
     pairs = [per_pair(length, model_width)] * 2
     narrow = per_slot(length, channels)
     out_gate = per_slot(length, channels, 1)
-    edge = per_slot(8, channels)
+    edge, edge_after = per_slot(EDGE, channels), per_slot(8, channels)
+    team_edges = [
+        pl.BlockSpec((1, 1, EDGE, model_width), lambda slot: (slot // 2, 0, length // EDGE, 0))
+    ] * 2
     out_matrix, in_matrix = whole(channels, model_width), whole(model_width, in_width)
     taps = whole(8, channels)
-    unit = 2 * 4 * length * model_width * channels
-
-    normed, projected, mixed, in_full, out_full, gains, kernel = run(
+
+    normed, projected, mixed, earlier, in_full, out_full, gains, kernel = run(
         project_kernel,
         (4,),
-        team_pairs + [whole(*first_all.shape)],
+        team_pairs + team_edges + [whole(*first_all.shape)],
         [
             per_slot(length, model_width),
             per_slot(length, in_width),
             narrow,
+            edge,
             in_matrix,
             out_matrix,
             whole(8, model_width),
@@ -527,32 +539,22 @@
             array(slot_wide, low),
             array((4, length, in_width), wide),
             array(slot_narrow, low),
+            array((4, EDGE, channels), wide),
             array((model_width, in_width), low),
             array((channels, model_width), low),
             array((8, model_width), wide),
             array((8, channels), wide),
         ],
         [pltpu.VMEM((model_width, SPARE), wide), pltpu.VMEM((channels, SPARE), wide)],
-        3 * unit,
-        [pair, other, first_all],
+        24,
+        7.5,
+        [pair, other, pair, other, first_all],
     )
     gain_one, gain_two = gains[0], gains[1]
 
     def by_core(first, second):
         return jnp.where(core == 0, first, second)
 
-    tails = mixed[:, length - 2 :]
-    sent = by_core(tails[1::2], tails[0::2])
-    received = lax.ppermute(sent, "fsdp", TO_NEXT)
-    nothing = jnp.zeros_like(received[0])
-    shifted = jnp.where(
-        z == 0, jnp.stack([nothing, received[0]]), jnp.stack([received[1], nothing])
-    )
-    before = jnp.where(plane == 0, shifted, received)
-    own_before = by_core(before, tails[1::2])
-    other_before = by_core(tails[0::2], before)
-    earlier = jnp.stack([own_before[0], other_before[0], own_before[1], other_before[1]])
-    earlier = jnp.pad(earlier.astype(wide), ((0, 0), (0, 6), (0, 0)))
     convolved, gated, branch_keep, branch_sent = run(
         branch_kernel,
         (4,),
@@ -565,13 +567,14 @@
             array(pair_wide, low),
         ],
         [],
-        unit,
+        16,
+        5.5,
         [mixed, earlier, projected, kernel, out_full],
     )
     branch_pair = core_sum(branch_keep, branch_sent)
     branch_other = to_z(branch_pair.astype(low))
     branch_other, down_full = lax.optimization_barrier((branch_other, down_full))
-    inputs = pair[:, 0].astype(wide)
+    inputs = pair[:, 0, :length].astype(wide)
     middle = inputs + branch_pair + branch_other.astype(wide)[::-1]
     scale_two = norm_scale(middle)
     normed_two = (middle * scale_two * gain_two).astype(low)
@@ -589,7 +592,8 @@
         [unit_slot] * 3 + pairs,
         [unit_shape] * 3 + [array(pair_wide, wide), array(pair_wide, low)],
         [],
-        5 * 2 * 4 * length * model_width * units,
+        40,
+        21,
         [normed_two, normed_swap, pair, other, ff_all, down_full],
     )
     grad_pair = core_sum(grad_keep, grad_sent)
@@ -599,25 +603,29 @@
     grad_sent, hidden, grad_gate, grad_upper = lax.optimization_barrier(
         (grad_sent, hidden, grad_gate, grad_upper)
     )
-    ff_grads, down_keep, down_sent = run(
+    (ff_grads,) = run(
         ff_grads_kernel,
         (4,),
-        pairs + outer_pairs + [unit_slot] * 3 + [whole(units, model_width)],
-        [whole(*ff_all.shape)] + pairs,
-        [array(ff_all.shape, low), array(pair_wide, wide), array(pair_wide, low)],
+        pairs + outer_pairs + [unit_slot] * 3,
+        [whole(*ff_all.shape)],
+        [array(ff_all.shape, low)],
         [
             pltpu.VMEM((model_width, units), wide),
             pltpu.VMEM((model_width, units), wide),
             pltpu.VMEM((units, model_width), wide),
         ],
-        0,
-        [normed_two, normed_swap, pair, other, hidden, grad_gate, grad_upper, down_full],
+        44,
+        16,
+        [normed_two, normed_swap, pair, other, hidden, grad_gate, grad_upper],
     )
     ff_share = scatter_rows(ff_grads)
-    grad_other, down_keep = lax.optimization_barrier((grad_other, down_keep))
+    down_term = jnp.dot(
+        hidden.reshape(4 * length, units), down_full, preferred_element_type=wide
+    ).reshape(4, length, model_width)
+    grad_other, ff_grads, down_term = lax.optimization_barrier((grad_other, ff_grads, down_term))
     grad_normed_two = grad_pair + grad_other.astype(wide)[::-1]
     grad_gain_two = jnp.sum(grad_normed_two[0] * middle[0] * scale_two[0], axis=0)
-    outer = pair[:, 1].astype(wide)
+    outer = pair[:, 1, :length].astype(wide)
     grad_middle = outer + norm_back(grad_normed_two * gain_two, middle, scale_two)
     grad_branch = grad_middle.astype(low)
     grad_swap = to_core(grad_branch)
@@ -629,7 +637,8 @@
         [narrow, narrow],
         [array(slot_narrow, low), array(slot_narrow, wide)],
         [],
-        unit,
+        16,
+        5,
         [grad_branch, grad_swap, out_full, convolved, projected],
     )
     heads = grad_conv[:, :2]
@@ -656,7 +665,8 @@
             pltpu.VMEM((SPARE, channels), wide),
             pltpu.VMEM((SPARE, model_width), wide),
         ],
-        unit,
+        20,
+        5.3,
         [grad_branch, grad_swap, gated, grad_conv, mixed, earlier, grad_gain_two[None]],
     )
     first_grads, normed_keep, normed_sent = run(
@@ -664,7 +674,7 @@
         (4,),
         [
             narrow,
-            edge,
+            edge_after,
             per_slot(length, in_width),
             narrow,
             per_slot(length, model_width),
@@ -676,7 +686,8 @@
         [whole(*first_all.shape)] + pairs,
         [array(first_all.shape, low), array(pair_wide, wide), array(pair_wide, low)],
         [pltpu.VMEM((model_width, in_width), wide), pltpu.VMEM((SPARE, model_width), wide)],
-        6 * unit,
+        32,
+        12,
         [
             grad_conv,
             later,
@@ -694,8 +705,8 @@
     first_grads = first_grads.reshape(PLANE, 4, rows, -1)
     first_arrived = plane_swap(first_grads)
 
-    down_sent, normed_sent = lax.optimization_barrier((down_sent, normed_sent))
-    result = middle[0] + own_sum(down_keep, down_sent)
+    down_term, normed_sent = lax.optimization_barrier((down_term, normed_sent))
+    result = middle[0] + own_sum(down_term[0::2], down_term[1::2].astype(low))
     grad_normed_own = own_sum(normed_keep, normed_sent)
     grad_inputs = grad_middle[0] + norm_back(
         grad_normed_own * gain_one, inputs[0], norm_scale(inputs[0])
@@ -709,15 +720,6 @@
         other = lax.ppermute(value, "rep", [(0, 1), (1, 0)])
         return value.astype(wide) + other.astype(wide)
 
-    down_total = both_reps(ff_share[:, :, 2 * units :])
-    down_rest = down_total[:, :, model_width:].reshape(block // rest, rest, -1)
-    down_rest = down_rest.transpose(1, 0, 2).reshape(rest, model_width)
-    down_total = jnp.concatenate(
-        [down_total[:, :, :model_width].reshape(block, model_width), down_rest], 0
-    )
-    out_total = both_reps(first_share[:, :, in_width:])
-    conv_total = out_total[0, :, channels + 2 : channels + 5]
-    out_total = out_total[:, :, :channels].transpose(1, 0, 2).reshape(rows, model_width)
     blocks = jnp.concatenate(
         [
             ff_share[:, :, : 2 * units],
@@ -734,6 +736,17 @@
         tiled=True,
         axis_index_groups=BOTH_TEAMS,
     )
+    owned = jnp.concatenate([ff_share[:, :, 2 * units :], first_share[:, :, in_width:]], 2)
+    owned, blocks = lax.optimization_barrier((owned, blocks))
+    owned = both_reps(owned)
+    down_total, out_total = owned[:, :, : model_width + SPARE], owned[:, :, model_width + SPARE :]
+    down_rest = down_total[:, :, model_width:].reshape(block // rest, rest, -1)
+    down_rest = down_rest.transpose(1, 0, 2).reshape(rest, model_width)
+    down_total = jnp.concatenate(
+        [down_total[:, :, :model_width].reshape(block, model_width), down_rest], 0
+    )
+    conv_total = out_total[0, :, channels + 2 : channels + 5]
+    out_total = out_total[:, :, :channels].transpose(1, 0, 2).reshape(rows, model_width)
     in_total, gain_total = run(
         in_total_kernel,
         (1,),
@@ -741,7 +754,8 @@
         [whole(rows, w_in.shape[1]), whole(rows, SPARE)],
         [array((rows, w_in.shape[1]), wide), array((rows, SPARE), wide)],
         [],
-        unit,
+        16,
+        3,
         [blocks],
     )
     ff_total = blocks[:, :, : 2 * units].astype(wide)

time: 334 us -> 345 us (1.033)
  blocking collectives: 0 us -> 58.8 us
  Pallas kernels: 79.9 us -> 52.7 us
  waiting for transfers between devices: 135 us -> 115 us
  starting transfers between devices: 45.1 us -> 34.2 us
  matrix products: 0 us -> 7.25 us
  other arithmetic: 31.3 us -> 35.1 us
    all_to_all x0 -> x1, blocking collectives: none -> 58.8 us  [plane_swap(): lax.all_to_all(blocks, 'fsdp', 0, 0, tiled=True, axis_index_groups=PLANES)]
    pallas_call x8, Pallas kernels: 79.9 us -> 52.7 us  [run(): pl.pallas_call(kernel, grid=grid, in_specs=in_specs, out_specs=out_specs,...]
    all_to_all x2 -> x1, waiting for transfers between devices: 30.3 us -> 6.48 us  [plane_swap(): lax.all_to_all(blocks, 'fsdp', 0, 0, tiled=True, axis_index_groups=PLANES)]
    ppermute x5, waiting for transfers between devices: 63.2 us -> 77.8 us  [to_z(): return lax.ppermute(value, 'fsdp', TO_Z)]
    all_gather x1, waiting for transfers between devices: 9.95 us -> 0.01 us  [gather_rows(): lax.all_gather(blocks.reshape(2, 2 * rows, columns), 'fsdp', axis=1, tile...]
    dot_general x0 -> x1, matrix products: none -> 7.25 us  [body(): jnp.dot(hidden.reshape(4 * length, units), down_full, preferred_element_t...]
    all_to_all x2 -> x1, starting transfers between devices: 11.3 us -> 4.45 us  [plane_swap(): lax.all_to_all(blocks, 'fsdp', 0, 0, tiled=True, axis_index_groups=PLANES)]
    ppermute x2 -> x1, starting transfers between devices: 6.16 us -> 0.37 us  [both_reps(): other = lax.ppermute(value, 'rep', [(0, 1), (1, 0)])]
  transfers between devices with their start and end apart: 22 -> 20, of which waited for: 16 -> 14; matrix products, arithmetic and copies ran while one was open for 11% -> 12% of each run, Pallas kernels for 11% -> 5%
where the time goes in v1:
time: 345 us; the launch traced here: 344 us
  waiting for transfers between devices  115 us (33%)
  blocking collectives  58.8 us (17%)
  Pallas kernels  52.7 us (15%)
  other arithmetic  35.1 us (10%)
  starting transfers between devices  34.2 us (10%)
  local copies, waits for them, and re-layouts  26.1 us (8%)
  between operations  14.9 us (4%)
  matrix products  7.25 us (2%)
    ppermute x5, waiting for transfers between devices, to_z(): return lax.ppermute(value, 'fsdp', TO_Z)  77.8 us
    all_to_all x1, blocking collectives, plane_swap(): lax.all_to_all(blocks, 'fsdp', 0, 0, tiled=True, axis_index_groups=PLANES)  58.8 us
    pallas_call x8, Pallas kernels, run(): pl.pallas_call(kernel, grid=grid, in_specs=in_specs, out_specs=out_specs,...  52.7 us
    all_to_all x1, waiting for transfers between devices, body(): lax.all_to_all(jnp.concatenate([blocks, blocks]), ('rep', 'fsdp'), 0, 0,...  11.7 us
    ppermute x7, starting transfers between devices, to_core(): return lax.ppermute(value, 'fsdp', TO_CORE)  9.36 us
    unnamed x93, local copies, waits for them, and re-layouts  8.93 us
    ppermute x7, waiting for transfers between devices, to_core(): return lax.ppermute(value, 'fsdp', TO_CORE)  7.37 us
    dot_general x1, matrix products, body(): jnp.dot(hidden.reshape(4 * length, units), down_full, preferred_element_t...  7.25 us
  transfers between devices with their start and end apart: 20, of which 14 were waited for; matrix products, arithmetic and copies ran while one was open for 12% of the time, Pallas kernels for 5%

profile of v1, /device:TPU:1, one launch (start us, length us, event | category | flops | bytes accessed | tf_op | source)
XLA Modules:
  0.0 343.8 jit_solution(17309744334287848140)
XLA Ops:
  8.0 1.5 reshape.166
  12.9 4.8 %all-to-all-start = ((bf16[4,16,3200]{2,1,0:T(8,128)(2,1)}), bf16[4,16,3200]{2,1,0:T(8,128)(2,1)S(1)}, u32[]{:S(2)}, u32[]{:S(2)}) async-start(bf16[4,16,3200]{2,1,0:T(8,128)(2,1)} %pad_maximum_fusion.4), calls=%async_computation | async-start | bytes 819200 | tf_op jit(solution)/shard_map/all_to_all | solution.py:87
  17.7 6.7 %all-to-all-done = bf16[4,16,3200]{2,1,0:T(8,128)(2,1)S(1)} async-done(((bf16[4,16,3200]{2,1,0:T(8,128)(2,1)}), bf16[4,16,3200]{2,1,0:T(8,128)(2,1)S(1)}, u32[]{:S(2)}, u32[]{:S(2)}) %all-to-all-start) | async-done | bytes 409632 | tf_op jit(solution)/shard_map/all_to_all | solution.py:87
  24.5 0.9 pad_maximum_fusion.3
  25.5 4.0 %collective-permute-start = (bf16[16,1024]{1,0:T(8,128)(2,1)S(1)}, bf16[16,1024]{1,0:T(8,128)(2,1)S(1)}, u32[]{:S(2)}, u32[]{:S(2)}) collective-permute-start(bf16[16,1024]{1,0:T(8,128)(2,1)S(1)} %slice.159), channel_id=1, source_target_pairs={{0,1},{1,2},{2,3},{3,4},{4,5},{5,6},{6,7},{7,8},{8,9},{9,10},{10,1... | collective-permute-start | bytes 98312 | tf_op jit(solution)/shard_map/ppermute | solution.py:502
  29.6 0.9 collective-permute-done
  30.6 1.2 fusion.20
  32.1 22.3 %collective-permute-done.1 = bf16[2,272,1024]{2,1,0:T(8,128)(2,1)S(1)} collective-permute-done((bf16[2,272,1024]{2,1,0:T(8,128)(2,1)}, bf16[2,272,1024]{2,1,0:T(8,128)(2,1)S(1)}, u32[]{:S(2)}, u32[]{:S(2)}) %collective-permute-start.1) | collective-permute-done | bytes 1114144 | tf_op jit(solution)/shard_map/ppermute | solution.py:50
  55.3 4.6 %collective-permute-start.2 = (bf16[2,2,272,1024]{3,2,1,0:T(8,128)(2,1)S(1)}, bf16[2,2,272,1024]{3,2,1,0:T(8,128)(2,1)S(1)}, u32[]{:S(2)}, u32[]{:S(2)}) collective-permute-start(bf16[2,2,272,1024]{3,2,1,0:T(8,128)(2,1)S(1)} %pad_maximum_fusion.pair_ref.pair_edge_ref), channel_id=1, source_target_pairs={{0,1},{1,0},{2,3},{3,2},{4,5},{5,4},{6,7},{7,6},{8,9},{9,8},{10,11... | collective-permute-start | bytes 6684680 | tf_op jit(solution)/shard_map/ppermute | solution.py:46
  60.3 58.8 %all_to_all.20 = bf16[16,4,16,1152]{3,2,1,0:T(8,128)(2,1)S(1)} all-to-all(bf16[16,4,16,1152]{3,2,1,0:T(8,128)(2,1)S(1)} %broadcast_in_dim.7), channel_id=1, replica_groups={{0,2,4,6,8,10,12,14,16,18,20,22,24,26,28,30},{1,3,5,7,9,11,13,15,17,19,..., dimensions={0} | all-to-all | bytes 4718592 | tf_op jit(solution)/shard_map/all_to_all | solution.py:91
  119.1 3.7 %shard_map.177 = (bf16[4,256,1024]{2,1,0:T(8,128)(2,1)S(1)}, f32[4,256,768]{2,1,0:T(8,128)S(1)}, bf16[4,256,256]{2,1,0:T(8,128)(2,1)S(1)}, f32[4,16,256]{2,1,0:T...) custom-call(bf16[2,2,272,1024]{3,2,1,0:T(8,128)(2,1)S(1)} %pad_maxim, ...), custom_call_target="tpu_custom_call" | custom-call | flops 8625000448 | tf_op jit(solution)/shard_map/pallas_call | solution.py:146
  122.8 1.7 shard_map.178
  125.9 1.2 collective-permute-start.3
  127.1 2.3 collective-permute-done.3
  129.4 1.4 fusion.3
  130.8 1.3 collective-permute-start.4
  132.1 1.0 slice.213
  133.0 1.8 slice.212
  135.1 1.6 pad_maximum_fusion.1
  136.7 18.7 %collective-permute-done.4 = bf16[2,256,1024]{2,1,0:T(8,128)(2,1)} collective-permute-done((bf16[2,256,1024]{2,1,0:T(8,128)(2,1)}, bf16[2,256,1024]{2,1,0:T(8,128)(2,1)}, u32[]{:S(2)}, u32[]{:S(2)}) %collective-permute-start.4) | collective-permute-done | bytes 1048608 | tf_op jit(solution)/shard_map/ppermute | solution.py:50
  155.5 1.5 convert_element_type.81
  157.0 1.8 multiply_reduce_fusion.1
  158.7 2.0 multiply_convert_fusion.own_ref
  160.7 1.5 collective-permute-start.5
  162.2 2.3 collective-permute-done.5.swap_ref
  164.5 19.4 %shard_map.179 = (bf16[4,256,1152]{2,1,0:T(8,128)(2,1)S(1)}, bf16[4,256,1152]{2,1,0:T(8,128)(2,1)S(1)}, bf16[4,256,1152]{2,1,0:T(8,128)(2,1)}, f32[2,256,1024]{2,1,0:T(8,128)S(1)}, bf16[2,256,1024]{2,1,0:T(8,128)(2,1)S(1)}) custom-call(bf16[2,256,1024]{2,1,0:T(8,128)(2,1)S(1)} %multiply_convert_fusion.own_ref, ...), custom_call_target="tpu_custom_call" | custom-call | flops 24149999616 | tf_op jit(solution)/shard_map/pallas_call | solution.py:146
  183.9 1.5 copy-done.20
  185.8 2.3 collective-permute-done.6
  188.0 1.3 fusion.4
  189.4 14.9 %shard_map.180 = bf16[1024,3456]{1,0:T(8,128)(2,1)} custom-call(bf16[2,256,1024]{2,1,0:T(8,128)(2,1)S(1)} %multiply_convert_fusion.own_ref, bf16[2,256,1024]{2,1,0:T(8,128)(2,1)S(1)} %collective-permute-done.5.swap_ref, bf16[2,2,272,1024]{3,2,1,0:T(8,128)(2,1)S(1)} %copy-done.1, bf16[2,2,272,1024]{3,2,1,0:T(8,128)(2,1)S(1)} %copy-done.4, ...), custom_call_target="tpu_custom_call" | custom-call | flops 18400000000 | tf_op jit(solution)/shard_map/pallas_call | solution.py:146
  204.2 1.4 collective-permute-start.7
  205.6 7.2 %fusion = f32[4,256,1024]{2,1,0:T(8,128)} fusion(bf16[4,256,1152]{2,1,0:T(8,128)(2,1)} %copy-done.6, bf16[1152,1024]{1,0:T(8,128)(2,1)} %bitcast.155), kind=kOutput, calls=%fused_computation.6 | convolution fusion | flops 2415919104 | bytes 8912896 | tf_op jit(solution)/shard_map/dot_general | solution.py:622
  212.8 16.2 %collective-permute-done.7 = bf16[2,256,1024]{2,1,0:T(8,128)(2,1)S(1)} collective-permute-done((bf16[2,256,1024]{2,1,0:T(8,128)(2,1)}, bf16[2,256,1024]{2,1,0:T(8,128)(2,1)S(1)}, u32[]{:S(2)}, u32[]{:S(2)}) %collective-permute-start.7) | collective-permute-done | bytes 1048608 | tf_op jit(solution)/shard_map/ppermute | solution.py:50
  229.3 2.4 multiply_reduce_fusion
  231.7 4.4 %fusion.21 = (bf16[2,256,1024]{2,1,0:T(8,128)(2,1)S(1)}, f32[2,256,1024]{2,1,0:T(8,128)}) fusion(f32[2,256]{1,0:T(2,128)S(1)} %broadcast_multiply_fusion, f32[2,256,1024]{2,1,0:T(8,128)} %get-tuple-element.99, f32[2,256,1024]{2,1,0:T(8,128)S(1)} %get-tuple-element.97, f32[1024]{0:T(1024)S(1)} %bitcast.175, f32[2,256]{1,0:T(2,128)S(1)} %add_rsqrt_fusion, ...), kind=kLoop, calls=%fused_computation.80 | loop fusion | flops 5242880 | bytes 9576448 | tf_op jit(solution)/shard_map/convert_element_type | solution.py:630
  236.1 1.1 collective-permute-start.8
  237.2 1.8 fusion.17
  239.5 1.9 copy-done.8
  241.4 1.5 shard_map.181
  243.0 1.4 collective-permute-start.9
  244.5 2.1 shard_map.182
  247.0 1.0 copy-done.9
  249.0 7.7 %shard_map.183 = (bf16[16,64,1152]{2,1,0:T(8,128)(2,1)}, f32[2,256,1024]{2,1,0:T(8,128)S(1)}, bf16[2,256,1024]{2,1,0:T(8,128)(2,1)S(1)}) custom-call(f32[4,256,256]{2,1,0:T(8,128)S(1)} %get-tuple-element.71.grad_conv_ref, f32[4,8,256]{2,1,0:T(8,128)S(1)} %select_maximum_fusion.later_ref, f32[4,256,768]{2,1,0:T(8,128)S(1)} %copy-done.9, ...), custom_call_target="tpu_custom_call" | custom-call | flops 13799999488 | tf_op jit(solution)/shard_map/pallas_call | solution.py:146
  257.7 1.0 slice.183
  259.4 1.4 fusion.6
  260.8 4.4 %all-to-all-start.2 = ((bf16[16,4,16,1152]{3,2,1,0:T(8,128)(2,1)}), bf16[16,4,16,1152]{3,2,1,0:T(8,128)(2,1)}, u32[]{:S(2)}, u32[]{:S(2)}) async-start(bf16[16,4,16,1152]{3,2,1,0:T(8,128)(2,1)} %bitcast.41), calls=%async_computation.2 | async-start | bytes 4718592 | tf_op jit(solution)/shard_map/all_to_all | solution.py:91
  265.3 1.7 convert_add_fusion.1
  267.1 1.4 collective-permute-start.13
  268.5 1.7 convert_add_fusion.2
  270.9 9.9 %collective-permute-done.13 = bf16[256,1024]{1,0:T(8,128)(2,1)S(1)} collective-permute-done((bf16[256,1024]{1,0:T(8,128)(2,1)S(1)}, bf16[256,1024]{1,0:T(8,128)(2,1)S(1)}, u32[]{:S(2)}, u32[]{:S(2)}) %collective-permute-start.13) | collective-permute-done | bytes 524320 | tf_op jit(solution)/shard_map/ppermute | solution.py:50
  281.2 10.8 %collective-permute-done.11 = bf16[256,1024]{1,0:T(8,128)(2,1)S(1)} collective-permute-done((bf16[256,1024]{1,0:T(8,128)(2,1)S(1)}, bf16[256,1024]{1,0:T(8,128)(2,1)S(1)}, u32[]{:S(2)}, u32[]{:S(2)}) %collective-permute-start.11) | collective-permute-done | bytes 524320 | tf_op jit(solution)/shard_map/ppermute | solution.py:50
  291.9 2.3 fusion.14
  294.2 1.3 fusion.11
  295.6 6.5 %all-to-all-done.2 = bf16[16,4,16,1152]{3,2,1,0:T(8,128)(2,1)} async-done(((bf16[16,4,16,1152]{3,2,1,0:T(8,128)(2,1)}), bf16[16,4,16,1152]{3,2,1,0:T(8,128)(2,1)}, u32[]{:S(2)}, u32[]{:S(2)}) %all-to-all-start.2) | async-done | bytes 2359328 | tf_op jit(solution)/shard_map/all_to_all | solution.py:91
  302.0 2.0 reduce_sum.62
  304.1 3.7 %reduce-scatter.2.cloned.1.call-done = bf16[2,32,3456]{2,1,0:T(8,128)(2,1)} async-done(((bf16[2,512,3456]{2,1,0:T(8,128)(2,1)}), bf16[2,32,3456]{2,1,0:T(8,128)(2,1)}) %reduce-scatter.2.cloned.1.call-update) | async-done | bytes 442384 | tf_op jit(solution)/shard_map/reduce_scatter | solution.py:107
  307.8 1.0 slice.233
  308.7 1.0 maximum_maximum_fusion
  309.7 4.9 %all-to-all-start.3 = ((bf16[8,16,3200]{2,1,0:T(8,128)(2,1)}), bf16[8,16,3200]{2,1,0:T(8,128)(2,1)S(1)}, u32[]{:S(2)}, u32[]{:S(2)}) async-start(bf16[8,16,3200]{2,1,0:T(8,128)(2,1)} %maximum_maximum_fusion), calls=%async_computation.4 | async-start | bytes 1638400 | tf_op jit(solution)/shard_map/all_to_all | solution.py:731
  314.6 0.9 slice.231
  315.5 11.7 %all-to-all-done.3.blocks_ref = bf16[8,16,3200]{2,1,0:T(8,128)(2,1)S(1)} async-done(((bf16[8,16,3200]{2,1,0:T(8,128)(2,1)}), bf16[8,16,3200]{2,1,0:T(8,128)(2,1)S(1)}, u32[]{:S(2)}, u32[]{:S(2)}) %all-to-all-start.3) | async-done | bytes 819232 | tf_op jit(solution)/shard_map/all_to_all | solution.py:731
  327.8 1.7 shard_map.184
  330.3 1.4 reshape.183
  332.6 1.4 reshape.185
  (173 shorter events, 18.1 us)
Async XLA Ops:
  7.2 3.1 copy-start.41
  9.5 1.7 copy-start.42
  10.9 13.6 %slice-start.1 = ((bf16[72,1024]{1,0:T(8,128)(2,1)}), bf16[8,1024]{1,0:T(8,128)(2,1)S(1)}, s32[]{:S(2)}) async-start(bf16[72,1024]{1,0:T(8,128)(2,1)} %param.18), calls=%async_computation.8 | async-start | bytes 32768 | tf_op jit(solution)/shard_map/slice | solution.py:475
  10.9 13.6 %slice-start.2 = ((bf16[72,1024]{1,0:T(8,128)(2,1)}), bf16[64,1024]{1,0:T(8,128)(2,1)S(1)}, s32[]{:S(2)}) async-start(bf16[72,1024]{1,0:T(8,128)(2,1)} %param.18), calls=%async_computation.9 | async-start | bytes 262144 | tf_op jit(solution)/shard_map/slice | solution.py:474
  11.8 13.7 %copy-start.39 = (bf16[256,1024]{1,0:T(8,128)(2,1)S(1)}, bf16[256,1024]{1,0:T(8,128)(2,1)}, u32[]{:S(2)}) copy-start(bf16[256,1024]{1,0:T(8,128)(2,1)} %param.10) | copy-start | bytes 1572868
  11.8 17.8 %copy-start.40 = (bf16[256,1024]{1,0:T(8,128)(2,1)S(1)}, bf16[256,1024]{1,0:T(8,128)(2,1)}, u32[]{:S(2)}) copy-start(bf16[256,1024]{1,0:T(8,128)(2,1)} %param.19) | copy-start | bytes 1572868
  12.9 11.6 %all-to-all-start = ((bf16[4,16,3200]{2,1,0:T(8,128)(2,1)}), bf16[4,16,3200]{2,1,0:T(8,128)(2,1)S(1)}, u32[]{:S(2)}, u32[]{:S(2)}) async-start(bf16[4,16,3200]{2,1,0:T(8,128)(2,1)} %pad_maximum_fusion.4), calls=%async_computation | async-start | bytes 819200 | tf_op jit(solution)/shard_map/all_to_all | solution.py:87
  17.7 114.3 %all-gather.2.cloned.1.call-start = ((), (), s32[]{:S(2)}) async-start(), calls=%async_computation.5 | async-start | bytes 7520256 | tf_op jit(solution)/shard_map/all_gather | solution.py:96
  24.5 7.6 %copy-start.38 = (bf16[4,16,3200]{2,1,0:T(8,128)(2,1)}, bf16[4,16,3200]{2,1,0:T(8,128)(2,1)S(1)}, u32[]{:S(2)}) copy-start(bf16[4,16,3200]{2,1,0:T(8,128)(2,1)S(1)} %all-to-all-done) | copy-start | bytes 1228804
  25.4 282.4 %reduce-scatter.2.cloned.1.call-start = ((), (), s32[]{:S(2)}) async-start(), calls=%async_computation.6 | async-start | bytes 7520256 | tf_op jit(solution)/shard_map/reduce_scatter | solution.py:107
  25.5 5.1 %collective-permute-start = (bf16[16,1024]{1,0:T(8,128)(2,1)S(1)}, bf16[16,1024]{1,0:T(8,128)(2,1)S(1)}, u32[]{:S(2)}, u32[]{:S(2)}) collective-permute-start(bf16[16,1024]{1,0:T(8,128)(2,1)S(1)} %slice.159), channel_id=1, source_target_pairs={{0,1},{1,2},{2,3},{3,4},{4,5},{5,6},{6,7},{7,8},{8,9},{9,10},{10,1... | collective-permute-start | bytes 98312 | tf_op jit(solution)/shard_map/ppermute | solution.py:502
  29.6 2.3 copy-start.44
  29.6 2.4 copy-start.43
  31.8 22.8 %copy-start.21 = (bf16[1,2,272,1024]{3,2,1,0:T(8,128)(2,1)}, bf16[1,2,272,1024]{3,2,1,0:T(8,128)(2,1)S(1)}, u32[]{:S(2)}) copy-start(bf16[1,2,272,1024]{3,2,1,0:T(8,128)(2,1)S(1)} %get-tuple-element.100) | copy-start | bytes 3342340
  31.8 22.6 %collective-permute-start.1 = (bf16[2,272,1024]{2,1,0:T(8,128)(2,1)}, bf16[2,272,1024]{2,1,0:T(8,128)(2,1)S(1)}, u32[]{:S(2)}, u32[]{:S(2)}) collective-permute-start(bf16[2,272,1024]{2,1,0:T(8,128)(2,1)} %get-tuple-element.101), channel_id=1, source_target_pairs={{0,32},{1,33},{2,34},{3,35},{4,36},{5,37},{6,38},{7,39},{8,40},{9,... | collective-permute-start | bytes 3342344 | tf_op jit(solution)/shard_map/ppermute | solution.py:50
  54.3 5.6 %slice-start = ((bf16[4,16,3200]{2,1,0:T(8,128)(2,1)}), bf16[4,16,768]{2,1,0:T(8,128)(2,1)S(1)}, s32[]{:S(2)}) async-start(bf16[4,16,3200]{2,1,0:T(8,128)(2,1)} %copy-done.38), calls=%async_computation.7 | async-start | bytes 196608 | tf_op jit(solution)/shard_map/slice | solution.py:486
  55.3 63.7 %copy-start = (bf16[2,2,272,1024]{3,2,1,0:T(8,128)(2,1)}, bf16[2,2,272,1024]{3,2,1,0:T(8,128)(2,1)S(1)}, u32[]{:S(2)}) copy-start(bf16[2,2,272,1024]{3,2,1,0:T(8,128)(2,1)S(1)} %pad_maximum_fusion.pair_ref.pair_edge_ref) | copy-start | bytes 6684676
  55.3 63.7 %collective-permute-start.2 = (bf16[2,2,272,1024]{3,2,1,0:T(8,128)(2,1)S(1)}, bf16[2,2,272,1024]{3,2,1,0:T(8,128)(2,1)S(1)}, u32[]{:S(2)}, u32[]{:S(2)}) collective-permute-start(bf16[2,2,272,1024]{3,2,1,0:T(8,128)(2,1)S(1)} %pad_maximum_fusion.pair_ref.pair_edge_ref), channel_id=1, source_target_pairs={{0,1},{1,0},{2,3},{3,2},{4,5},{5,4},{6,7},{7,6},{8,9},{9,8},{10,11... | collective-permute-start | bytes 6684680 | tf_op jit(solution)/shard_map/ppermute | solution.py:46
  119.1 3.7 %copy-start.3 = (bf16[2,2,272,1024]{3,2,1,0:T(8,128)(2,1)}, bf16[2,2,272,1024]{3,2,1,0:T(8,128)(2,1)S(1)}, u32[]{:S(2)}) copy-start(bf16[2,2,272,1024]{3,2,1,0:T(8,128)(2,1)S(1)} %collective-permute-done.2.other_ref.other_edge_ref) | copy-start | bytes 6684676
  122.8 1.8 copy-start.7
  122.8 2.5 copy-start.10
  122.8 2.9 copy-start.12
  122.8 3.0 copy-start.14
  122.8 3.1 copy-start.16
  125.9 4.8 %copy-start.18 = (bf16[4,256,256]{2,1,0:T(8,128)(2,1)}, bf16[4,256,256]{2,1,0:T(8,128)(2,1)S(1)}, u32[]{:S(2)}) copy-start(bf16[4,256,256]{2,1,0:T(8,128)(2,1)S(1)} %get-tuple-element.75.gated_ref) | copy-start | bytes 1572868
  125.9 3.5 %collective-permute-start.3 = (bf16[2,256,1024]{2,1,0:T(8,128)(2,1)S(1)}, bf16[2,256,1024]{2,1,0:T(8,128)(2,1)S(1)}, u32[]{:S(2)}, u32[]{:S(2)}) collective-permute-start(bf16[2,256,1024]{2,1,0:T(8,128)(2,1)S(1)} %get-tuple-element.56), channel_id=1, source_target_pairs={{0,1},{1,0},{2,3},{3,2},{4,5},{5,4},{6,7},{7,6},{8,9},{9,8},{10,11... | collective-permute-start | bytes 3145736 | tf_op jit(solution)/shard_map/ppermute | solution.py:46
  130.8 24.7 %collective-permute-start.4 = (bf16[2,256,1024]{2,1,0:T(8,128)(2,1)}, bf16[2,256,1024]{2,1,0:T(8,128)(2,1)}, u32[]{:S(2)}, u32[]{:S(2)}) collective-permute-start(bf16[2,256,1024]{2,1,0:T(8,128)(2,1)} %fusion.3), channel_id=1, source_target_pairs={{0,32},{1,33},{2,34},{3,35},{4,36},{5,37},{6,38},{7,39},{8,40},{9,... | collective-permute-start | bytes 3145736 | tf_op jit(solution)/shard_map/ppermute | solution.py:50
  135.1 21.8 %copy-start.37 = (bf16[2,256,1024]{2,1,0:T(8,128)(2,1)S(1)}, bf16[2,256,1024]{2,1,0:T(8,128)(2,1)}, u32[]{:S(2)}) copy-start(bf16[2,256,1024]{2,1,0:T(8,128)(2,1)} %copy-done.36) | copy-start | bytes 3145732
  136.7 20.2 %copy-start.22 = (bf16[1,2,272,1024]{3,2,1,0:T(8,128)(2,1)S(1)}, bf16[1,2,272,1024]{3,2,1,0:T(8,128)(2,1)}, u32[]{:S(2)}) copy-start(bf16[1,2,272,1024]{3,2,1,0:T(8,128)(2,1)} %copy-done.21) | copy-start | bytes 3342340
  136.7 20.2 %copy-start.26 = (bf16[2,272,1024]{2,1,0:T(8,128)(2,1)S(1)}, bf16[2,272,1024]{2,1,0:T(8,128)(2,1)}, u32[]{:S(2)}) copy-start(bf16[2,272,1024]{2,1,0:T(8,128)(2,1)} %copy-done.25) | copy-start | bytes 3342340
  156.9 7.5 %copy-start.4 = (bf16[2,2,272,1024]{3,2,1,0:T(8,128)(2,1)S(1)}, bf16[2,2,272,1024]{3,2,1,0:T(8,128)(2,1)}, u32[]{:S(2)}) copy-start(bf16[2,2,272,1024]{3,2,1,0:T(8,128)(2,1)} %copy-done.3) | copy-start | bytes 6684676
  158.7 5.8 %copy-start.1 = (bf16[2,2,272,1024]{3,2,1,0:T(8,128)(2,1)S(1)}, bf16[2,2,272,1024]{3,2,1,0:T(8,128)(2,1)}, u32[]{:S(2)}) copy-start(bf16[2,2,272,1024]{3,2,1,0:T(8,128)(2,1)} %copy-done) | copy-start | bytes 6684676
  160.7 3.7 %collective-permute-start.5 = (bf16[2,256,1024]{2,1,0:T(8,128)(2,1)S(1)}, bf16[2,256,1024]{2,1,0:T(8,128)(2,1)S(1)}, u32[]{:S(2)}, u32[]{:S(2)}) collective-permute-start(bf16[2,256,1024]{2,1,0:T(8,128)(2,1)S(1)} %multiply_convert_fusion.own_ref), channel_id=1, source_target_pairs={{0,1},{1,0},{2,3},{3,2},{4,5},{5,4},{6,7},{7,6},{8,9},{9,8},{10,11... | collective-permute-start | bytes 3145736 | tf_op jit(solution)/shard_map/ppermute | solution.py:46
  183.9 1.5 copy-start.20
  185.4 4.0 %copy-start.6 = (bf16[4,256,1152]{2,1,0:T(8,128)(2,1)}, bf16[4,256,1152]{2,1,0:T(8,128)(2,1)S(1)}, u32[]{:S(2)}) copy-start(bf16[4,256,1152]{2,1,0:T(8,128)(2,1)S(1)} %get-tuple-element.65.hidden_ref) | copy-start | bytes 7077892
  185.4 2.7 collective-permute-start.6
  204.2 24.8 %collective-permute-start.7 = (bf16[2,256,1024]{2,1,0:T(8,128)(2,1)}, bf16[2,256,1024]{2,1,0:T(8,128)(2,1)S(1)}, u32[]{:S(2)}, u32[]{:S(2)}) collective-permute-start(bf16[2,256,1024]{2,1,0:T(8,128)(2,1)} %fusion.4), channel_id=1, source_target_pairs={{0,32},{1,33},{2,34},{3,35},{4,36},{5,37},{6,38},{7,39},{8,40},{9,... | collective-permute-start | bytes 3145736 | tf_op jit(solution)/shard_map/ppermute | solution.py:50
  212.8 16.4 %copy-start.35 = (bf16[2,256,1024]{2,1,0:T(8,128)(2,1)S(1)}, bf16[2,256,1024]{2,1,0:T(8,128)(2,1)}, u32[]{:S(2)}) copy-start(bf16[2,256,1024]{2,1,0:T(8,128)(2,1)} %copy-done.34) | copy-start | bytes 3145732
  229.3 2.4 copy-start.23
  229.3 2.4 copy-start.27
  231.6 4.5 %copy-start.29 = (f32[2,256,1024]{2,1,0:T(8,128)}, f32[2,256,1024]{2,1,0:T(8,128)S(1)}, u32[]{:S(2)}) copy-start(f32[2,256,1024]{2,1,0:T(8,128)S(1)} %get-tuple-element.97) | copy-start | bytes 6291460
  236.1 3.4 collective-permute-start.8
  237.2 2.3 copy-start.15
  239.5 1.9 copy-start.8
  241.4 3.0 copy-start.17
  241.4 3.0 copy-start.19
  243.0 3.6 %collective-permute-start.9 = (f32[2,2,256]{2,1,0:T(2,128)S(1)}, f32[2,2,256]{2,1,0:T(2,128)S(1)}, u32[]{:S(2)}, u32[]{:S(2)}) collective-permute-start(f32[2,2,256]{2,1,0:T(2,128)S(1)} %broadcast_select_fusion.2), channel_id=1, source_target_pairs={{0,30},{1,31},{2,0},{3,1},{4,2},{5,3},{6,4},{7,5},{8,6},{9,7},{10,... | collective-permute-start | bytes 12296 | tf_op jit(solution)/shard_map/ppermute | solution.py:646
  244.4 2.2 copy-start.2
  244.4 2.6 copy-start.5
  244.4 3.5 %copy-start.9 = (f32[4,256,768]{2,1,0:T(8,128)S(1)}, f32[4,256,768]{2,1,0:T(8,128)}, u32[]{:S(2)}) copy-start(f32[4,256,768]{2,1,0:T(8,128)} %copy-done.7) | copy-start | bytes 9437188
  244.5 4.1 %copy-start.11 = (bf16[4,256,1024]{2,1,0:T(8,128)(2,1)S(1)}, bf16[4,256,1024]{2,1,0:T(8,128)(2,1)}, u32[]{:S(2)}) copy-start(bf16[4,256,1024]{2,1,0:T(8,128)(2,1)} %copy-done.10) | copy-start | bytes 6291460
  244.5 4.5 %copy-start.13 = (bf16[1024,768]{1,0:T(8,128)(2,1)S(1)}, bf16[1024,768]{1,0:T(8,128)(2,1)}, u32[]{:S(2)}) copy-start(bf16[1024,768]{1,0:T(8,128)(2,1)} %copy-done.12) | copy-start | bytes 4718596
  249.0 8.4 %copy-start.30 = (f32[4,256,1024]{2,1,0:T(8,128)S(1)}, f32[4,256,1024]{2,1,0:T(8,128)}, u32[]{:S(2)}) copy-start(f32[4,256,1024]{2,1,0:T(8,128)} %fusion) | copy-start | bytes 12582916
  256.8 8.5 %collective-permute-start.12 = (bf16[2,256,1024]{2,1,0:T(8,128)(2,1)S(1)}, bf16[2,256,1024]{2,1,0:T(8,128)(2,1)}, u32[]{:S(2)}, u32[]{:S(2)}) collective-permute-start(bf16[2,256,1024]{2,1,0:T(8,128)(2,1)S(1)} %get-tuple-element.81), channel_id=1, source_target_pairs={{0,1},{1,0},{2,3},{3,2},{4,5},{5,4},{6,7},{7,6},{8,9},{9,8},{10,11... | collective-permute-start | bytes 3145736 | tf_op jit(solution)/shard_map/ppermute | solution.py:46
  257.7 1.7 copy-start.24
  258.7 9.7 %collective-permute-start.10 = (bf16[2,256,1024]{2,1,0:T(8,128)(2,1)}, bf16[2,256,1024]{2,1,0:T(8,128)(2,1)}, u32[]{:S(2)}, u32[]{:S(2)}) collective-permute-start(bf16[2,256,1024]{2,1,0:T(8,128)(2,1)} %slice.183), channel_id=1, source_target_pairs={{0,1},{1,0},{2,3},{3,2},{4,5},{5,4},{6,7},{7,6},{8,9},{9,8},{10,11... | collective-permute-start | bytes 3145736 | tf_op jit(solution)/shard_map/ppermute | solution.py:46
  260.8 41.2 %all-to-all-start.2 = ((bf16[16,4,16,1152]{3,2,1,0:T(8,128)(2,1)}), bf16[16,4,16,1152]{3,2,1,0:T(8,128)(2,1)}, u32[]{:S(2)}, u32[]{:S(2)}) async-start(bf16[16,4,16,1152]{3,2,1,0:T(8,128)(2,1)} %bitcast.41), calls=%async_computation.2 | async-start | bytes 4718592 | tf_op jit(solution)/shard_map/all_to_all | solution.py:91
  265.3 3.2 copy-start.31
  267.1 13.7 %copy-start.32 = (f32[2,1,256,1024]{3,2,1,0:T(8,128)S(1)}, f32[2,1,256,1024]{3,2,1,0:T(8,128)}, u32[]{:S(2)}) copy-start(f32[2,1,256,1024]{3,2,1,0:T(8,128)} %fusion.6) | copy-start | bytes 6291460
  267.1 13.7 %collective-permute-start.13 = (bf16[256,1024]{1,0:T(8,128)(2,1)S(1)}, bf16[256,1024]{1,0:T(8,128)(2,1)S(1)}, u32[]{:S(2)}, u32[]{:S(2)}) collective-permute-start(bf16[256,1024]{1,0:T(8,128)(2,1)S(1)} %fusion.19), channel_id=1, source_target_pairs={{0,32},{1,33},{2,34},{3,35},{4,36},{5,37},{6,38},{7,39},{8,40},{9,... | collective-permute-start | bytes 1572872 | tf_op jit(solution)/shard_map/ppermute | solution.py:50
  270.2 21.7 %collective-permute-start.11 = (bf16[256,1024]{1,0:T(8,128)(2,1)S(1)}, bf16[256,1024]{1,0:T(8,128)(2,1)S(1)}, u32[]{:S(2)}, u32[]{:S(2)}) collective-permute-start(bf16[256,1024]{1,0:T(8,128)(2,1)S(1)} %fusion.18), channel_id=1, source_target_pairs={{0,32},{1,33},{2,34},{3,35},{4,36},{5,37},{6,38},{7,39},{8,40},{9,... | collective-permute-start | bytes 1572872 | tf_op jit(solution)/shard_map/ppermute | solution.py:50
  281.1 13.1 %copy-start.33 = (f32[2,256,1024]{2,1,0:T(8,128)S(1)}, f32[2,256,1024]{2,1,0:T(8,128)}, u32[]{:S(2)}) copy-start(f32[2,256,1024]{2,1,0:T(8,128)} %get-tuple-element.95) | copy-start | bytes 6291460
  309.7 17.5 %all-to-all-start.3 = ((bf16[8,16,3200]{2,1,0:T(8,128)(2,1)}), bf16[8,16,3200]{2,1,0:T(8,128)(2,1)S(1)}, u32[]{:S(2)}, u32[]{:S(2)}) async-start(bf16[8,16,3200]{2,1,0:T(8,128)(2,1)} %maximum_maximum_fusion), calls=%async_computation.4 | async-start | bytes 1638400 | tf_op jit(solution)/shard_map/all_to_all | solution.py:731
  327.2 7.5 %collective-permute-start.14 = (bf16[4,16,1536]{2,1,0:T(8,128)(2,1)S(1)}, bf16[4,16,1536]{2,1,0:T(8,128)(2,1)S(1)}, u32[]{:S(2)}, u32[]{:S(2)}) collective-permute-start(bf16[4,16,1536]{2,1,0:T(8,128)(2,1)S(1)} %pad_maximum_fusion.6), channel_id=1, source_target_pairs={{0,64},{64,0},{1,65},{65,1},{2,66},{66,2},{3,67},{67,3},{4,68},{68... | collective-permute-start | bytes 589832 | tf_op jit(solution)/shard_map/ppermute | solution.py:720
  (4 other events, 5.1 us)
Sparse Core Ops, SparseCore 0:
  25.5 91.7 all-gather.1
  204.4 103.3 reduce-scatter.1

commit v2 on v1

--- a/solution.py
+++ b/solution.py
@@ -31,6 +31,7 @@
 
 TO_CORE = moves(lambda z, plane, core: (z, plane, 1 - core))
 TO_Z = moves(lambda z, plane, core: (1 - z, plane, core))
+TO_BOTH = moves(lambda z, plane, core: (1 - z, plane, 1 - core))
 TO_FOLLOWING = [(index, index + 1) for index in range(2 * HALF - 1)]
 TO_PREVIOUS = moves(lambda z, plane, core: (z, (plane - 1) % PLANE, core))
 TEAMS = [
@@ -50,6 +51,10 @@
     return lax.ppermute(value, "fsdp", TO_Z)
 
 
+def to_both(value):
+    return lax.ppermute(value, "fsdp", TO_BOTH)
+
+
 def norm_scale(values):
     return lax.rsqrt(jnp.mean(values * values, axis=-1, keepdims=True) + epsilon)
 
@@ -113,10 +118,6 @@
     ).reshape(4, -1, columns)
 
 
-def slots_of(pair, other):
-    return jnp.stack([pair[0], other[0], pair[1], other[1]])
-
-
 def core_sum(keep, sent):
     return keep + to_core(sent).astype(jnp.float32)
 
@@ -136,10 +137,6 @@
 
 def per_pair(length, width):
     return pl.BlockSpec((1, length, width), lambda slot: (slot // 2, 0, 0))
-
-
-def pair_of_values(length, width, which):
-    return pl.BlockSpec((1, 1, length, width), lambda slot: (slot // 2, which, 0, 0))
 
 
 def run(kernel, grid, in_specs, out_specs, out_shape, scratch, room, busy, values):
@@ -165,6 +162,13 @@
     return jnp.where(slot % 2 == 0, even, odd)
 
 
+def pick_slot(slot, *values):
+    picked = values[0]
+    for index in range(1, 4):
+        picked = jnp.where(slot == index, values[index], picked)
+    return picked
+
+
 def shifted_in(values, rows_before, steps):
     moved = pltpu.roll(values, steps, 0)
     row = lax.broadcasted_iota(jnp.int32, values.shape, 0)
@@ -194,7 +198,7 @@
 
 
 def project_kernel(
-    pair_ref, other_ref, pair_edge_ref, other_edge_ref, first_ref,
+    slot0_ref, slot1_ref, slot2_ref, slot3_ref, first_ref,
     normed_ref, proj_ref, mixed_ref, earlier_ref, in_ref, out_ref, gains_ref, taps_ref,
     column, taps_column,
 ):
@@ -227,8 +231,10 @@
         mixed = (projected[:, :channels] * projected[:, 2 * channels :]).astype(jnp.bfloat16)
         return normed, projected, mixed
 
-    normed_ref[0], proj_ref[0], mixed_ref[0] = project(pick(slot, pair_ref[0, 0], other_ref[0, 0]))
-    edge = project(pick(slot, pair_edge_ref[0, 0], other_edge_ref[0, 0]))[2]
+    values = pick_slot(slot, slot0_ref[...], slot1_ref[...], slot2_ref[...], slot3_ref[...])
+    length = normed_ref.shape[1]
+    normed_ref[0], proj_ref[0], mixed_ref[0] = project(values[:length])
+    edge = project(values[length:])[2]
     earlier_ref[0] = edge.astype(jnp.float32)
 
 
@@ -251,6 +257,34 @@
     store_pair(slot, branch, keep_ref, sent_ref)
 
 
+def middle_kernel(
+    own_ref, far_ref, branch_ref, crossed_ref, gains_ref, middle_ref, normed_ref
+):
+    inputs = jnp.where(pl.program_id(0) == 0, own_ref[...], far_ref[...])
+    middle = inputs[: branch_ref.shape[1]].astype(jnp.float32) + branch_ref[0]
+    middle += crossed_ref[0].astype(jnp.float32)
+    middle_ref[0] = middle
+    normed_ref[0] = (middle * norm_scale(middle) * gains_ref[1:2]).astype(jnp.bfloat16)
+
+
+def grad_middle_kernel(
+    grad_ref, crossed_ref, middle_ref, outer_ref, gains_ref,
+    grad_middle_ref, branch_ref, gain_ref,
+):
+    grad_normed = grad_ref[0] + crossed_ref[0].astype(jnp.float32)
+    middle = middle_ref[0]
+    scale = norm_scale(middle)
+
+    @pl.when(pl.program_id(0) == 0)
+    def _():
+        gain_ref[...] = jnp.sum(grad_normed * middle * scale, axis=0, keepdims=True)
+
+    grad_middle = norm_back(grad_normed * gains_ref[1:2], middle, scale)
+    grad_middle += outer_ref[0].astype(jnp.float32)
+    grad_middle_ref[0] = grad_middle
+    branch_ref[0] = grad_middle.astype(jnp.bfloat16)
+
+
 def ff_kernel(
     own_ref, swap_ref, pair_ref, other_ref, weights_ref, down_ref,
     hidden_ref, grad_gate_ref, grad_up_ref, keep_ref, sent_ref,
@@ -258,7 +292,7 @@
     slot = pl.program_id(0)
     units = down_ref.shape[0]
     normed = pick(slot, own_ref[0], swap_ref[0])
-    outer = pick(slot, pair_ref[0, 0], other_ref[0, 0])
+    outer = pick(slot, pair_ref[0], other_ref[0])
     for start in range(0, units, CHUNK):
         lanes = slice(start, min(start + CHUNK, units))
         up_lanes = slice(units + lanes.start, units + lanes.stop)
@@ -287,7 +321,7 @@
     block = width // PLANE
     rest = each - block
     normed = pick(slot, own_ref[0], swap_ref[0])
-    outer = pick(slot, pair_ref[0, 0], other_ref[0, 0])
+    outer = pick(slot, pair_ref[0], other_ref[0])
 
     @pl.when(slot == 0)
     def _():
@@ -375,7 +409,7 @@
 
 def project_back_kernel(
     grad_conv_ref, later_ref, proj_ref, grad_out_ref, normed_ref, in_ref, taps_ref,
-    pair_ref, other_ref, part_ref, spare_ref,
+    slot0_ref, slot1_ref, slot2_ref, slot3_ref, part_ref, spare_ref,
     pack_ref, keep_ref, sent_ref,
     total, gain_rows,
 ):
@@ -406,7 +440,8 @@
     total[...] += contract_rows(normed_ref[0], grad_projected)
     grad_normed = contract_cols(grad_projected, in_ref[...])
     store_pair(slot, grad_normed, keep_ref, sent_ref)
-    values = pick(slot, pair_ref[0, 0], other_ref[0, 0]).astype(jnp.float32)
+    values = pick_slot(slot, slot0_ref[...], slot1_ref[...], slot2_ref[...], slot3_ref[...])
+    values = values[: grad_normed.shape[0]].astype(jnp.float32)
     gain_rows[0:1] += jnp.sum(grad_normed * values * norm_scale(values), axis=0, keepdims=True)
 
     @pl.when(slot == 3)
@@ -461,6 +496,11 @@
     rows = w_in.shape[0]
     channels = model_width // 4
 
+    before = lax.ppermute(tokens[length - EDGE :], "fsdp", TO_FOLLOWING)
+    extended = jnp.concatenate([tokens, before], 0)
+    slots = [extended, to_core(extended), to_z(extended), to_both(extended)]
+    outer_z = to_z(cotangent)
+
     block = 4 * rows
     rest = w_down.shape[0] - block
     units = w_down.shape[0] * PLANE
@@ -490,6 +530,7 @@
         2,
     )
     first_all = plane_swap(jnp.broadcast_to(first_pack, (PLANE,) + first_pack.shape))
+    first_all, slots, outer_z = lax.optimization_barrier((first_all, slots, outer_z))
     first_all = first_all.reshape(PLANE, 4 * rows, -1)
 
     main_rows = ff_all[:, 2 * units : 2 * units + model_width].reshape(2, PLANE, 2 * rows, -1)
@@ -499,32 +540,20 @@
     rest_rows = rest_rows.transpose(0, 2, 1, 3).reshape(PLANE, rest, model_width)
     down_full = jnp.concatenate([main_rows, rest_rows], 1).reshape(units, model_width)
 
-    before = lax.ppermute(tokens[length - EDGE :], "fsdp", TO_FOLLOWING)
-    pair = jnp.stack(
-        [
-            jnp.concatenate([tokens, before], 0),
-            jnp.concatenate([cotangent, jnp.zeros_like(before)], 0),
-        ]
-    )
-    pair = jnp.stack([pair, to_z(pair)])
-    other = to_core(pair)
-    team_pairs = [pair_of_values(length, model_width, 0)] * 2
+    team_slots = [whole(length + EDGE, model_width)] * 4
     slot_wide, slot_narrow = (4, length, model_width), (4, length, channels)
     pair_wide = (2, length, model_width)
     pairs = [per_pair(length, model_width)] * 2
     narrow = per_slot(length, channels)
     out_gate = per_slot(length, channels, 1)
     edge, edge_after = per_slot(EDGE, channels), per_slot(8, channels)
-    team_edges = [
-        pl.BlockSpec((1, 1, EDGE, model_width), lambda slot: (slot // 2, 0, length // EDGE, 0))
-    ] * 2
     out_matrix, in_matrix = whole(channels, model_width), whole(model_width, in_width)
     taps = whole(8, channels)
 
     normed, projected, mixed, earlier, in_full, out_full, gains, kernel = run(
         project_kernel,
         (4,),
-        team_pairs + team_edges + [whole(*first_all.shape)],
+        team_slots + [whole(*first_all.shape)],
         [
             per_slot(length, model_width),
             per_slot(length, in_width),
@@ -547,10 +576,9 @@
         ],
         [pltpu.VMEM((model_width, SPARE), wide), pltpu.VMEM((channels, SPARE), wide)],
         24,
-        7.5,
-        [pair, other, pair, other, first_all],
-    )
-    gain_one, gain_two = gains[0], gains[1]
+        4,
+        [*slots, first_all],
+    )
 
     def by_core(first, second):
         return jnp.where(core == 0, first, second)
@@ -568,33 +596,46 @@
         ],
         [],
         16,
-        5.5,
+        2,
         [mixed, earlier, projected, kernel, out_full],
     )
     branch_pair = core_sum(branch_keep, branch_sent)
+    outer_pair = jnp.stack([cotangent, outer_z])
+    outer_other = to_core(outer_pair)
     branch_other = to_z(branch_pair.astype(low))
-    branch_other, down_full = lax.optimization_barrier((branch_other, down_full))
-    inputs = pair[:, 0, :length].astype(wide)
-    middle = inputs + branch_pair + branch_other.astype(wide)[::-1]
-    scale_two = norm_scale(middle)
-    normed_two = (middle * scale_two * gain_two).astype(low)
+    branch_other, down_full, outer_other = lax.optimization_barrier(
+        (branch_other, down_full, outer_other)
+    )
+    one = pl.BlockSpec((1, length, model_width), lambda index: (index, 0, 0))
+    crossed = pl.BlockSpec((1, length, model_width), lambda index: (1 - index, 0, 0))
+    gain_rows = whole(8, model_width)
+    middle, normed_two = run(
+        middle_kernel,
+        (2,),
+        team_slots[:2] + [one, crossed, gain_rows],
+        [one, one],
+        [array(pair_wide, wide), array(pair_wide, low)],
+        [],
+        20,
+        3,
+        [slots[0], slots[2], branch_pair, branch_other, gains],
+    )
     normed_swap = to_core(normed_two)
 
-    outer_pairs = [pair_of_values(length, model_width, 1)] * 2
     unit_slot = per_slot(length, units)
     unit_shape = array((4, length, units), low)
     hidden, grad_gate, grad_upper, grad_keep, grad_sent = run(
         ff_kernel,
         (4,),
         pairs
-        + outer_pairs
+        + pairs
         + [whole(*ff_all.shape), whole(units, model_width)],
         [unit_slot] * 3 + pairs,
         [unit_shape] * 3 + [array(pair_wide, wide), array(pair_wide, low)],
         [],
         40,
         21,
-        [normed_two, normed_swap, pair, other, ff_all, down_full],
+        [normed_two, normed_swap, outer_pair, outer_other, ff_all, down_full],
     )
     grad_pair = core_sum(grad_keep, grad_sent)
     grad_sent = grad_pair.astype(low)
@@ -606,7 +647,7 @@
     (ff_grads,) = run(
         ff_grads_kernel,
         (4,),
-        pairs + outer_pairs + [unit_slot] * 3,
+        pairs + pairs + [unit_slot] * 3,
         [whole(*ff_all.shape)],
         [array(ff_all.shape, low)],
         [
@@ -616,18 +657,24 @@
         ],
         44,
         16,
-        [normed_two, normed_swap, pair, other, hidden, grad_gate, grad_upper],
+        [normed_two, normed_swap, outer_pair, outer_other, hidden, grad_gate, grad_upper],
     )
     ff_share = scatter_rows(ff_grads)
     down_term = jnp.dot(
         hidden.reshape(4 * length, units), down_full, preferred_element_type=wide
     ).reshape(4, length, model_width)
     grad_other, ff_grads, down_term = lax.optimization_barrier((grad_other, ff_grads, down_term))
-    grad_normed_two = grad_pair + grad_other.astype(wide)[::-1]
-    grad_gain_two = jnp.sum(grad_normed_two[0] * middle[0] * scale_two[0], axis=0)
-    outer = pair[:, 1, :length].astype(wide)
-    grad_middle = outer + norm_back(grad_normed_two * gain_two, middle, scale_two)
-    grad_branch = grad_middle.astype(low)
+    grad_middle, grad_branch, grad_gain_two = run(
+        grad_middle_kernel,
+        (2,),
+        [one, crossed, one, one, gain_rows],
+        [one, one, whole(1, model_width)],
+        [array(pair_wide, wide), array(pair_wide, low), array((1, model_width), wide)],
+        [],
+        24,
+        4,
+        [grad_pair, grad_other, middle, outer_pair, gains],
+    )
     grad_swap = to_core(grad_branch)
 
     grad_out, grad_conv = run(
@@ -638,7 +685,7 @@
         [array(slot_narrow, low), array(slot_narrow, wide)],
         [],
         16,
-        5,
+        2,
         [grad_branch, grad_swap, out_full, convolved, projected],
     )
     heads = grad_conv[:, :2]
@@ -666,8 +713,8 @@
             pltpu.VMEM((SPARE, model_width), wide),
         ],
         20,
-        5.3,
-        [grad_branch, grad_swap, gated, grad_conv, mixed, earlier, grad_gain_two[None]],
+        2.5,
+        [grad_branch, grad_swap, gated, grad_conv, mixed, earlier, grad_gain_two],
     )
     first_grads, normed_keep, normed_sent = run(
         project_back_kernel,
@@ -681,13 +728,13 @@
             in_matrix,
             taps,
         ]
-        + team_pairs
+        + team_slots
         + [whole(*part_shape), whole(*spare_shape)],
         [whole(*first_all.shape)] + pairs,
         [array(first_all.shape, low), array(pair_wide, wide), array(pair_wide, low)],
         [pltpu.VMEM((model_width, in_width), wide), pltpu.VMEM((SPARE, model_width), wide)],
         32,
-        12,
+        8,
         [
             grad_conv,
             later,
@@ -696,8 +743,7 @@
             normed,
             in_full,
             kernel,
-            pair,
-            other,
+            *slots,
             out_part,
             spare_part,
         ],
@@ -708,8 +754,9 @@
     down_term, normed_sent = lax.optimization_barrier((down_term, normed_sent))
     result = middle[0] + own_sum(down_term[0::2], down_term[1::2].astype(low))
     grad_normed_own = own_sum(normed_keep, normed_sent)
+    inputs = tokens.astype(wide)
     grad_inputs = grad_middle[0] + norm_back(
-        grad_normed_own * gain_one, inputs[0], norm_scale(inputs[0])
+        grad_normed_own * gains[0], inputs, norm_scale(inputs)
     )
     result, grad_inputs, first_arrived = lax.optimization_barrier(
         (result.astype(low), grad_inputs, first_arrived)
@@ -755,7 +802,7 @@
         [array((rows, w_in.shape[1]), wide), array((rows, SPARE), wide)],
         [],
         16,
-        3,
+        2,
         [blocks],
     )
     ff_total = blocks[:, :, : 2 * units].astype(wide)

time: 345 us -> 335 us (0.971)
  blocking collectives: 58.8 us -> 0 us
  starting transfers between devices: 34.2 us -> 68.9 us
  other arithmetic: 35.1 us -> 16.3 us
  waiting for transfers between devices: 115 us -> 133 us
  Pallas kernels: 52.7 us -> 61.5 us
  local copies, waits for them, and re-layouts: 26.1 us -> 32.8 us
    all_to_all x1 -> x0, blocking collectives: 58.8 us -> none  [plane_swap(): lax.all_to_all(blocks, 'fsdp', 0, 0, tiled=True, axis_index_groups=PLANES)]
    ppermute x5 -> x6, starting transfers between devices: 4.8 us -> 36.9 us  [to_z(): return lax.ppermute(value, 'fsdp', TO_Z)]
    ppermute x5 -> x6, waiting for transfers between devices: 77.8 us -> 90.4 us  [to_z(): return lax.ppermute(value, 'fsdp', TO_Z)]
    convert_element_type x5 -> x0, other arithmetic: 9.53 us -> none  [the longest x1 4.41 us: body(): grad_branch = grad_middle.astype(low)]
    pallas_call x8 -> x10, Pallas kernels: 52.7 us -> 61.5 us  [run(): pl.pallas_call(kernel, grid=grid, in_specs=in_specs, out_specs=out_specs,...]
    all_to_all x1 -> x2, starting transfers between devices: 4.45 us -> 11.4 us  [plane_swap(): lax.all_to_all(blocks, 'fsdp', 0, 0, tiled=True, axis_index_groups=PLANES)]
    ppermute x7 -> x8, starting transfers between devices: 9.36 us -> 3.91 us  [to_core(): return lax.ppermute(value, 'fsdp', TO_CORE)]
    unnamed x93 -> x92, local copies, waits for them, and re-layouts: 8.93 us -> 14.3 us
  transfers between devices with their start and end apart: 20 -> 24, of which waited for: 14 -> 14; matrix products, arithmetic and copies ran while one was open for 12% -> 9% of each run, Pallas kernels for 5% -> 8%
where the time goes in v2:
time: 335 us; the launch traced here: 334 us
  waiting for transfers between devices  133 us (40%)
  starting transfers between devices  68.9 us (21%)
  Pallas kernels  61.5 us (18%)
  local copies, waits for them, and re-layouts  32.8 us (10%)
  other arithmetic  16.3 us (5%)
  between operations  14.9 us (4%)
  matrix products  7.22 us (2%)
    ppermute x6, waiting for transfers between devices, to_z(): return lax.ppermute(value, 'fsdp', TO_Z)  90.4 us
    pallas_call x10, Pallas kernels, run(): pl.pallas_call(kernel, grid=grid, in_specs=in_specs, out_specs=out_specs,...  61.5 us
    ppermute x6, starting transfers between devices, to_z(): return lax.ppermute(value, 'fsdp', TO_Z)  36.9 us
    unnamed x92, local copies, waits for them, and re-layouts  14.3 us
    all_to_all x1, waiting for transfers between devices, body(): lax.all_to_all(jnp.concatenate([blocks, blocks]), ('rep', 'fsdp'), 0, 0,...  11.7 us
    all_to_all x2, starting transfers between devices, plane_swap(): lax.all_to_all(blocks, 'fsdp', 0, 0, tiled=True, axis_index_groups=PLANES)  11.4 us
    ppermute x8, waiting for transfers between devices, to_core(): return lax.ppermute(value, 'fsdp', TO_CORE)  9.17 us
    dot_general x1, matrix products, body(): jnp.dot(hidden.reshape(4 * length, units), down_full, preferred_element_t...  7.22 us
  transfers between devices with their start and end apart: 24, of which 14 were waited for; matrix products, arithmetic and copies ran while one was open for 9% of the time, Pallas kernels for 8%

profile of v2, /device:TPU:1, one launch (start us, length us, event | category | flops | bytes accessed | tf_op | source)
XLA Modules:
  0.0 334.3 jit_solution(14329724925288259608)
XLA Ops:
  8.0 1.5 reshape.132
  12.9 4.8 %all-to-all-start = ((bf16[4,16,3200]{2,1,0:T(8,128)(2,1)}), bf16[4,16,3200]{2,1,0:T(8,128)(2,1)S(1)}, u32[]{:S(2)}, u32[]{:S(2)}) async-start(bf16[4,16,3200]{2,1,0:T(8,128)(2,1)} %pad_maximum_fusion.3), calls=%async_computation | async-start | bytes 819200 | tf_op jit(solution)/shard_map/all_to_all | solution.py:92
  17.7 6.7 %all-to-all-done = bf16[4,16,3200]{2,1,0:T(8,128)(2,1)S(1)} async-done(((bf16[4,16,3200]{2,1,0:T(8,128)(2,1)}), bf16[4,16,3200]{2,1,0:T(8,128)(2,1)S(1)}, u32[]{:S(2)}, u32[]{:S(2)}) %all-to-all-start) | async-done | bytes 409632 | tf_op jit(solution)/shard_map/all_to_all | solution.py:92
  25.6 1.7 broadcast_in_dim.10
  27.3 7.0 %all-to-all-start.1 = ((bf16[16,4,16,1152]{3,2,1,0:T(8,128)(2,1)}), bf16[16,4,16,1152]{3,2,1,0:T(8,128)(2,1)S(1)}, u32[]{:S(2)}, u32[]{:S(2)}) async-start(bf16[16,4,16,1152]{3,2,1,0:T(8,128)(2,1)} %broadcast_in_dim.10), calls=%async_computation.1 | async-start | bytes 4718592 | tf_op jit(solution)/shard_map/all_to_all | solution.py:96
  34.3 4.6 %collective-permute-start = (bf16[16,1024]{1,0:T(8,128)(2,1)S(1)}, bf16[16,1024]{1,0:T(8,128)(2,1)S(1)}, u32[]{:S(2)}, u32[]{:S(2)}) collective-permute-start(bf16[16,1024]{1,0:T(8,128)(2,1)S(1)} %slice.139), channel_id=1, source_target_pairs={{0,1},{1,2},{2,3},{3,4},{4,5},{5,6},{6,7},{7,8},{8,9},{9,10},{10,1... | collective-permute-start | bytes 98312 | tf_op jit(solution)/shard_map/ppermute | solution.py:499
  39.0 4.3 %collective-permute-done = bf16[16,1024]{1,0:T(8,128)(2,1)S(1)} collective-permute-done((bf16[16,1024]{1,0:T(8,128)(2,1)S(1)}, bf16[16,1024]{1,0:T(8,128)(2,1)S(1)}, u32[]{:S(2)}, u32[]{:S(2)}) %collective-permute-start) | collective-permute-done | bytes 32800 | tf_op jit(solution)/shard_map/ppermute | solution.py:499
  43.3 30.1 %collective-permute-start.2 = (bf16[272,1024]{1,0:T(8,128)(2,1)S(1)}, bf16[272,1024]{1,0:T(8,128)(2,1)S(1)}, u32[]{:S(2)}, u32[]{:S(2)}) collective-permute-start(bf16[272,1024]{1,0:T(8,128)(2,1)S(1)} %constant_dynamic-update-slice_fusion.slot0_ref.own_ref), channel_id=1, source_target_pairs={{0,32},{1,33},{2,34},{3,35},{4,36},{5,37},{6,38},{7,39},{8,40},{9,... | collective-permute-start | bytes 1671176 | tf_op jit(solution)/shard_map/ppermute | solution.py:51
  73.5 1.7 collective-permute-start.4
  75.1 34.5 %collective-permute-done.4 = bf16[256,1024]{1,0:T(8,128)(2,1)S(1)} collective-permute-done((bf16[256,1024]{1,0:T(8,128)(2,1)}, bf16[256,1024]{1,0:T(8,128)(2,1)S(1)}, u32[]{:S(2)}, u32[]{:S(2)}) %collective-permute-start.4) | collective-permute-done | bytes 524320 | tf_op jit(solution)/shard_map/ppermute | solution.py:51
  110.4 0.8 copy-done.11
  111.2 0.8 copy-done.15
  112.0 1.1 copy-done.9
  113.1 1.1 copy-done.12
  114.1 1.1 copy-done.16
  115.2 3.8 %shard_map.177 = (bf16[4,256,1024]{2,1,0:T(8,128)(2,1)S(1)}, f32[4,256,768]{2,1,0:T(8,128)S(1)}, bf16[4,256,256]{2,1,0:T(8,128)(2,1)S(1)}, f32[4,16,256]{2,1,0:T...) custom-call(bf16[272,1024]{1,0:T(8,128)(2,1)S(1)} %constant_dynamic-, ...), custom_call_target="tpu_custom_call" | custom-call | flops 4600000000 | tf_op jit(solution)/shard_map/pallas_call | solution.py:143
  119.1 1.7 shard_map.178
  123.0 2.1 collective-permute-done.5
  125.1 1.4 fusion.17
  126.5 1.5 collective-permute-start.6
  128.0 1.0 slice.183
  129.0 1.8 slice.182
  131.1 1.7 pad_maximum_fusion
  132.8 18.5 %collective-permute-done.6.crossed_ref = bf16[2,256,1024]{2,1,0:T(8,128)(2,1)} collective-permute-done((bf16[2,256,1024]{2,1,0:T(8,128)(2,1)}, bf16[2,256,1024]{2,1,0:T(8,128)(2,1)}, u32[]{:S(2)}, u32[]{:S(2)}) %collective-permute-start.6) | collective-permute-done | bytes 1048608 | tf_op jit(solution)/shard_map/ppermute | solution.py:51
  151.3 1.7 shard_map.179
  153.0 1.3 copy-done
  154.3 1.2 collective-permute-start.8
  155.5 2.3 collective-permute-done.8.swap_ref
  157.8 18.9 %shard_map.180 = (bf16[4,256,1152]{2,1,0:T(8,128)(2,1)S(1)}, bf16[4,256,1152]{2,1,0:T(8,128)(2,1)S(1)}, bf16[4,256,1152]{2,1,0:T(8,128)(2,1)S(1)}, f32[2,256,1024]{2,1,0:T(8,128)S(1)}, bf16[2,256,1024]{2,1,0:T(8,128)(2,1)S(1)}) custom-call(bf16[2,256,1024]{2,1,0:T(8,128)(2,1)S(1)} %get-tuple-element.78.own_ref, ...), custom_call_target="tpu_custom_call" | custom-call | flops 24149999616 | tf_op jit(solution)/shard_map/pallas_call | solution.py:143
  177.2 2.3 collective-permute-done.9
  179.5 1.4 fusion.16
  180.9 15.0 %shard_map.181 = bf16[1024,3456]{1,0:T(8,128)(2,1)} custom-call(bf16[2,256,1024]{2,1,0:T(8,128)(2,1)S(1)} %get-tuple-element.78.own_ref, bf16[2,256,1024]{2,1,0:T(8,128)(2,1)S(1)} %collective-permute-done.8.swap_ref, bf16[2,256,1024]{2,1,0:T(8,128)(2,1)S(1)} %pad_maximum_fusion.1.pair_ref.outer_ref, bf16[2,256,1024]{2,1,0:T(8,128)(2,1)} %collective-permute-done.7.other_ref, ...), custom_call_target="tpu_custom_call" | custom-call | flops 18400000000 | tf_op jit(solution)/shard_map/pallas_call | solution.py:143
  195.9 1.5 collective-permute-start.10
  197.4 7.2 %fusion = f32[4,256,1024]{2,1,0:T(8,128)} fusion(bf16[4,256,1152]{2,1,0:T(8,128)(2,1)} %copy-done.25, bf16[1152,1024]{1,0:T(8,128)(2,1)} %bitcast.109), kind=kOutput, calls=%fused_computation.1 | convolution fusion | flops 2415919104 | bytes 8912896 | tf_op jit(solution)/shard_map/dot_general | solution.py:663
  204.7 16.0 %collective-permute-done.10.crossed_ref = bf16[2,256,1024]{2,1,0:T(8,128)(2,1)S(1)} collective-permute-done((bf16[2,256,1024]{2,1,0:T(8,128)(2,1)}, bf16[2,256,1024]{2,1,0:T(8,128)(2,1)S(1)}, u32[]{:S(2)}, u32[]{:S(2)}) %collective-permute-start.10) | collective-permute-done | bytes 1048608 | tf_op jit(solution)/shard_map/ppermute | solution.py:51
  220.7 2.4 shard_map.182
  223.1 1.3 copy-done.3
  224.4 1.1 collective-permute-start.11
  225.5 2.5 collective-permute-done.11.swap_ref
  228.0 1.9 copy-done.19
  230.0 1.2 copy-done.22
  231.2 1.0 copy-done.24
  232.3 3.3 %shard_map.183 = (bf16[4,256,256]{2,1,0:T(8,128)(2,1)S(1)}, f32[4,256,256]{2,1,0:T(8,128)S(1)}) custom-call(bf16[2,256,1024]{2,1,0:T(8,128)(2,1)} %get-tuple-element.91.own_ref, bf16[2,256,1024]{2,1,0:T(8,128)(2,1)S(1)} %collective-permute-done.11.swap_ref, bf16[256,1024]{1,0:T(8,128)(2,1)S(1)} %copy-done.24, f32[4,256,256]{2,1,0:T(8,128)S(1)} %copy-done.22, ...), custom_call_target="tpu_custom_call" | custom-call | flops 2300000000 | tf_op jit(solution)/shard_map/pallas_call | solution.py:143
  236.0 4.7 %shard_map.184 = (bf16[16,64,256]{2,1,0:T(8,128)(2,1)S(1)}, f32[16,64,128]{2,1,0:T(8,128)S(1)}) custom-call(bf16[2,256,1024]{2,1,0:T(8,128)(2,1)} %get-tuple-element.91.own_ref, bf16[2,256,1024]{2,1,0:T(8,128)(2,1)S(1)} %collective-permute-done.11.swap_ref, bf16[4,256,256]{2,1,0:T(8,128)(2,1)S(1)} %copy-done.29, ...), custom_call_target="tpu_custom_call" | custom-call | flops 2875000064 | tf_op jit(solution)/shard_map/pallas_call | solution.py:143
  240.9 8.1 %shard_map.185 = (bf16[16,64,1152]{2,1,0:T(8,128)(2,1)}, f32[2,256,1024]{2,1,0:T(8,128)S(1)}, bf16[2,256,1024]{2,1,0:T(8,128)(2,1)}) custom-call(f32[4,256,256]{2,1,0:T(8,128)S(1)} %get-tuple-element.93.grad_conv_ref, f32[4,8,256]{2,1,0:T(8,128)S(1)} %select_maximum_fusion.later_ref, f32[4,256,768]{2,1,0:T(8,128)S(1)} %copy-done.20, ...), custom_call_target="tpu_custom_call" | custom-call | flops 9200000000 | tf_op jit(solution)/shard_map/pallas_call | solution.py:143
  249.9 1.0 slice.156
  251.0 4.4 %all-to-all-start.2 = ((bf16[16,4,16,1152]{3,2,1,0:T(8,128)(2,1)}), bf16[16,4,16,1152]{3,2,1,0:T(8,128)(2,1)}, u32[]{:S(2)}, u32[]{:S(2)}) async-start(bf16[16,4,16,1152]{3,2,1,0:T(8,128)(2,1)} %bitcast.32), calls=%async_computation.2 | async-start | bytes 4718592 | tf_op jit(solution)/shard_map/all_to_all | solution.py:96
  255.4 1.8 convert_add_fusion
  257.3 1.6 collective-permute-start.16
  260.0 10.6 %collective-permute-done.16 = bf16[256,1024]{1,0:T(8,128)(2,1)S(1)} collective-permute-done((bf16[256,1024]{1,0:T(8,128)(2,1)S(1)}, bf16[256,1024]{1,0:T(8,128)(2,1)S(1)}, u32[]{:S(2)}, u32[]{:S(2)}) %collective-permute-start.16) | collective-permute-done | bytes 524320 | tf_op jit(solution)/shard_map/ppermute | solution.py:51
  271.1 10.8 %collective-permute-done.14 = bf16[256,1024]{1,0:T(8,128)(2,1)S(1)} collective-permute-done((bf16[256,1024]{1,0:T(8,128)(2,1)S(1)}, bf16[256,1024]{1,0:T(8,128)(2,1)S(1)}, u32[]{:S(2)}, u32[]{:S(2)}) %collective-permute-start.14) | collective-permute-done | bytes 524320 | tf_op jit(solution)/shard_map/ppermute | solution.py:51
  281.9 1.1 fusion.13
  283.0 1.4 fusion.7
  284.4 6.9 %all-to-all-done.2 = bf16[16,4,16,1152]{3,2,1,0:T(8,128)(2,1)} async-done(((bf16[16,4,16,1152]{3,2,1,0:T(8,128)(2,1)}), bf16[16,4,16,1152]{3,2,1,0:T(8,128)(2,1)}, u32[]{:S(2)}, u32[]{:S(2)}) %all-to-all-start.2) | async-done | bytes 2359328 | tf_op jit(solution)/shard_map/all_to_all | solution.py:96
  291.3 2.0 reduce_sum.32
  293.3 3.4 %reduce-scatter.2.cloned.1.call-done = bf16[2,32,3456]{2,1,0:T(8,128)(2,1)} async-done(((bf16[2,512,3456]{2,1,0:T(8,128)(2,1)}), bf16[2,32,3456]{2,1,0:T(8,128)(2,1)}) %reduce-scatter.2.cloned.1.call-update) | async-done | bytes 442384 | tf_op jit(solution)/shard_map/reduce_scatter | solution.py:112
  296.7 1.0 slice.196
  297.7 1.0 maximum_maximum_fusion
  298.7 6.4 %all-to-all-start.3 = ((bf16[8,16,3200]{2,1,0:T(8,128)(2,1)}), bf16[8,16,3200]{2,1,0:T(8,128)(2,1)S(1)}, u32[]{:S(2)}, u32[]{:S(2)}) async-start(bf16[8,16,3200]{2,1,0:T(8,128)(2,1)} %maximum_maximum_fusion), calls=%async_computation.4 | async-start | bytes 1638400 | tf_op jit(solution)/shard_map/all_to_all | solution.py:778
  305.1 0.9 slice.194
  306.1 11.7 %all-to-all-done.3.blocks_ref = bf16[8,16,3200]{2,1,0:T(8,128)(2,1)S(1)} async-done(((bf16[8,16,3200]{2,1,0:T(8,128)(2,1)}), bf16[8,16,3200]{2,1,0:T(8,128)(2,1)S(1)}, u32[]{:S(2)}, u32[]{:S(2)}) %all-to-all-start.3) | async-done | bytes 819232 | tf_op jit(solution)/shard_map/all_to_all | solution.py:778
  318.3 1.7 shard_map.186
  320.9 1.4 reshape.149
  323.2 1.4 reshape.151
  (167 shorter events, 17.0 us)
Async XLA Ops:
  7.2 3.1 copy-start.40
  9.5 1.7 copy-start.41
  10.9 13.6 %slice-start = ((bf16[72,1024]{1,0:T(8,128)(2,1)}), bf16[8,1024]{1,0:T(8,128)(2,1)S(1)}, s32[]{:S(2)}) async-start(bf16[72,1024]{1,0:T(8,128)(2,1)} %param.18), calls=%async_computation.7 | async-start | bytes 32768 | tf_op jit(solution)/shard_map/slice | solution.py:515
  10.9 13.6 %slice-start.1 = ((bf16[72,1024]{1,0:T(8,128)(2,1)}), bf16[64,1024]{1,0:T(8,128)(2,1)S(1)}, s32[]{:S(2)}) async-start(bf16[72,1024]{1,0:T(8,128)(2,1)} %param.18), calls=%async_computation.8 | async-start | bytes 262144 | tf_op jit(solution)/shard_map/slice | solution.py:514
  11.8 13.6 %copy-start.43 = (bf16[16,3]{0,1:T(4,128)(2,1)S(1)}, bf16[16,3]{0,1:T(4,128)(2,1)}, u32[]{:S(2)}) copy-start(bf16[16,3]{0,1:T(4,128)(2,1)} %param.13) | copy-start | bytes 292
  11.8 13.8 %copy-start.42 = (bf16[16,1024]{1,0:T(8,128)(2,1)S(1)}, bf16[16,1024]{1,0:T(8,128)(2,1)}, u32[]{:S(2)}) copy-start(bf16[16,1024]{1,0:T(8,128)(2,1)} %param.14) | copy-start | bytes 98308
  12.9 11.6 %all-to-all-start = ((bf16[4,16,3200]{2,1,0:T(8,128)(2,1)}), bf16[4,16,3200]{2,1,0:T(8,128)(2,1)S(1)}, u32[]{:S(2)}, u32[]{:S(2)}) async-start(bf16[4,16,3200]{2,1,0:T(8,128)(2,1)} %pad_maximum_fusion.3), calls=%async_computation | async-start | bytes 819200 | tf_op jit(solution)/shard_map/all_to_all | solution.py:92
  17.7 110.3 %all-gather.2.cloned.1.call-start = ((), (), s32[]{:S(2)}) async-start(), calls=%async_computation.5 | async-start | bytes 7520256 | tf_op jit(solution)/shard_map/all_gather | solution.py:101
  27.3 7.0 %copy-start.37 = (bf16[256,1024]{1,0:T(8,128)(2,1)S(1)}, bf16[256,1024]{1,0:T(8,128)(2,1)}, u32[]{:S(2)}) copy-start(bf16[256,1024]{1,0:T(8,128)(2,1)} %param.10) | copy-start | bytes 1572868
  27.3 84.7 %all-to-all-start.1 = ((bf16[16,4,16,1152]{3,2,1,0:T(8,128)(2,1)}), bf16[16,4,16,1152]{3,2,1,0:T(8,128)(2,1)S(1)}, u32[]{:S(2)}, u32[]{:S(2)}) async-start(bf16[16,4,16,1152]{3,2,1,0:T(8,128)(2,1)} %broadcast_in_dim.10), calls=%async_computation.1 | async-start | bytes 4718592 | tf_op jit(solution)/shard_map/all_to_all | solution.py:96
  34.3 262.4 %reduce-scatter.2.cloned.1.call-start = ((), (), s32[]{:S(2)}) async-start(), calls=%async_computation.6 | async-start | bytes 7520256 | tf_op jit(solution)/shard_map/reduce_scatter | solution.py:112
  34.3 9.0 %collective-permute-start = (bf16[16,1024]{1,0:T(8,128)(2,1)S(1)}, bf16[16,1024]{1,0:T(8,128)(2,1)S(1)}, u32[]{:S(2)}, u32[]{:S(2)}) collective-permute-start(bf16[16,1024]{1,0:T(8,128)(2,1)S(1)} %slice.139), channel_id=1, source_target_pairs={{0,1},{1,2},{2,3},{3,4},{4,5},{5,6},{6,7},{7,8},{8,9},{9,10},{10,1... | collective-permute-start | bytes 98312 | tf_op jit(solution)/shard_map/ppermute | solution.py:499
  43.3 75.7 %copy-start.5 = (bf16[272,1024]{1,0:T(8,128)(2,1)}, bf16[272,1024]{1,0:T(8,128)(2,1)S(1)}, u32[]{:S(2)}) copy-start(bf16[272,1024]{1,0:T(8,128)(2,1)S(1)} %constant_dynamic-update-slice_fusion.slot0_ref.own_ref) | copy-start | bytes 1671172
  43.3 66.3 %collective-permute-start.1 = (bf16[272,1024]{1,0:T(8,128)(2,1)S(1)}, bf16[272,1024]{1,0:T(8,128)(2,1)S(1)}, u32[]{:S(2)}, u32[]{:S(2)}) collective-permute-start(bf16[272,1024]{1,0:T(8,128)(2,1)S(1)} %constant_dynamic-update-slice_fusion.slot0_ref.own_ref), channel_id=1, source_target_pairs={{0,1},{1,0},{2,3},{3,2},{4,5},{5,4},{6,7},{7,6},{8,9},{9,8},{10,11... | collective-permute-start | bytes 1671176 | tf_op jit(solution)/shard_map/ppermute | solution.py:47
  43.3 67.0 %collective-permute-start.2 = (bf16[272,1024]{1,0:T(8,128)(2,1)S(1)}, bf16[272,1024]{1,0:T(8,128)(2,1)S(1)}, u32[]{:S(2)}, u32[]{:S(2)}) collective-permute-start(bf16[272,1024]{1,0:T(8,128)(2,1)S(1)} %constant_dynamic-update-slice_fusion.slot0_ref.own_ref), channel_id=1, source_target_pairs={{0,32},{1,33},{2,34},{3,35},{4,36},{5,37},{6,38},{7,39},{8,40},{9,... | collective-permute-start | bytes 1671176 | tf_op jit(solution)/shard_map/ppermute | solution.py:51
  73.4 37.8 %collective-permute-start.3 = (bf16[272,1024]{1,0:T(8,128)(2,1)S(1)}, bf16[272,1024]{1,0:T(8,128)(2,1)S(1)}, u32[]{:S(2)}, u32[]{:S(2)}) collective-permute-start(bf16[272,1024]{1,0:T(8,128)(2,1)S(1)} %constant_dynamic-update-slice_fusion.slot0_ref.own_ref), channel_id=1, source_target_pairs={{0,33},{1,32},{2,35},{3,34},{4,37},{5,36},{6,39},{7,38},{8,41},{9,... | collective-permute-start | bytes 1671176 | tf_op jit(solution)/shard_map/ppermute | solution.py:55
  73.5 36.1 %collective-permute-start.4 = (bf16[256,1024]{1,0:T(8,128)(2,1)}, bf16[256,1024]{1,0:T(8,128)(2,1)S(1)}, u32[]{:S(2)}, u32[]{:S(2)}) collective-permute-start(bf16[256,1024]{1,0:T(8,128)(2,1)} %param.19), channel_id=1, source_target_pairs={{0,32},{1,33},{2,34},{3,35},{4,36},{5,37},{6,38},{7,39},{8,40},{9,... | collective-permute-start | bytes 1572872 | tf_op jit(solution)/shard_map/ppermute | solution.py:51
  112.0 1.1 copy-start.9
  119.0 1.8 copy-start.18
  119.0 1.8 copy-start.23
  119.1 2.0 copy-start.26
  119.1 2.7 copy-start.30
  119.1 3.2 copy-start.32
  119.1 3.8 %copy-start.39 = (bf16[256,1024]{1,0:T(8,128)(2,1)S(1)}, bf16[256,1024]{1,0:T(8,128)(2,1)}, u32[]{:S(2)}) copy-start(bf16[256,1024]{1,0:T(8,128)(2,1)} %param.19) | copy-start | bytes 1572868
  122.3 2.9 copy-start.21
  122.3 4.3 %copy-start.28 = (bf16[4,256,256]{2,1,0:T(8,128)(2,1)}, bf16[4,256,256]{2,1,0:T(8,128)(2,1)S(1)}, u32[]{:S(2)}) copy-start(bf16[4,256,256]{2,1,0:T(8,128)(2,1)S(1)} %get-tuple-element.97.gated_ref) | copy-start | bytes 1572868
  122.3 2.9 collective-permute-start.5
  123.0 9.8 %collective-permute-start.7 = (bf16[2,256,1024]{2,1,0:T(8,128)(2,1)S(1)}, bf16[2,256,1024]{2,1,0:T(8,128)(2,1)}, u32[]{:S(2)}, u32[]{:S(2)}) collective-permute-start(bf16[2,256,1024]{2,1,0:T(8,128)(2,1)S(1)} %pad_maximum_fusion.1.pair_ref.outer_ref), channel_id=1, source_target_pairs={{0,1},{1,0},{2,3},{3,2},{4,5},{5,4},{6,7},{7,6},{8,9},{9,8},{10,11... | collective-permute-start | bytes 3145736 | tf_op jit(solution)/shard_map/ppermute | solution.py:47
  126.5 24.7 %collective-permute-start.6 = (bf16[2,256,1024]{2,1,0:T(8,128)(2,1)}, bf16[2,256,1024]{2,1,0:T(8,128)(2,1)}, u32[]{:S(2)}, u32[]{:S(2)}) collective-permute-start(bf16[2,256,1024]{2,1,0:T(8,128)(2,1)} %get-tuple-element.120), channel_id=1, source_target_pairs={{0,32},{1,33},{2,34},{3,35},{4,36},{5,37},{6,38},{7,39},{8,40},{9,... | collective-permute-start | bytes 3145736 | tf_op jit(solution)/shard_map/ppermute | solution.py:51
  131.1 20.2 %copy-start.6 = (bf16[272,1024]{1,0:T(8,128)(2,1)S(1)}, bf16[272,1024]{1,0:T(8,128)(2,1)}, u32[]{:S(2)}) copy-start(bf16[272,1024]{1,0:T(8,128)(2,1)} %copy-done.5) | copy-start | bytes 1671172
  131.1 20.2 %copy-start.13 = (bf16[272,1024]{1,0:T(8,128)(2,1)S(1)}, bf16[272,1024]{1,0:T(8,128)(2,1)}, u32[]{:S(2)}) copy-start(bf16[272,1024]{1,0:T(8,128)(2,1)} %copy-done.11) | copy-start | bytes 1671172
  153.0 1.3 copy-start
  154.3 3.5 %collective-permute-start.8 = (bf16[2,256,1024]{2,1,0:T(8,128)(2,1)S(1)}, bf16[2,256,1024]{2,1,0:T(8,128)(2,1)S(1)}, u32[]{:S(2)}, u32[]{:S(2)}) collective-permute-start(bf16[2,256,1024]{2,1,0:T(8,128)(2,1)S(1)} %get-tuple-element.78.own_ref), channel_id=1, source_target_pairs={{0,1},{1,0},{2,3},{3,2},{4,5},{5,4},{6,7},{7,6},{8,9},{9,8},{10,11... | collective-permute-start | bytes 3145736 | tf_op jit(solution)/shard_map/ppermute | solution.py:47
  176.7 4.2 %copy-start.34 = (bf16[4,256,1152]{2,1,0:T(8,128)(2,1)}, bf16[4,256,1152]{2,1,0:T(8,128)(2,1)S(1)}, u32[]{:S(2)}) copy-start(bf16[4,256,1152]{2,1,0:T(8,128)(2,1)S(1)} %get-tuple-element.88.grad_up_ref) | copy-start | bytes 7077892
  176.7 4.2 %copy-start.25 = (bf16[4,256,1152]{2,1,0:T(8,128)(2,1)}, bf16[4,256,1152]{2,1,0:T(8,128)(2,1)S(1)}, u32[]{:S(2)}) copy-start(bf16[4,256,1152]{2,1,0:T(8,128)(2,1)S(1)} %get-tuple-element.86.hidden_ref) | copy-start | bytes 7077892
  176.8 2.7 collective-permute-start.9
  195.9 24.8 %copy-start.1 = (f32[2,256,1024]{2,1,0:T(8,128)S(1)}, f32[2,256,1024]{2,1,0:T(8,128)}, u32[]{:S(2)}) copy-start(f32[2,256,1024]{2,1,0:T(8,128)} %copy-done) | copy-start | bytes 6291460
  195.9 24.8 %collective-permute-start.10 = (bf16[2,256,1024]{2,1,0:T(8,128)(2,1)}, bf16[2,256,1024]{2,1,0:T(8,128)(2,1)S(1)}, u32[]{:S(2)}, u32[]{:S(2)}) collective-permute-start(bf16[2,256,1024]{2,1,0:T(8,128)(2,1)} %get-tuple-element.118), channel_id=1, source_target_pairs={{0,32},{1,33},{2,34},{3,35},{4,36},{5,37},{6,38},{7,39},{8,40},{9,... | collective-permute-start | bytes 3145736 | tf_op jit(solution)/shard_map/ppermute | solution.py:51
  223.1 1.3 copy-start.3
  224.4 3.6 %collective-permute-start.11 = (bf16[2,256,1024]{2,1,0:T(8,128)(2,1)}, bf16[2,256,1024]{2,1,0:T(8,128)(2,1)S(1)}, u32[]{:S(2)}, u32[]{:S(2)}) collective-permute-start(bf16[2,256,1024]{2,1,0:T(8,128)(2,1)} %get-tuple-element.91.own_ref), channel_id=1, source_target_pairs={{0,1},{1,0},{2,3},{3,2},{4,5},{5,4},{6,7},{7,6},{8,9},{9,8},{10,11... | collective-permute-start | bytes 3145736 | tf_op jit(solution)/shard_map/ppermute | solution.py:47
  228.0 1.9 copy-start.19
  229.9 1.2 copy-start.22
  232.2 3.7 %copy-start.27 = (bf16[4,256,256]{2,1,0:T(8,128)(2,1)S(1)}, bf16[4,256,256]{2,1,0:T(8,128)(2,1)}, u32[]{:S(2)}) copy-start(bf16[4,256,256]{2,1,0:T(8,128)(2,1)} %copy-done.26) | copy-start | bytes 1572868
  232.2 3.7 %copy-start.29 = (bf16[4,256,256]{2,1,0:T(8,128)(2,1)S(1)}, bf16[4,256,256]{2,1,0:T(8,128)(2,1)}, u32[]{:S(2)}) copy-start(bf16[4,256,256]{2,1,0:T(8,128)(2,1)} %copy-done.28) | copy-start | bytes 1572868
  235.6 5.1 %collective-permute-start.12 = (f32[2,2,256]{2,1,0:T(2,128)S(1)}, f32[2,2,256]{2,1,0:T(2,128)S(1)}, u32[]{:S(2)}, u32[]{:S(2)}) collective-permute-start(f32[2,2,256]{2,1,0:T(2,128)S(1)} %broadcast_select_fusion.2), channel_id=1, source_target_pairs={{0,30},{1,31},{2,0},{3,1},{4,2},{5,3},{6,4},{7,5},{8,6},{9,7},{10,... | collective-permute-start | bytes 12296 | tf_op jit(solution)/shard_map/ppermute | solution.py:693
  236.0 4.9 %copy-start.7 = (bf16[272,1024]{1,0:T(8,128)(2,1)S(1)}, bf16[272,1024]{1,0:T(8,128)(2,1)}, u32[]{:S(2)}) copy-start(bf16[272,1024]{1,0:T(8,128)(2,1)} %copy-done.5) | copy-start | bytes 1671172
  236.0 4.9 %copy-start.10 = (bf16[272,1024]{1,0:T(8,128)(2,1)S(1)}, bf16[272,1024]{1,0:T(8,128)(2,1)}, u32[]{:S(2)}) copy-start(bf16[272,1024]{1,0:T(8,128)(2,1)} %copy-done.8) | copy-start | bytes 1671172
  236.0 4.9 %copy-start.14 = (bf16[272,1024]{1,0:T(8,128)(2,1)S(1)}, bf16[272,1024]{1,0:T(8,128)(2,1)}, u32[]{:S(2)}) copy-start(bf16[272,1024]{1,0:T(8,128)(2,1)} %copy-done.11) | copy-start | bytes 1671172
  236.0 4.9 %copy-start.17 = (bf16[272,1024]{1,0:T(8,128)(2,1)S(1)}, bf16[272,1024]{1,0:T(8,128)(2,1)}, u32[]{:S(2)}) copy-start(bf16[272,1024]{1,0:T(8,128)(2,1)} %copy-done.15) | copy-start | bytes 1671172
  236.0 4.9 %copy-start.20 = (f32[4,256,768]{2,1,0:T(8,128)S(1)}, f32[4,256,768]{2,1,0:T(8,128)}, u32[]{:S(2)}) copy-start(f32[4,256,768]{2,1,0:T(8,128)} %copy-done.18) | copy-start | bytes 9437188
  236.0 4.9 %copy-start.31 = (bf16[4,256,1024]{2,1,0:T(8,128)(2,1)S(1)}, bf16[4,256,1024]{2,1,0:T(8,128)(2,1)}, u32[]{:S(2)}) copy-start(bf16[4,256,1024]{2,1,0:T(8,128)(2,1)} %copy-done.30) | copy-start | bytes 6291460
  236.0 4.9 %copy-start.33 = (bf16[1024,768]{1,0:T(8,128)(2,1)S(1)}, bf16[1024,768]{1,0:T(8,128)(2,1)}, u32[]{:S(2)}) copy-start(bf16[1024,768]{1,0:T(8,128)(2,1)} %copy-done.32) | copy-start | bytes 4718596
  240.9 8.6 %copy-start.35 = (f32[4,256,1024]{2,1,0:T(8,128)S(1)}, f32[4,256,1024]{2,1,0:T(8,128)}, u32[]{:S(2)}) copy-start(f32[4,256,1024]{2,1,0:T(8,128)} %fusion) | copy-start | bytes 12582916
  249.1 6.3 %collective-permute-start.15 = (bf16[2,256,1024]{2,1,0:T(8,128)(2,1)}, bf16[2,256,1024]{2,1,0:T(8,128)(2,1)}, u32[]{:S(2)}, u32[]{:S(2)}) collective-permute-start(bf16[2,256,1024]{2,1,0:T(8,128)(2,1)} %get-tuple-element.105), channel_id=1, source_target_pairs={{0,1},{1,0},{2,3},{3,2},{4,5},{5,4},{6,7},{7,6},{8,9},{9,8},{10,11... | collective-permute-start | bytes 3145736 | tf_op jit(solution)/shard_map/ppermute | solution.py:47
  250.9 8.0 %collective-permute-start.13 = (bf16[2,256,1024]{2,1,0:T(8,128)(2,1)}, bf16[2,256,1024]{2,1,0:T(8,128)(2,1)S(1)}, u32[]{:S(2)}, u32[]{:S(2)}) collective-permute-start(bf16[2,256,1024]{2,1,0:T(8,128)(2,1)} %slice.156), channel_id=1, source_target_pairs={{0,1},{1,0},{2,3},{3,2},{4,5},{5,4},{6,7},{7,6},{8,9},{9,8},{10,11... | collective-permute-start | bytes 3145736 | tf_op jit(solution)/shard_map/ppermute | solution.py:47
  251.0 40.3 %all-to-all-start.2 = ((bf16[16,4,16,1152]{3,2,1,0:T(8,128)(2,1)}), bf16[16,4,16,1152]{3,2,1,0:T(8,128)(2,1)}, u32[]{:S(2)}, u32[]{:S(2)}) async-start(bf16[16,4,16,1152]{3,2,1,0:T(8,128)(2,1)} %bitcast.32), calls=%async_computation.2 | async-start | bytes 4718592 | tf_op jit(solution)/shard_map/all_to_all | solution.py:96
  255.4 3.5 %copy-start.36 = (f32[4,256,1024]{2,1,0:T(8,128)S(1)}, f32[4,256,1024]{2,1,0:T(8,128)}, u32[]{:S(2)}) copy-start(f32[4,256,1024]{2,1,0:T(8,128)} %fusion) | copy-start | bytes 12582916
  257.3 13.3 %copy-start.38 = (bf16[256,1024]{1,0:T(8,128)(2,1)S(1)}, bf16[256,1024]{1,0:T(8,128)(2,1)}, u32[]{:S(2)}) copy-start(bf16[256,1024]{1,0:T(8,128)(2,1)} %param.10) | copy-start | bytes 1572868
  257.3 13.3 %collective-permute-start.16 = (bf16[256,1024]{1,0:T(8,128)(2,1)S(1)}, bf16[256,1024]{1,0:T(8,128)(2,1)S(1)}, u32[]{:S(2)}, u32[]{:S(2)}) collective-permute-start(bf16[256,1024]{1,0:T(8,128)(2,1)S(1)} %fusion.15), channel_id=1, source_target_pairs={{0,32},{1,33},{2,34},{3,35},{4,36},{5,37},{6,38},{7,39},{8,40},{9,... | collective-permute-start | bytes 1572872 | tf_op jit(solution)/shard_map/ppermute | solution.py:51
  259.4 22.5 %copy-start.2 = (f32[2,256,1024]{2,1,0:T(8,128)S(1)}, f32[2,256,1024]{2,1,0:T(8,128)}, u32[]{:S(2)}) copy-start(f32[2,256,1024]{2,1,0:T(8,128)} %copy-done) | copy-start | bytes 6291460
  259.5 22.4 %collective-permute-start.14 = (bf16[256,1024]{1,0:T(8,128)(2,1)S(1)}, bf16[256,1024]{1,0:T(8,128)(2,1)S(1)}, u32[]{:S(2)}, u32[]{:S(2)}) collective-permute-start(bf16[256,1024]{1,0:T(8,128)(2,1)S(1)} %fusion.14), channel_id=1, source_target_pairs={{0,32},{1,33},{2,34},{3,35},{4,36},{5,37},{6,38},{7,39},{8,40},{9,... | collective-permute-start | bytes 1572872 | tf_op jit(solution)/shard_map/ppermute | solution.py:51
  271.1 11.9 %copy-start.4 = (f32[2,256,1024]{2,1,0:T(8,128)S(1)}, f32[2,256,1024]{2,1,0:T(8,128)}, u32[]{:S(2)}) copy-start(f32[2,256,1024]{2,1,0:T(8,128)} %copy-done.3) | copy-start | bytes 6291460
  298.7 19.1 %all-to-all-start.3 = ((bf16[8,16,3200]{2,1,0:T(8,128)(2,1)}), bf16[8,16,3200]{2,1,0:T(8,128)(2,1)S(1)}, u32[]{:S(2)}, u32[]{:S(2)}) async-start(bf16[8,16,3200]{2,1,0:T(8,128)(2,1)} %maximum_maximum_fusion), calls=%async_computation.4 | async-start | bytes 1638400 | tf_op jit(solution)/shard_map/all_to_all | solution.py:778
  317.8 7.5 %collective-permute-start.17 = (bf16[4,16,1536]{2,1,0:T(8,128)(2,1)S(1)}, bf16[4,16,1536]{2,1,0:T(8,128)(2,1)S(1)}, u32[]{:S(2)}, u32[]{:S(2)}) collective-permute-start(bf16[4,16,1536]{2,1,0:T(8,128)(2,1)S(1)} %pad_maximum_fusion.5), channel_id=1, source_target_pairs={{0,64},{64,0},{1,65},{65,1},{2,66},{66,2},{3,67},{67,3},{4,68},{68... | collective-permute-start | bytes 589832 | tf_op jit(solution)/shard_map/ppermute | solution.py:767
  (6 other events, 5.6 us)
Sparse Core Ops, SparseCore 0:
  25.5 89.6 all-gather.1
  196.0 100.6 reduce-scatter.1

commit v3 on v2

--- a/solution.py
+++ b/solution.py
@@ -31,7 +31,6 @@
 
 TO_CORE = moves(lambda z, plane, core: (z, plane, 1 - core))
 TO_Z = moves(lambda z, plane, core: (1 - z, plane, core))
-TO_BOTH = moves(lambda z, plane, core: (1 - z, plane, 1 - core))
 TO_FOLLOWING = [(index, index + 1) for index in range(2 * HALF - 1)]
 TO_PREVIOUS = moves(lambda z, plane, core: (z, (plane - 1) % PLANE, core))
 TEAMS = [
@@ -49,10 +48,6 @@
 
 def to_z(value):
     return lax.ppermute(value, "fsdp", TO_Z)
-
-
-def to_both(value):
-    return lax.ppermute(value, "fsdp", TO_BOTH)
 
 
 def norm_scale(values):
@@ -162,13 +157,6 @@
     return jnp.where(slot % 2 == 0, even, odd)
 
 
-def pick_slot(slot, *values):
-    picked = values[0]
-    for index in range(1, 4):
-        picked = jnp.where(slot == index, values[index], picked)
-    return picked
-
-
 def shifted_in(values, rows_before, steps):
     moved = pltpu.roll(values, steps, 0)
     row = lax.broadcasted_iota(jnp.int32, values.shape, 0)
@@ -198,7 +186,7 @@
 
 
 def project_kernel(
-    slot0_ref, slot1_ref, slot2_ref, slot3_ref, first_ref,
+    pair_ref, other_ref, pair_edge_ref, other_edge_ref, first_ref,
     normed_ref, proj_ref, mixed_ref, earlier_ref, in_ref, out_ref, gains_ref, taps_ref,
     column, taps_column,
 ):
@@ -231,10 +219,8 @@
         mixed = (projected[:, :channels] * projected[:, 2 * channels :]).astype(jnp.bfloat16)
         return normed, projected, mixed
 
-    values = pick_slot(slot, slot0_ref[...], slot1_ref[...], slot2_ref[...], slot3_ref[...])
-    length = normed_ref.shape[1]
-    normed_ref[0], proj_ref[0], mixed_ref[0] = project(values[:length])
-    edge = project(values[length:])[2]
+    normed_ref[0], proj_ref[0], mixed_ref[0] = project(pick(slot, pair_ref[0], other_ref[0]))
+    edge = project(pick(slot, pair_edge_ref[0], other_edge_ref[0]))[2]
     earlier_ref[0] = edge.astype(jnp.float32)
 
 
@@ -257,11 +243,8 @@
     store_pair(slot, branch, keep_ref, sent_ref)
 
 
-def middle_kernel(
-    own_ref, far_ref, branch_ref, crossed_ref, gains_ref, middle_ref, normed_ref
-):
-    inputs = jnp.where(pl.program_id(0) == 0, own_ref[...], far_ref[...])
-    middle = inputs[: branch_ref.shape[1]].astype(jnp.float32) + branch_ref[0]
+def middle_kernel(inputs_ref, branch_ref, crossed_ref, gains_ref, middle_ref, normed_ref):
+    middle = inputs_ref[0].astype(jnp.float32) + branch_ref[0]
     middle += crossed_ref[0].astype(jnp.float32)
     middle_ref[0] = middle
     normed_ref[0] = (middle * norm_scale(middle) * gains_ref[1:2]).astype(jnp.bfloat16)
@@ -409,7 +392,7 @@
 
 def project_back_kernel(
     grad_conv_ref, later_ref, proj_ref, grad_out_ref, normed_ref, in_ref, taps_ref,
-    slot0_ref, slot1_ref, slot2_ref, slot3_ref, part_ref, spare_ref,
+    pair_ref, other_ref, part_ref, spare_ref,
     pack_ref, keep_ref, sent_ref,
     total, gain_rows,
 ):
@@ -440,8 +423,7 @@
     total[...] += contract_rows(normed_ref[0], grad_projected)
     grad_normed = contract_cols(grad_projected, in_ref[...])
     store_pair(slot, grad_normed, keep_ref, sent_ref)
-    values = pick_slot(slot, slot0_ref[...], slot1_ref[...], slot2_ref[...], slot3_ref[...])
-    values = values[: grad_normed.shape[0]].astype(jnp.float32)
+    values = pick(slot, pair_ref[0], other_ref[0]).astype(jnp.float32)
     gain_rows[0:1] += jnp.sum(grad_normed * values * norm_scale(values), axis=0, keepdims=True)
 
     @pl.when(slot == 3)
@@ -498,8 +480,7 @@
 
     before = lax.ppermute(tokens[length - EDGE :], "fsdp", TO_FOLLOWING)
     extended = jnp.concatenate([tokens, before], 0)
-    slots = [extended, to_core(extended), to_z(extended), to_both(extended)]
-    outer_z = to_z(cotangent)
+    extended_z = to_z(extended)
 
     block = 4 * rows
     rest = w_down.shape[0] - block
@@ -529,9 +510,13 @@
         ],
         2,
     )
+    first_pack, extended_z = lax.optimization_barrier((first_pack, extended_z))
+    pair = jnp.stack([extended, extended_z])
+    other = to_core(pair)
     first_all = plane_swap(jnp.broadcast_to(first_pack, (PLANE,) + first_pack.shape))
-    first_all, slots, outer_z = lax.optimization_barrier((first_all, slots, outer_z))
+    first_all, outer = lax.optimization_barrier((first_all, cotangent))
     first_all = first_all.reshape(PLANE, 4 * rows, -1)
+    outer_z = to_z(outer)
 
     main_rows = ff_all[:, 2 * units : 2 * units + model_width].reshape(2, PLANE, 2 * rows, -1)
     main_rows = main_rows.transpose(1, 0, 2, 3).reshape(PLANE, block, model_width)
@@ -540,20 +525,23 @@
     rest_rows = rest_rows.transpose(0, 2, 1, 3).reshape(PLANE, rest, model_width)
     down_full = jnp.concatenate([main_rows, rest_rows], 1).reshape(units, model_width)
 
-    team_slots = [whole(length + EDGE, model_width)] * 4
+    team_pairs = [per_pair(length, model_width)] * 2
     slot_wide, slot_narrow = (4, length, model_width), (4, length, channels)
     pair_wide = (2, length, model_width)
     pairs = [per_pair(length, model_width)] * 2
     narrow = per_slot(length, channels)
     out_gate = per_slot(length, channels, 1)
     edge, edge_after = per_slot(EDGE, channels), per_slot(8, channels)
+    team_edges = [
+        pl.BlockSpec((1, EDGE, model_width), lambda slot: (slot // 2, length // EDGE, 0))
+    ] * 2
     out_matrix, in_matrix = whole(channels, model_width), whole(model_width, in_width)
     taps = whole(8, channels)
 
     normed, projected, mixed, earlier, in_full, out_full, gains, kernel = run(
         project_kernel,
         (4,),
-        team_slots + [whole(*first_all.shape)],
+        team_pairs + team_edges + [whole(*first_all.shape)],
         [
             per_slot(length, model_width),
             per_slot(length, in_width),
@@ -576,8 +564,8 @@
         ],
         [pltpu.VMEM((model_width, SPARE), wide), pltpu.VMEM((channels, SPARE), wide)],
         24,
-        4,
-        [*slots, first_all],
+        0.2,
+        [pair, other, pair, other, first_all],
     )
 
     def by_core(first, second):
@@ -596,13 +584,14 @@
         ],
         [],
         16,
-        2,
+        0.2,
         [mixed, earlier, projected, kernel, out_full],
     )
     branch_pair = core_sum(branch_keep, branch_sent)
-    outer_pair = jnp.stack([cotangent, outer_z])
+    branch_sent, outer_z = lax.optimization_barrier((branch_pair.astype(low), outer_z))
+    outer_pair = jnp.stack([outer, outer_z])
     outer_other = to_core(outer_pair)
-    branch_other = to_z(branch_pair.astype(low))
+    branch_other = to_z(branch_sent)
     branch_other, down_full, outer_other = lax.optimization_barrier(
         (branch_other, down_full, outer_other)
     )
@@ -612,13 +601,13 @@
     middle, normed_two = run(
         middle_kernel,
         (2,),
-        team_slots[:2] + [one, crossed, gain_rows],
+        [one, one, crossed, gain_rows],
         [one, one],
         [array(pair_wide, wide), array(pair_wide, low)],
         [],
         20,
         3,
-        [slots[0], slots[2], branch_pair, branch_other, gains],
+        [pair, branch_pair, branch_other, gains],
     )
     normed_swap = to_core(normed_two)
 
@@ -641,9 +630,6 @@
     grad_sent = grad_pair.astype(low)
     grad_other = to_z(grad_sent)
 
-    grad_sent, hidden, grad_gate, grad_upper = lax.optimization_barrier(
-        (grad_sent, hidden, grad_gate, grad_upper)
-    )
     (ff_grads,) = run(
         ff_grads_kernel,
         (4,),
@@ -728,7 +714,7 @@
             in_matrix,
             taps,
         ]
-        + team_slots
+        + team_pairs
         + [whole(*part_shape), whole(*spare_shape)],
         [whole(*first_all.shape)] + pairs,
         [array(first_all.shape, low), array(pair_wide, wide), array(pair_wide, low)],
@@ -743,7 +729,8 @@
             normed,
             in_full,
             kernel,
-            *slots,
+            pair,
+            other,
             out_part,
             spare_part,
         ],

time: 335 us -> 338 us (level)
  waiting for transfers between devices: 133 us -> 149 us
  starting transfers between devices: 68.9 us -> 53.9 us
  Pallas kernels: 61.5 us -> 66.3 us
    ppermute x6, starting transfers between devices: 36.9 us -> 1.79 us  [to_z(): return lax.ppermute(value, 'fsdp', TO_Z)]
    all_to_all x2, waiting for transfers between devices: 6.95 us -> 37.7 us  [plane_swap(): lax.all_to_all(blocks, 'fsdp', 0, 0, tiled=True, axis_index_groups=PLANES)]
    ppermute x6, waiting for transfers between devices: 90.4 us -> 76.8 us  [to_z(): return lax.ppermute(value, 'fsdp', TO_Z)]
    ppermute x8, starting transfers between devices: 3.91 us -> 16.2 us  [to_core(): return lax.ppermute(value, 'fsdp', TO_CORE)]
    pallas_call x10, Pallas kernels: 61.5 us -> 66.3 us  [run(): pl.pallas_call(kernel, grid=grid, in_specs=in_specs, out_specs=out_specs,...]
    ppermute x1, starting transfers between devices: 0.3 us -> 5.04 us  [body(): received = lax.ppermute(sent, 'fsdp', TO_PREVIOUS)]
    ppermute x1, waiting for transfers between devices: 4.35 us -> 0.96 us  [body(): before = lax.ppermute(tokens[length - EDGE:], 'fsdp', TO_FOLLOWING)]
    unnamed x92 -> x80, local copies, waits for them, and re-layouts: 14.3 us -> 12.4 us
  transfers between devices with their start and end apart: 24 -> 23, of which waited for: 14 -> 16; matrix products, arithmetic and copies ran while one was open for 9% -> 9% of each run, Pallas kernels for 8% -> 9%
where the time goes in v3:
time: 338 us; the launch traced here: 337 us
  waiting for transfers between devices  149 us (44%)
  Pallas kernels  66.3 us (20%)
  starting transfers between devices  53.9 us (16%)
  local copies, waits for them, and re-layouts  31 us (9%)
  other arithmetic  17.6 us (5%)
  between operations  14.8 us (4%)
  matrix products  4.45 us (1%)
    ppermute x6, waiting for transfers between devices, to_z(): return lax.ppermute(value, 'fsdp', TO_Z)  76.8 us
    pallas_call x10, Pallas kernels, run(): pl.pallas_call(kernel, grid=grid, in_specs=in_specs, out_specs=out_specs,...  66.3 us
    all_to_all x2, waiting for transfers between devices, plane_swap(): lax.all_to_all(blocks, 'fsdp', 0, 0, tiled=True, axis_index_groups=PLANES)  37.7 us
    ppermute x8, starting transfers between devices, to_core(): return lax.ppermute(value, 'fsdp', TO_CORE)  16.2 us
    all_to_all x2, starting transfers between devices, plane_swap(): lax.all_to_all(blocks, 'fsdp', 0, 0, tiled=True, axis_index_groups=PLANES)  13.5 us
    unnamed x80, local copies, waits for them, and re-layouts  12.4 us
    all_to_all x1, waiting for transfers between devices, body(): lax.all_to_all(jnp.concatenate([blocks, blocks]), ('rep', 'fsdp'), 0, 0,...  11.7 us
    ppermute x8, waiting for transfers between devices, to_core(): return lax.ppermute(value, 'fsdp', TO_CORE)  9.7 us
  transfers between devices with their start and end apart: 23, of which 16 were waited for; matrix products, arithmetic and copies ran while one was open for 9% of the time, Pallas kernels for 9%

profile of v3, /device:TPU:1, one launch (start us, length us, event | category | flops | bytes accessed | tf_op | source)
XLA Modules:
  0.0 336.8 jit_solution(6735511237153684494)
XLA Ops:
  8.0 1.5 reshape.132
  12.9 5.0 %all-to-all-start = ((bf16[4,16,3200]{2,1,0:T(8,128)(2,1)}), bf16[4,16,3200]{2,1,0:T(8,128)(2,1)S(1)}, u32[]{:S(2)}, u32[]{:S(2)}) async-start(bf16[4,16,3200]{2,1,0:T(8,128)(2,1)} %pad_maximum_fusion.4), calls=%async_computation | async-start | bytes 819200 | tf_op jit(solution)/shard_map/all_to_all | solution.py:87
  17.8 6.7 %all-to-all-done = bf16[4,16,3200]{2,1,0:T(8,128)(2,1)S(1)} async-done(((bf16[4,16,3200]{2,1,0:T(8,128)(2,1)}), bf16[4,16,3200]{2,1,0:T(8,128)(2,1)S(1)}, u32[]{:S(2)}, u32[]{:S(2)}) %all-to-all-start) | async-done | bytes 409632 | tf_op jit(solution)/shard_map/all_to_all | solution.py:87
  25.5 4.1 %collective-permute-start = (bf16[16,1024]{1,0:T(8,128)(2,1)S(1)}, bf16[16,1024]{1,0:T(8,128)(2,1)S(1)}, u32[]{:S(2)}, u32[]{:S(2)}) collective-permute-start(bf16[16,1024]{1,0:T(8,128)(2,1)S(1)} %slice.137), channel_id=1, source_target_pairs={{0,1},{1,2},{2,3},{3,4},{4,5},{5,6},{6,7},{7,8},{8,9},{9,10},{10,1... | collective-permute-start | bytes 98312 | tf_op jit(solution)/shard_map/ppermute | solution.py:481
  29.6 1.0 collective-permute-done
  30.9 10.1 %collective-permute-done.1 = bf16[272,1024]{1,0:T(8,128)(2,1)S(1)} collective-permute-done((bf16[272,1024]{1,0:T(8,128)(2,1)S(1)}, bf16[272,1024]{1,0:T(8,128)(2,1)S(1)}, u32[]{:S(2)}, u32[]{:S(2)}) %collective-permute-start.1) | collective-permute-done | bytes 557088 | tf_op jit(solution)/shard_map/ppermute | solution.py:50
  41.0 1.7 broadcast_in_dim.10
  42.7 8.8 %all-to-all-start.1 = ((bf16[16,4,16,1152]{3,2,1,0:T(8,128)(2,1)}), bf16[16,4,16,1152]{3,2,1,0:T(8,128)(2,1)S(1)}, u32[]{:S(2)}, u32[]{:S(2)}) async-start(bf16[16,4,16,1152]{3,2,1,0:T(8,128)(2,1)} %broadcast_in_dim.10), calls=%async_computation.1 | async-start | bytes 4718592 | tf_op jit(solution)/shard_map/all_to_all | solution.py:91
  51.6 1.3 pad_maximum_fusion.1.pair_ref.pair_edge_ref.inputs_ref
  52.9 2.6 collective-permute-start.2
  55.5 33.2 %all-to-all-done.1 = bf16[16,4,16,1152]{3,2,1,0:T(8,128)(2,1)S(1)} async-done(((bf16[16,4,16,1152]{3,2,1,0:T(8,128)(2,1)}), bf16[16,4,16,1152]{3,2,1,0:T(8,128)(2,1)S(1)}, u32[]{:S(2)}, u32[]{:S(2)}) %all-to-all-start.1) | async-done | bytes 2359328 | tf_op jit(solution)/shard_map/all_to_all | solution.py:91
  88.7 4.9 %shard_map.177 = (bf16[4,256,1024]{2,1,0:T(8,128)(2,1)S(1)}, f32[4,256,768]{2,1,0:T(8,128)S(1)}, bf16[4,256,256]{2,1,0:T(8,128)(2,1)S(1)}, f32[4,16,256]{2,1,0:T...) custom-call(bf16[2,272,1024]{2,1,0:T(8,128)(2,1)S(1)} %pad_maximum_f, ...), custom_call_target="tpu_custom_call" | custom-call | flops 230000000 | tf_op jit(solution)/shard_map/pallas_call | solution.py:138
  93.7 1.4 copy-done.14
  95.0 1.2 copy-done.16
  96.3 1.7 shard_map.178
  98.3 8.6 %collective-permute-start.3 = (bf16[2,256,1024]{2,1,0:T(8,128)(2,1)S(1)}, bf16[2,256,1024]{2,1,0:T(8,128)(2,1)S(1)}, u32[]{:S(2)}, u32[]{:S(2)}) collective-permute-start(bf16[2,256,1024]{2,1,0:T(8,128)(2,1)S(1)} %get-tuple-element.68), channel_id=1, source_target_pairs={{0,1},{1,0},{2,3},{3,2},{4,5},{5,4},{6,7},{7,6},{8,9},{9,8},{10,11... | collective-permute-start | bytes 3145736 | tf_op jit(solution)/shard_map/ppermute | solution.py:46
  106.9 2.3 collective-permute-done.3
  109.2 1.4 fusion.17
  110.6 9.8 %collective-permute-done.4 = bf16[256,1024]{1,0:T(8,128)(2,1)S(1)} collective-permute-done((bf16[256,1024]{1,0:T(8,128)(2,1)S(1)}, bf16[256,1024]{1,0:T(8,128)(2,1)S(1)}, u32[]{:S(2)}, u32[]{:S(2)}) %collective-permute-start.4) | collective-permute-done | bytes 524320 | tf_op jit(solution)/shard_map/ppermute | solution.py:50
  120.6 1.1 pad_maximum_fusion.2.pair_ref.outer_ref
  121.6 1.0 collective-permute-start.6
  122.6 1.0 slice.183
  123.5 1.8 slice.182
  125.6 1.7 pad_maximum_fusion
  127.3 17.2 %collective-permute-done.5.crossed_ref = bf16[2,256,1024]{2,1,0:T(8,128)(2,1)} collective-permute-done((bf16[2,256,1024]{2,1,0:T(8,128)(2,1)}, bf16[2,256,1024]{2,1,0:T(8,128)(2,1)}, u32[]{:S(2)}, u32[]{:S(2)}) %collective-permute-start.5) | collective-permute-done | bytes 1048608 | tf_op jit(solution)/shard_map/ppermute | solution.py:50
  144.5 1.7 shard_map.179
  146.2 1.3 copy-done.3
  147.6 1.8 collective-permute-start.7
  149.3 2.3 collective-permute-done.7.swap_ref
  151.6 19.0 %shard_map.180 = (bf16[4,256,1152]{2,1,0:T(8,128)(2,1)S(1)}, bf16[4,256,1152]{2,1,0:T(8,128)(2,1)S(1)}, bf16[4,256,1152]{2,1,0:T(8,128)(2,1)S(1)}, f32[2,256,1024]{2,1,0:T(8,128)S(1)}, bf16[2,256,1024]{2,1,0:T(8,128)(2,1)S(1)}) custom-call(bf16[2,256,1024]{2,1,0:T(8,128)(2,1)S(1)} %get-tuple-element.75.own_ref, ...), custom_call_target="tpu_custom_call" | custom-call | flops 24149999616 | tf_op jit(solution)/shard_map/pallas_call | solution.py:138
  170.7 1.0 copy-done.20
  171.7 1.4 copy-done.25
  173.1 15.9 %shard_map.181 = bf16[1024,3456]{1,0:T(8,128)(2,1)} custom-call(bf16[2,256,1024]{2,1,0:T(8,128)(2,1)S(1)} %get-tuple-element.75.own_ref, bf16[2,256,1024]{2,1,0:T(8,128)(2,1)S(1)} %collective-permute-done.7.swap_ref, bf16[2,256,1024]{2,1,0:T(8,128)(2,1)} %pad_maximum_fusion.2.pair_ref.outer_ref, bf16[2,256,1024]{2,1,0:T(8,128)(2,1)} %collective-permute-done.6.other_ref, ...), custom_call_target="tpu_custom_call" | custom-call | flops 18400000000 | tf_op jit(solution)/shard_map/pallas_call | solution.py:138
  189.4 2.5 collective-permute-done.8
  192.7 0.9 copy-done.24
  194.3 4.5 %fusion = f32[4,256,1024]{2,1,0:T(8,128)} fusion(bf16[4,256,1152]{2,1,0:T(8,128)(2,1)S(1)} %copy-done.24, bf16[1152,1024]{1,0:T(8,128)(2,1)S(1)} %bitcast.111), kind=kOutput, calls=%fused_computation.1 | convolution fusion | flops 2415919104 | bytes 8912896 | tf_op jit(solution)/shard_map/dot_general | solution.py:649
  198.8 18.2 %collective-permute-done.9.crossed_ref = bf16[2,256,1024]{2,1,0:T(8,128)(2,1)S(1)} collective-permute-done((bf16[2,256,1024]{2,1,0:T(8,128)(2,1)S(1)}, bf16[2,256,1024]{2,1,0:T(8,128)(2,1)S(1)}, u32[]{:S(2)}, u32[]{:S(2)}) %collective-permute-start.9) | collective-permute-done | bytes 1048608 | tf_op jit(solution)/shard_map/ppermute | solution.py:50
  217.0 3.6 %shard_map.182 = (f32[2,256,1024]{2,1,0:T(8,128)S(1)}, bf16[2,256,1024]{2,1,0:T(8,128)(2,1)}, f32[1,1024]{1,0:T(1,128)S(1)}) custom-call(f32[2,256,1024]{2,1,0:T(8,128)S(1)} %get-tuple-element.113.grad_ref, bf16[2,256,1024]{2,1,0:T(8,128)(2,1)S(1)} %collective-permute-done.9.crossed_ref, f32[2,256,1024]{2,1,0:T(8,128)S(1)} %copy-done.4, ...), custom_call_target="tpu_custom_call" | custom-call | flops 4600000000 | tf_op jit(solution)/shard_map/pallas_call | solution.py:138
  220.5 1.3 copy-done.6
  221.9 1.1 collective-permute-start.10
  223.0 2.6 collective-permute-done.10.swap_ref
  225.7 2.2 copy-done.1
  227.8 3.7 %shard_map.183 = (bf16[4,256,256]{2,1,0:T(8,128)(2,1)S(1)}, f32[4,256,256]{2,1,0:T(8,128)S(1)}) custom-call(bf16[2,256,1024]{2,1,0:T(8,128)(2,1)} %get-tuple-element.85.own_ref, bf16[2,256,1024]{2,1,0:T(8,128)(2,1)} %collective-permute-done.10.swap_ref, bf16[256,1024]{1,0:T(8,128)(2,1)S(1)} %copy-done.11, f32[4,256,256]{2,1,0:T(8,128)S(1)} %copy-done.19, ...), custom_call_target="tpu_custom_call" | custom-call | flops 2300000000 | tf_op jit(solution)/shard_map/pallas_call | solution.py:138
  231.5 5.0 %collective-permute-start.11 = (f32[2,2,256]{2,1,0:T(2,128)S(1)}, f32[2,2,256]{2,1,0:T(2,128)S(1)}, u32[]{:S(2)}, u32[]{:S(2)}) collective-permute-start(f32[2,2,256]{2,1,0:T(2,128)S(1)} %broadcast_select_fusion.2), channel_id=1, source_target_pairs={{0,30},{1,31},{2,0},{3,1},{4,2},{5,3},{6,4},{7,5},{8,6},{9,7},{10,... | collective-permute-start | bytes 12296 | tf_op jit(solution)/shard_map/ppermute | solution.py:679
  236.6 4.9 %shard_map.184 = (bf16[16,64,256]{2,1,0:T(8,128)(2,1)S(1)}, f32[16,64,128]{2,1,0:T(8,128)S(1)}) custom-call(bf16[2,256,1024]{2,1,0:T(8,128)(2,1)} %get-tuple-element.85.own_ref, bf16[2,256,1024]{2,1,0:T(8,128)(2,1)} %collective-permute-done.10.swap_ref, bf16[4,256,256]{2,1,0:T(8,128)(2,1)S(1)} %copy-done.22, ...), custom_call_target="tpu_custom_call" | custom-call | flops 2875000064 | tf_op jit(solution)/shard_map/pallas_call | solution.py:138
  241.6 9.2 %shard_map.185 = (bf16[16,64,1152]{2,1,0:T(8,128)(2,1)}, f32[2,256,1024]{2,1,0:T(8,128)S(1)}, bf16[2,256,1024]{2,1,0:T(8,128)(2,1)}) custom-call(f32[4,256,256]{2,1,0:T(8,128)S(1)} %get-tuple-element.87.grad_conv_ref, f32[4,8,256]{2,1,0:T(8,128)S(1)} %select_maximum_fusion.later_ref, f32[4,256,768]{2,1,0:T(8,128)S(1)} %copy-done.2, ...), custom_call_target="tpu_custom_call" | custom-call | flops 9200000000 | tf_op jit(solution)/shard_map/pallas_call | solution.py:138
  251.8 1.0 slice.156
  252.8 4.7 %all-to-all-start.2 = ((bf16[16,4,16,1152]{3,2,1,0:T(8,128)(2,1)}), bf16[16,4,16,1152]{3,2,1,0:T(8,128)(2,1)}, u32[]{:S(2)}, u32[]{:S(2)}) async-start(bf16[16,4,16,1152]{3,2,1,0:T(8,128)(2,1)} %bitcast.34), calls=%async_computation.2 | async-start | bytes 4718592 | tf_op jit(solution)/shard_map/all_to_all | solution.py:91
  257.5 1.8 convert_add_fusion
  260.6 1.1 collective-permute-start.13
  261.6 10.7 %collective-permute-done.15 = bf16[256,1024]{1,0:T(8,128)(2,1)S(1)} collective-permute-done((bf16[256,1024]{1,0:T(8,128)(2,1)S(1)}, bf16[256,1024]{1,0:T(8,128)(2,1)S(1)}, u32[]{:S(2)}, u32[]{:S(2)}) %collective-permute-start.15) | collective-permute-done | bytes 524320 | tf_op jit(solution)/shard_map/ppermute | solution.py:50
  272.7 10.8 %collective-permute-done.13 = bf16[256,1024]{1,0:T(8,128)(2,1)S(1)} collective-permute-done((bf16[256,1024]{1,0:T(8,128)(2,1)S(1)}, bf16[256,1024]{1,0:T(8,128)(2,1)S(1)}, u32[]{:S(2)}, u32[]{:S(2)}) %collective-permute-start.13) | collective-permute-done | bytes 524320 | tf_op jit(solution)/shard_map/ppermute | solution.py:50
  283.5 1.1 fusion.13
  284.6 1.4 fusion.7
  286.0 4.5 %all-to-all-done.2 = bf16[16,4,16,1152]{3,2,1,0:T(8,128)(2,1)} async-done(((bf16[16,4,16,1152]{3,2,1,0:T(8,128)(2,1)}), bf16[16,4,16,1152]{3,2,1,0:T(8,128)(2,1)}, u32[]{:S(2)}, u32[]{:S(2)}) %all-to-all-start.2) | async-done | bytes 2359328 | tf_op jit(solution)/shard_map/all_to_all | solution.py:91
  290.5 2.0 reduce_sum.32
  292.5 5.3 %reduce-scatter.2.cloned.1.call-done = bf16[2,32,3456]{2,1,0:T(8,128)(2,1)} async-done(((bf16[2,512,3456]{2,1,0:T(8,128)(2,1)}), bf16[2,32,3456]{2,1,0:T(8,128)(2,1)}) %reduce-scatter.2.cloned.1.call-update) | async-done | bytes 442384 | tf_op jit(solution)/shard_map/reduce_scatter | solution.py:107
  297.8 1.0 slice.196
  298.8 1.0 maximum_maximum_fusion
  299.8 7.8 %all-to-all-start.3 = ((bf16[8,16,3200]{2,1,0:T(8,128)(2,1)}), bf16[8,16,3200]{2,1,0:T(8,128)(2,1)S(1)}, u32[]{:S(2)}, u32[]{:S(2)}) async-start(bf16[8,16,3200]{2,1,0:T(8,128)(2,1)} %maximum_maximum_fusion), calls=%async_computation.4 | async-start | bytes 1638400 | tf_op jit(solution)/shard_map/all_to_all | solution.py:765
  308.6 11.7 %all-to-all-done.3.blocks_ref = bf16[8,16,3200]{2,1,0:T(8,128)(2,1)S(1)} async-done(((bf16[8,16,3200]{2,1,0:T(8,128)(2,1)}), bf16[8,16,3200]{2,1,0:T(8,128)(2,1)S(1)}, u32[]{:S(2)}, u32[]{:S(2)}) %all-to-all-start.3) | async-done | bytes 819232 | tf_op jit(solution)/shard_map/all_to_all | solution.py:765
  320.8 1.7 shard_map.186
  323.3 1.4 reshape.149
  325.6 1.4 reshape.151
  (154 shorter events, 16.7 us)
Async XLA Ops:
  7.2 3.1 copy-start.34
  9.5 1.7 copy-start.35
  10.9 13.8 %slice-start = ((bf16[72,1024]{1,0:T(8,128)(2,1)}), bf16[8,1024]{1,0:T(8,128)(2,1)S(1)}, s32[]{:S(2)}) async-start(bf16[72,1024]{1,0:T(8,128)(2,1)} %param.18), calls=%async_computation.7 | async-start | bytes 32768 | tf_op jit(solution)/shard_map/slice | solution.py:496
  10.9 13.7 %slice-start.1 = ((bf16[72,1024]{1,0:T(8,128)(2,1)}), bf16[64,1024]{1,0:T(8,128)(2,1)S(1)}, s32[]{:S(2)}) async-start(bf16[72,1024]{1,0:T(8,128)(2,1)} %param.18), calls=%async_computation.8 | async-start | bytes 262144 | tf_op jit(solution)/shard_map/slice | solution.py:495
  11.8 13.7 %copy-start.28 = (bf16[256,1024]{1,0:T(8,128)(2,1)S(1)}, bf16[256,1024]{1,0:T(8,128)(2,1)}, u32[]{:S(2)}) copy-start(bf16[256,1024]{1,0:T(8,128)(2,1)} %param.10) | copy-start | bytes 1572868
  12.9 17.8 %copy-start.37 = (bf16[16,3]{0,1:T(4,128)(2,1)S(1)}, bf16[16,3]{0,1:T(4,128)(2,1)}, u32[]{:S(2)}) copy-start(bf16[16,3]{0,1:T(4,128)(2,1)} %param.13) | copy-start | bytes 292
  12.9 17.9 %copy-start.36 = (bf16[16,1024]{1,0:T(8,128)(2,1)S(1)}, bf16[16,1024]{1,0:T(8,128)(2,1)}, u32[]{:S(2)}) copy-start(bf16[16,1024]{1,0:T(8,128)(2,1)} %param.14) | copy-start | bytes 98308
  12.9 11.7 %all-to-all-start = ((bf16[4,16,3200]{2,1,0:T(8,128)(2,1)}), bf16[4,16,3200]{2,1,0:T(8,128)(2,1)S(1)}, u32[]{:S(2)}, u32[]{:S(2)}) async-start(bf16[4,16,3200]{2,1,0:T(8,128)(2,1)} %pad_maximum_fusion.4), calls=%async_computation | async-start | bytes 819200 | tf_op jit(solution)/shard_map/all_to_all | solution.py:87
  17.8 104.7 %all-gather.2.cloned.1.call-start = ((), (), s32[]{:S(2)}) async-start(), calls=%async_computation.5 | async-start | bytes 7520256 | tf_op jit(solution)/shard_map/all_gather | solution.py:96
  25.5 5.1 %collective-permute-start = (bf16[16,1024]{1,0:T(8,128)(2,1)S(1)}, bf16[16,1024]{1,0:T(8,128)(2,1)S(1)}, u32[]{:S(2)}, u32[]{:S(2)}) collective-permute-start(bf16[16,1024]{1,0:T(8,128)(2,1)S(1)} %slice.137), channel_id=1, source_target_pairs={{0,1},{1,2},{2,3},{3,4},{4,5},{5,6},{6,7},{7,8},{8,9},{9,10},{10,1... | collective-permute-start | bytes 98312 | tf_op jit(solution)/shard_map/ppermute | solution.py:481
  30.6 12.2 %copy-start.31 = (bf16[272,1024]{1,0:T(8,128)(2,1)}, bf16[272,1024]{1,0:T(8,128)(2,1)S(1)}, u32[]{:S(2)}) copy-start(bf16[272,1024]{1,0:T(8,128)(2,1)S(1)} %constant_dynamic-update-slice_fusion) | copy-start | bytes 1671172
  30.6 10.4 %collective-permute-start.1 = (bf16[272,1024]{1,0:T(8,128)(2,1)S(1)}, bf16[272,1024]{1,0:T(8,128)(2,1)S(1)}, u32[]{:S(2)}, u32[]{:S(2)}) collective-permute-start(bf16[272,1024]{1,0:T(8,128)(2,1)S(1)} %constant_dynamic-update-slice_fusion), channel_id=1, source_target_pairs={{0,32},{1,33},{2,34},{3,35},{4,36},{5,37},{6,38},{7,39},{8,40},{9,... | collective-permute-start | bytes 1671176 | tf_op jit(solution)/shard_map/ppermute | solution.py:50
  41.0 1.7 copy-start.32
  42.7 46.0 %all-to-all-start.1 = ((bf16[16,4,16,1152]{3,2,1,0:T(8,128)(2,1)}), bf16[16,4,16,1152]{3,2,1,0:T(8,128)(2,1)S(1)}, u32[]{:S(2)}, u32[]{:S(2)}) async-start(bf16[16,4,16,1152]{3,2,1,0:T(8,128)(2,1)} %broadcast_in_dim.10), calls=%async_computation.1 | async-start | bytes 4718592 | tf_op jit(solution)/shard_map/all_to_all | solution.py:91
  51.5 246.2 %reduce-scatter.2.cloned.1.call-start = ((), (), s32[]{:S(2)}) async-start(), calls=%async_computation.6 | async-start | bytes 7520256 | tf_op jit(solution)/shard_map/reduce_scatter | solution.py:107
  52.9 35.8 %collective-permute-start.2 = (bf16[2,272,1024]{2,1,0:T(8,128)(2,1)S(1)}, bf16[2,272,1024]{2,1,0:T(8,128)(2,1)}, u32[]{:S(2)}, u32[]{:S(2)}) collective-permute-start(bf16[2,272,1024]{2,1,0:T(8,128)(2,1)S(1)} %pad_maximum_fusion.1.pair_ref.pair_edge_ref.inputs_ref), channel_id=1, source_target_pairs={{0,1},{1,0},{2,3},{3,2},{4,5},{5,4},{6,7},{7,6},{8,9},{9,8},{10,11... | collective-permute-start | bytes 3342344 | tf_op jit(solution)/shard_map/ppermute | solution.py:46
  93.6 1.4 copy-start.14
  95.0 1.2 copy-start.16
  96.3 1.7 copy-start
  96.3 1.9 copy-start.8
  96.3 2.0 copy-start.10
  96.3 2.0 copy-start.12
  96.3 10.6 %copy-start.33 = (bf16[256,1024]{1,0:T(8,128)(2,1)S(1)}, bf16[256,1024]{1,0:T(8,128)(2,1)}, u32[]{:S(2)}) copy-start(bf16[256,1024]{1,0:T(8,128)(2,1)} %param.19) | copy-start | bytes 1572868
  98.3 12.3 %copy-start.18 = (f32[4,256,256]{2,1,0:T(8,128)}, f32[4,256,256]{2,1,0:T(8,128)S(1)}, u32[]{:S(2)}) copy-start(f32[4,256,256]{2,1,0:T(8,128)S(1)} %get-tuple-element.86.convolved_ref) | copy-start | bytes 3145732
  98.3 12.3 %copy-start.21 = (bf16[4,256,256]{2,1,0:T(8,128)(2,1)}, bf16[4,256,256]{2,1,0:T(8,128)(2,1)S(1)}, u32[]{:S(2)}) copy-start(bf16[4,256,256]{2,1,0:T(8,128)(2,1)S(1)} %get-tuple-element.91.gated_ref) | copy-start | bytes 1572868
  98.3 10.9 %collective-permute-start.3 = (bf16[2,256,1024]{2,1,0:T(8,128)(2,1)S(1)}, bf16[2,256,1024]{2,1,0:T(8,128)(2,1)S(1)}, u32[]{:S(2)}, u32[]{:S(2)}) collective-permute-start(bf16[2,256,1024]{2,1,0:T(8,128)(2,1)S(1)} %get-tuple-element.68), channel_id=1, source_target_pairs={{0,1},{1,0},{2,3},{3,2},{4,5},{5,4},{6,7},{7,6},{8,9},{9,8},{10,11... | collective-permute-start | bytes 3145736 | tf_op jit(solution)/shard_map/ppermute | solution.py:46
  106.9 13.5 %collective-permute-start.4 = (bf16[256,1024]{1,0:T(8,128)(2,1)S(1)}, bf16[256,1024]{1,0:T(8,128)(2,1)S(1)}, u32[]{:S(2)}, u32[]{:S(2)}) collective-permute-start(bf16[256,1024]{1,0:T(8,128)(2,1)S(1)} %copy-done.33), channel_id=1, source_target_pairs={{0,32},{1,33},{2,34},{3,35},{4,36},{5,37},{6,38},{7,39},{8,40},{9,... | collective-permute-start | bytes 1572872 | tf_op jit(solution)/shard_map/ppermute | solution.py:50
  120.4 24.1 %collective-permute-start.5 = (bf16[2,256,1024]{2,1,0:T(8,128)(2,1)}, bf16[2,256,1024]{2,1,0:T(8,128)(2,1)}, u32[]{:S(2)}, u32[]{:S(2)}) collective-permute-start(bf16[2,256,1024]{2,1,0:T(8,128)(2,1)} %get-tuple-element.70), channel_id=1, source_target_pairs={{0,32},{1,33},{2,34},{3,35},{4,36},{5,37},{6,38},{7,39},{8,40},{9,... | collective-permute-start | bytes 3145736 | tf_op jit(solution)/shard_map/ppermute | solution.py:50
  121.6 22.9 %collective-permute-start.6 = (bf16[2,256,1024]{2,1,0:T(8,128)(2,1)}, bf16[2,256,1024]{2,1,0:T(8,128)(2,1)}, u32[]{:S(2)}, u32[]{:S(2)}) collective-permute-start(bf16[2,256,1024]{2,1,0:T(8,128)(2,1)} %pad_maximum_fusion.2.pair_ref.outer_ref), channel_id=1, source_target_pairs={{0,1},{1,0},{2,3},{3,2},{4,5},{5,4},{6,7},{7,6},{8,9},{9,8},{10,11... | collective-permute-start | bytes 3145736 | tf_op jit(solution)/shard_map/ppermute | solution.py:46
  125.6 18.9 %copy-start.13 = (f32[8,1024]{1,0:T(8,128)S(1)}, f32[8,1024]{1,0:T(8,128)}, u32[]{:S(2)}) copy-start(f32[8,1024]{1,0:T(8,128)} %copy-done.12) | copy-start | bytes 98308
  146.2 1.3 copy-start.3
  147.6 4.1 %collective-permute-start.7 = (bf16[2,256,1024]{2,1,0:T(8,128)(2,1)S(1)}, bf16[2,256,1024]{2,1,0:T(8,128)(2,1)S(1)}, u32[]{:S(2)}, u32[]{:S(2)}) collective-permute-start(bf16[2,256,1024]{2,1,0:T(8,128)(2,1)S(1)} %get-tuple-element.75.own_ref), channel_id=1, source_target_pairs={{0,1},{1,0},{2,3},{3,2},{4,5},{5,4},{6,7},{7,6},{8,9},{9,8},{10,11... | collective-permute-start | bytes 3145736 | tf_op jit(solution)/shard_map/ppermute | solution.py:46
  170.7 1.0 copy-start.20
  171.7 1.4 copy-start.25
  173.1 15.9 %copy-start.23 = (bf16[4,256,1152]{2,1,0:T(8,128)(2,1)}, bf16[4,256,1152]{2,1,0:T(8,128)(2,1)S(1)}, u32[]{:S(2)}) copy-start(bf16[4,256,1152]{2,1,0:T(8,128)(2,1)S(1)} %get-tuple-element.80.hidden_ref) | copy-start | bytes 7077892
  189.0 3.0 collective-permute-start.8
  191.9 1.7 copy-start.24
  191.9 2.4 copy-start.30
  192.4 24.6 %copy-start.4 = (f32[2,256,1024]{2,1,0:T(8,128)S(1)}, f32[2,256,1024]{2,1,0:T(8,128)}, u32[]{:S(2)}) copy-start(f32[2,256,1024]{2,1,0:T(8,128)} %copy-done.3) | copy-start | bytes 6291460
  192.4 24.6 %collective-permute-start.9 = (bf16[2,256,1024]{2,1,0:T(8,128)(2,1)S(1)}, bf16[2,256,1024]{2,1,0:T(8,128)(2,1)S(1)}, u32[]{:S(2)}, u32[]{:S(2)}) collective-permute-start(bf16[2,256,1024]{2,1,0:T(8,128)(2,1)S(1)} %get-tuple-element.112), channel_id=1, source_target_pairs={{0,32},{1,33},{2,34},{3,35},{4,36},{5,37},{6,38},{7,39},{8,40},{9,... | collective-permute-start | bytes 3145736 | tf_op jit(solution)/shard_map/ppermute | solution.py:50
  217.0 8.7 %copy-start.11 = (bf16[256,1024]{1,0:T(8,128)(2,1)S(1)}, bf16[256,1024]{1,0:T(8,128)(2,1)}, u32[]{:S(2)}) copy-start(bf16[256,1024]{1,0:T(8,128)(2,1)} %copy-done.10) | copy-start | bytes 1572868
  217.0 8.7 %copy-start.19 = (f32[4,256,256]{2,1,0:T(8,128)S(1)}, f32[4,256,256]{2,1,0:T(8,128)}, u32[]{:S(2)}) copy-start(f32[4,256,256]{2,1,0:T(8,128)} %copy-done.18) | copy-start | bytes 3145732
  220.5 1.3 copy-start.6
  221.9 3.8 %collective-permute-start.10 = (bf16[2,256,1024]{2,1,0:T(8,128)(2,1)}, bf16[2,256,1024]{2,1,0:T(8,128)(2,1)}, u32[]{:S(2)}, u32[]{:S(2)}) collective-permute-start(bf16[2,256,1024]{2,1,0:T(8,128)(2,1)} %get-tuple-element.85.own_ref), channel_id=1, source_target_pairs={{0,1},{1,0},{2,3},{3,2},{4,5},{5,4},{6,7},{7,6},{8,9},{9,8},{10,11... | collective-permute-start | bytes 3145736 | tf_op jit(solution)/shard_map/ppermute | solution.py:46
  225.6 2.2 copy-start.1
  227.8 8.7 %copy-start.9 = (bf16[4,256,256]{2,1,0:T(8,128)(2,1)S(1)}, bf16[4,256,256]{2,1,0:T(8,128)(2,1)}, u32[]{:S(2)}) copy-start(bf16[4,256,256]{2,1,0:T(8,128)(2,1)} %copy-done.8) | copy-start | bytes 1572868
  227.8 8.7 %copy-start.22 = (bf16[4,256,256]{2,1,0:T(8,128)(2,1)S(1)}, bf16[4,256,256]{2,1,0:T(8,128)(2,1)}, u32[]{:S(2)}) copy-start(bf16[4,256,256]{2,1,0:T(8,128)(2,1)} %copy-done.21) | copy-start | bytes 1572868
  231.5 9.9 %collective-permute-start.11 = (f32[2,2,256]{2,1,0:T(2,128)S(1)}, f32[2,2,256]{2,1,0:T(2,128)S(1)}, u32[]{:S(2)}, u32[]{:S(2)}) collective-permute-start(f32[2,2,256]{2,1,0:T(2,128)S(1)} %broadcast_select_fusion.2), channel_id=1, source_target_pairs={{0,30},{1,31},{2,0},{3,1},{4,2},{5,3},{6,4},{7,5},{8,6},{9,7},{10,... | collective-permute-start | bytes 12296 | tf_op jit(solution)/shard_map/ppermute | solution.py:679
  236.6 5.0 %copy-start.2 = (f32[4,256,768]{2,1,0:T(8,128)S(1)}, f32[4,256,768]{2,1,0:T(8,128)}, u32[]{:S(2)}) copy-start(f32[4,256,768]{2,1,0:T(8,128)} %copy-done) | copy-start | bytes 9437188
  236.6 5.0 %copy-start.15 = (bf16[4,256,1024]{2,1,0:T(8,128)(2,1)S(1)}, bf16[4,256,1024]{2,1,0:T(8,128)(2,1)}, u32[]{:S(2)}) copy-start(bf16[4,256,1024]{2,1,0:T(8,128)(2,1)} %copy-done.14) | copy-start | bytes 6291460
  236.6 5.0 %copy-start.17 = (bf16[1024,768]{1,0:T(8,128)(2,1)S(1)}, bf16[1024,768]{1,0:T(8,128)(2,1)}, u32[]{:S(2)}) copy-start(bf16[1024,768]{1,0:T(8,128)(2,1)} %copy-done.16) | copy-start | bytes 4718596
  241.6 9.9 %copy-start.26 = (f32[4,256,1024]{2,1,0:T(8,128)S(1)}, f32[4,256,1024]{2,1,0:T(8,128)}, u32[]{:S(2)}) copy-start(f32[4,256,1024]{2,1,0:T(8,128)} %fusion) | copy-start | bytes 12582916
  250.7 6.8 %collective-permute-start.14 = (bf16[2,256,1024]{2,1,0:T(8,128)(2,1)}, bf16[2,256,1024]{2,1,0:T(8,128)(2,1)}, u32[]{:S(2)}, u32[]{:S(2)}) collective-permute-start(bf16[2,256,1024]{2,1,0:T(8,128)(2,1)} %get-tuple-element.99), channel_id=1, source_target_pairs={{0,1},{1,0},{2,3},{3,2},{4,5},{5,4},{6,7},{7,6},{8,9},{9,8},{10,11... | collective-permute-start | bytes 3145736 | tf_op jit(solution)/shard_map/ppermute | solution.py:46
  252.8 6.9 %collective-permute-start.12 = (bf16[2,256,1024]{2,1,0:T(8,128)(2,1)}, bf16[2,256,1024]{2,1,0:T(8,128)(2,1)S(1)}, u32[]{:S(2)}, u32[]{:S(2)}) collective-permute-start(bf16[2,256,1024]{2,1,0:T(8,128)(2,1)} %slice.156), channel_id=1, source_target_pairs={{0,1},{1,0},{2,3},{3,2},{4,5},{5,4},{6,7},{7,6},{8,9},{9,8},{10,11... | collective-permute-start | bytes 3145736 | tf_op jit(solution)/shard_map/ppermute | solution.py:46
  252.8 37.7 %all-to-all-start.2 = ((bf16[16,4,16,1152]{3,2,1,0:T(8,128)(2,1)}), bf16[16,4,16,1152]{3,2,1,0:T(8,128)(2,1)}, u32[]{:S(2)}, u32[]{:S(2)}) async-start(bf16[16,4,16,1152]{3,2,1,0:T(8,128)(2,1)} %bitcast.34), calls=%async_computation.2 | async-start | bytes 4718592 | tf_op jit(solution)/shard_map/all_to_all | solution.py:91
  257.5 2.5 copy-start.27
  259.5 12.9 %copy-start.29 = (bf16[256,1024]{1,0:T(8,128)(2,1)S(1)}, bf16[256,1024]{1,0:T(8,128)(2,1)}, u32[]{:S(2)}) copy-start(bf16[256,1024]{1,0:T(8,128)(2,1)} %param.10) | copy-start | bytes 1572868
  259.5 12.8 %collective-permute-start.15 = (bf16[256,1024]{1,0:T(8,128)(2,1)S(1)}, bf16[256,1024]{1,0:T(8,128)(2,1)S(1)}, u32[]{:S(2)}, u32[]{:S(2)}) collective-permute-start(bf16[256,1024]{1,0:T(8,128)(2,1)S(1)} %fusion.15), channel_id=1, source_target_pairs={{0,32},{1,33},{2,34},{3,35},{4,36},{5,37},{6,38},{7,39},{8,40},{9,... | collective-permute-start | bytes 1572872 | tf_op jit(solution)/shard_map/ppermute | solution.py:50
  260.5 23.1 %copy-start.5 = (f32[2,256,1024]{2,1,0:T(8,128)S(1)}, f32[2,256,1024]{2,1,0:T(8,128)}, u32[]{:S(2)}) copy-start(f32[2,256,1024]{2,1,0:T(8,128)} %copy-done.3) | copy-start | bytes 6291460
  260.6 23.0 %collective-permute-start.13 = (bf16[256,1024]{1,0:T(8,128)(2,1)S(1)}, bf16[256,1024]{1,0:T(8,128)(2,1)S(1)}, u32[]{:S(2)}, u32[]{:S(2)}) collective-permute-start(bf16[256,1024]{1,0:T(8,128)(2,1)S(1)} %fusion.14), channel_id=1, source_target_pairs={{0,32},{1,33},{2,34},{3,35},{4,36},{5,37},{6,38},{7,39},{8,40},{9,... | collective-permute-start | bytes 1572872 | tf_op jit(solution)/shard_map/ppermute | solution.py:50
  272.7 11.9 %copy-start.7 = (f32[2,256,1024]{2,1,0:T(8,128)S(1)}, f32[2,256,1024]{2,1,0:T(8,128)}, u32[]{:S(2)}) copy-start(f32[2,256,1024]{2,1,0:T(8,128)} %copy-done.6) | copy-start | bytes 6291460
  299.8 20.4 %all-to-all-start.3 = ((bf16[8,16,3200]{2,1,0:T(8,128)(2,1)}), bf16[8,16,3200]{2,1,0:T(8,128)(2,1)S(1)}, u32[]{:S(2)}, u32[]{:S(2)}) async-start(bf16[8,16,3200]{2,1,0:T(8,128)(2,1)} %maximum_maximum_fusion), calls=%async_computation.4 | async-start | bytes 1638400 | tf_op jit(solution)/shard_map/all_to_all | solution.py:765
  320.2 7.5 %collective-permute-start.16 = (bf16[4,16,1536]{2,1,0:T(8,128)(2,1)S(1)}, bf16[4,16,1536]{2,1,0:T(8,128)(2,1)S(1)}, u32[]{:S(2)}, u32[]{:S(2)}) collective-permute-start(bf16[4,16,1536]{2,1,0:T(8,128)(2,1)S(1)} %pad_maximum_fusion.6), channel_id=1, source_target_pairs={{0,64},{64,0},{1,65},{65,1},{2,66},{66,2},{3,67},{67,3},{4,68},{68... | collective-permute-start | bytes 589832 | tf_op jit(solution)/shard_map/ppermute | solution.py:754
Sparse Core Ops, SparseCore 0:
  25.6 84.1 all-gather.1
  189.1 108.6 reduce-scatter.1

commit v4 on v3

--- a/solution.py
+++ b/solution.py
@@ -11,7 +11,7 @@
 PLANE = SIDE * SIDE
 HALF = PLANE * 2
 SPARE = 128
-EDGE = 16
+EDGE = 8
 CHUNK = 256
 MIB = 1024 * 1024
 
@@ -31,7 +31,7 @@
 
 TO_CORE = moves(lambda z, plane, core: (z, plane, 1 - core))
 TO_Z = moves(lambda z, plane, core: (1 - z, plane, core))
-TO_FOLLOWING = [(index, index + 1) for index in range(2 * HALF - 1)]
+TO_NEXT = moves(lambda z, plane, core: (z, (plane + 1) % PLANE, core))
 TO_PREVIOUS = moves(lambda z, plane, core: (z, (plane - 1) % PLANE, core))
 TEAMS = [
     [place(z, plane, core) for z in range(2) for core in range(2)] for plane in range(PLANE)
@@ -132,6 +132,10 @@
 
 def per_pair(length, width):
     return pl.BlockSpec((1, length, width), lambda slot: (slot // 2, 0, 0))
+
+
+def pair_of_values(length, width, which):
+    return pl.BlockSpec((1, 1, length, width), lambda slot: (slot // 2, which, 0, 0))
 
 
 def run(kernel, grid, in_specs, out_specs, out_shape, scratch, room, busy, values):
@@ -186,8 +190,8 @@
 
 
 def project_kernel(
-    pair_ref, other_ref, pair_edge_ref, other_edge_ref, first_ref,
-    normed_ref, proj_ref, mixed_ref, earlier_ref, in_ref, out_ref, gains_ref, taps_ref,
+    pair_ref, other_ref, first_ref,
+    normed_ref, proj_ref, mixed_ref, in_ref, out_ref, gains_ref, taps_ref,
     column, taps_column,
 ):
     slot = pl.program_id(0)
@@ -212,16 +216,13 @@
         gains_ref[...] = column[...].T[:8]
         taps_ref[...] = taps_column[...].T[:8]
 
-    def project(values):
-        values = values.astype(jnp.float32)
-        normed = (values * norm_scale(values) * gains_ref[0:1]).astype(jnp.bfloat16)
-        projected = jnp.dot(normed, in_ref[...], preferred_element_type=jnp.float32)
-        mixed = (projected[:, :channels] * projected[:, 2 * channels :]).astype(jnp.bfloat16)
-        return normed, projected, mixed
-
-    normed_ref[0], proj_ref[0], mixed_ref[0] = project(pick(slot, pair_ref[0], other_ref[0]))
-    edge = project(pick(slot, pair_edge_ref[0], other_edge_ref[0]))[2]
-    earlier_ref[0] = edge.astype(jnp.float32)
+    values = pick(slot, pair_ref[0, 0], other_ref[0, 0]).astype(jnp.float32)
+    normed = (values * norm_scale(values) * gains_ref[0:1]).astype(jnp.bfloat16)
+    normed_ref[0] = normed
+    projected = jnp.dot(normed, in_ref[...], preferred_element_type=jnp.float32)
+    proj_ref[0] = projected
+    mixed = projected[:, :channels] * projected[:, 2 * channels :]
+    mixed_ref[0] = mixed.astype(jnp.bfloat16)
 
 
 def branch_kernel(
@@ -244,7 +245,7 @@
 
 
 def middle_kernel(inputs_ref, branch_ref, crossed_ref, gains_ref, middle_ref, normed_ref):
-    middle = inputs_ref[0].astype(jnp.float32) + branch_ref[0]
+    middle = inputs_ref[0, 0].astype(jnp.float32) + branch_ref[0]
     middle += crossed_ref[0].astype(jnp.float32)
     middle_ref[0] = middle
     normed_ref[0] = (middle * norm_scale(middle) * gains_ref[1:2]).astype(jnp.bfloat16)
@@ -263,7 +264,7 @@
         gain_ref[...] = jnp.sum(grad_normed * middle * scale, axis=0, keepdims=True)
 
     grad_middle = norm_back(grad_normed * gains_ref[1:2], middle, scale)
-    grad_middle += outer_ref[0].astype(jnp.float32)
+    grad_middle += outer_ref[0, 0].astype(jnp.float32)
     grad_middle_ref[0] = grad_middle
     branch_ref[0] = grad_middle.astype(jnp.bfloat16)
 
@@ -275,7 +276,7 @@
     slot = pl.program_id(0)
     units = down_ref.shape[0]
     normed = pick(slot, own_ref[0], swap_ref[0])
-    outer = pick(slot, pair_ref[0], other_ref[0])
+    outer = pick(slot, pair_ref[0, 0], other_ref[0, 0])
     for start in range(0, units, CHUNK):
         lanes = slice(start, min(start + CHUNK, units))
         up_lanes = slice(units + lanes.start, units + lanes.stop)
@@ -304,7 +305,7 @@
     block = width // PLANE
     rest = each - block
     normed = pick(slot, own_ref[0], swap_ref[0])
-    outer = pick(slot, pair_ref[0], other_ref[0])
+    outer = pick(slot, pair_ref[0, 0], other_ref[0, 0])
 
     @pl.when(slot == 0)
     def _():
@@ -423,7 +424,7 @@
     total[...] += contract_rows(normed_ref[0], grad_projected)
     grad_normed = contract_cols(grad_projected, in_ref[...])
     store_pair(slot, grad_normed, keep_ref, sent_ref)
-    values = pick(slot, pair_ref[0], other_ref[0]).astype(jnp.float32)
+    values = pick(slot, pair_ref[0, 0], other_ref[0, 0]).astype(jnp.float32)
     gain_rows[0:1] += jnp.sum(grad_normed * values * norm_scale(values), axis=0, keepdims=True)
 
     @pl.when(slot == 3)
@@ -478,10 +479,6 @@
     rows = w_in.shape[0]
     channels = model_width // 4
 
-    before = lax.ppermute(tokens[length - EDGE :], "fsdp", TO_FOLLOWING)
-    extended = jnp.concatenate([tokens, before], 0)
-    extended_z = to_z(extended)
-
     block = 4 * rows
     rest = w_down.shape[0] - block
     units = w_down.shape[0] * PLANE
@@ -510,13 +507,8 @@
         ],
         2,
     )
-    first_pack, extended_z = lax.optimization_barrier((first_pack, extended_z))
-    pair = jnp.stack([extended, extended_z])
-    other = to_core(pair)
     first_all = plane_swap(jnp.broadcast_to(first_pack, (PLANE,) + first_pack.shape))
-    first_all, outer = lax.optimization_barrier((first_all, cotangent))
     first_all = first_all.reshape(PLANE, 4 * rows, -1)
-    outer_z = to_z(outer)
 
     main_rows = ff_all[:, 2 * units : 2 * units + model_width].reshape(2, PLANE, 2 * rows, -1)
     main_rows = main_rows.transpose(1, 0, 2, 3).reshape(PLANE, block, model_width)
@@ -525,28 +517,28 @@
     rest_rows = rest_rows.transpose(0, 2, 1, 3).reshape(PLANE, rest, model_width)
     down_full = jnp.concatenate([main_rows, rest_rows], 1).reshape(units, model_width)
 
-    team_pairs = [per_pair(length, model_width)] * 2
+    pair = jnp.stack([tokens, cotangent])
+    pair = jnp.stack([pair, to_z(pair)])
+    other = to_core(pair)
+    team_pairs = [pair_of_values(length, model_width, 0)] * 2
+    outer_pairs = [pair_of_values(length, model_width, 1)] * 2
     slot_wide, slot_narrow = (4, length, model_width), (4, length, channels)
     pair_wide = (2, length, model_width)
     pairs = [per_pair(length, model_width)] * 2
     narrow = per_slot(length, channels)
     out_gate = per_slot(length, channels, 1)
     edge, edge_after = per_slot(EDGE, channels), per_slot(8, channels)
-    team_edges = [
-        pl.BlockSpec((1, EDGE, model_width), lambda slot: (slot // 2, length // EDGE, 0))
-    ] * 2
     out_matrix, in_matrix = whole(channels, model_width), whole(model_width, in_width)
     taps = whole(8, channels)
 
-    normed, projected, mixed, earlier, in_full, out_full, gains, kernel = run(
+    normed, projected, mixed, in_full, out_full, gains, kernel = run(
         project_kernel,
         (4,),
-        team_pairs + team_edges + [whole(*first_all.shape)],
+        team_pairs + [whole(*first_all.shape)],
         [
             per_slot(length, model_width),
             per_slot(length, in_width),
             narrow,
-            edge,
             in_matrix,
             out_matrix,
             whole(8, model_width),
@@ -556,7 +548,6 @@
             array(slot_wide, low),
             array((4, length, in_width), wide),
             array(slot_narrow, low),
-            array((4, EDGE, channels), wide),
             array((model_width, in_width), low),
             array((channels, model_width), low),
             array((8, model_width), wide),
@@ -564,13 +555,25 @@
         ],
         [pltpu.VMEM((model_width, SPARE), wide), pltpu.VMEM((channels, SPARE), wide)],
         24,
-        0.2,
-        [pair, other, pair, other, first_all],
+        4,
+        [pair, other, first_all],
     )
 
     def by_core(first, second):
         return jnp.where(core == 0, first, second)
 
+    tails = mixed[:, length - 2 :]
+    sent = by_core(tails[1::2], tails[0::2])
+    received = lax.ppermute(sent, "fsdp", TO_NEXT)
+    nothing = jnp.zeros_like(received[0])
+    shifted = jnp.where(
+        z == 0, jnp.stack([nothing, received[0]]), jnp.stack([received[1], nothing])
+    )
+    before = jnp.where(plane == 0, shifted, received)
+    own_before = by_core(before, tails[1::2])
+    other_before = by_core(tails[0::2], before)
+    earlier = jnp.stack([own_before[0], other_before[0], own_before[1], other_before[1]])
+    earlier = jnp.pad(earlier.astype(wide), ((0, 0), (EDGE - 2, 0), (0, 0)))
     convolved, gated, branch_keep, branch_sent = run(
         branch_kernel,
         (4,),
@@ -584,24 +587,23 @@
         ],
         [],
         16,
-        0.2,
+        2,
         [mixed, earlier, projected, kernel, out_full],
     )
     branch_pair = core_sum(branch_keep, branch_sent)
-    branch_sent, outer_z = lax.optimization_barrier((branch_pair.astype(low), outer_z))
-    outer_pair = jnp.stack([outer, outer_z])
-    outer_other = to_core(outer_pair)
-    branch_other = to_z(branch_sent)
-    branch_other, down_full, outer_other = lax.optimization_barrier(
-        (branch_other, down_full, outer_other)
-    )
+    branch_other = to_z(branch_pair.astype(low))
+    branch_other, down_full = lax.optimization_barrier((branch_other, down_full))
     one = pl.BlockSpec((1, length, model_width), lambda index: (index, 0, 0))
     crossed = pl.BlockSpec((1, length, model_width), lambda index: (1 - index, 0, 0))
+    tokens_one, outer_one = (
+        pl.BlockSpec((1, 1, length, model_width), lambda index, which=which: (index, which, 0, 0))
+        for which in range(2)
+    )
     gain_rows = whole(8, model_width)
     middle, normed_two = run(
         middle_kernel,
         (2,),
-        [one, one, crossed, gain_rows],
+        [tokens_one, one, crossed, gain_rows],
         [one, one],
         [array(pair_wide, wide), array(pair_wide, low)],
         [],
@@ -617,14 +619,14 @@
         ff_kernel,
         (4,),
         pairs
-        + pairs
+        + outer_pairs
         + [whole(*ff_all.shape), whole(units, model_width)],
         [unit_slot] * 3 + pairs,
         [unit_shape] * 3 + [array(pair_wide, wide), array(pair_wide, low)],
         [],
         40,
         21,
-        [normed_two, normed_swap, outer_pair, outer_other, ff_all, down_full],
+        [normed_two, normed_swap, pair, other, ff_all, down_full],
     )
     grad_pair = core_sum(grad_keep, grad_sent)
     grad_sent = grad_pair.astype(low)
@@ -633,7 +635,7 @@
     (ff_grads,) = run(
         ff_grads_kernel,
         (4,),
-        pairs + pairs + [unit_slot] * 3,
+        pairs + outer_pairs + [unit_slot] * 3,
         [whole(*ff_all.shape)],
         [array(ff_all.shape, low)],
         [
@@ -643,7 +645,7 @@
         ],
         44,
         16,
-        [normed_two, normed_swap, outer_pair, outer_other, hidden, grad_gate, grad_upper],
+        [normed_two, normed_swap, pair, other, hidden, grad_gate, grad_upper],
     )
     ff_share = scatter_rows(ff_grads)
     down_term = jnp.dot(
@@ -653,13 +655,13 @@
     grad_middle, grad_branch, grad_gain_two = run(
         grad_middle_kernel,
         (2,),
-        [one, crossed, one, one, gain_rows],
+        [one, crossed, one, outer_one, gain_rows],
         [one, one, whole(1, model_width)],
         [array(pair_wide, wide), array(pair_wide, low), array((1, model_width), wide)],
         [],
         24,
         4,
-        [grad_pair, grad_other, middle, outer_pair, gains],
+        [grad_pair, grad_other, middle, pair, gains],
     )
     grad_swap = to_core(grad_branch)
 

time: 338 us -> 311 us (0.920)
  waiting for transfers between devices: 149 us -> 133 us
  starting transfers between devices: 53.9 us -> 39.8 us
  local copies, waits for them, and re-layouts: 31 us -> 36 us
  Pallas kernels: 66.3 us -> 61.5 us
    ppermute x6 -> x5, waiting for transfers between devices: 76.8 us -> 59.6 us  [to_z(): return lax.ppermute(value, 'fsdp', TO_Z)]
    all_to_all x2, waiting for transfers between devices: 37.7 us -> 23.2 us  [plane_swap(): lax.all_to_all(blocks, 'fsdp', 0, 0, tiled=True, axis_index_groups=PLANES)]
    all_gather x1, waiting for transfers between devices: 0.01 us -> 13.1 us  [gather_rows(): lax.all_gather(blocks.reshape(2, 2 * rows, columns), 'fsdp', axis=1, tile...]
    ppermute x8 -> x7, starting transfers between devices: 16.2 us -> 10.8 us  [to_core(): return lax.ppermute(value, 'fsdp', TO_CORE)]
    unnamed x80 -> x65, local copies, waits for them, and re-layouts: 12.4 us -> 17.5 us
    pallas_call x10, Pallas kernels: 66.3 us -> 61.5 us  [run(): pl.pallas_call(kernel, grid=grid, in_specs=in_specs, out_specs=out_specs,...]
    ppermute x1, starting transfers between devices: 5.04 us -> 0.3 us  [body(): received = lax.ppermute(sent, 'fsdp', TO_PREVIOUS)]
    ppermute x8 -> x7, waiting for transfers between devices: 9.7 us -> 9.37 us  [to_core(): return lax.ppermute(value, 'fsdp', TO_CORE)]
  transfers between devices with their start and end apart: 23 -> 21, of which waited for: 16 -> 17; matrix products, arithmetic and copies ran while one was open for 9% -> 11% of each run, Pallas kernels for 9% -> 8%
where the time goes in v4:
time: 311 us; the launch traced here: 310 us
  waiting for transfers between devices  133 us (43%)
  Pallas kernels  61.5 us (20%)
  starting transfers between devices  39.8 us (13%)
  local copies, waits for them, and re-layouts  36 us (12%)
  other arithmetic  20.8 us (7%)
  between operations  14.8 us (5%)
  matrix products  4.41 us (1%)
    pallas_call x10, Pallas kernels, run(): pl.pallas_call(kernel, grid=grid, in_specs=in_specs, out_specs=out_specs,...  61.5 us
    ppermute x5, waiting for transfers between devices, to_z(): return lax.ppermute(value, 'fsdp', TO_Z)  59.6 us
    all_to_all x2, waiting for transfers between devices, plane_swap(): lax.all_to_all(blocks, 'fsdp', 0, 0, tiled=True, axis_index_groups=PLANES)  23.2 us
    unnamed x65, local copies, waits for them, and re-layouts  17.5 us
    all_gather x1, waiting for transfers between devices, gather_rows(): lax.all_gather(blocks.reshape(2, 2 * rows, columns), 'fsdp', axis=1, tile...  13.1 us
    all_to_all x1, waiting for transfers between devices, body(): lax.all_to_all(jnp.concatenate([blocks, blocks]), ('rep', 'fsdp'), 0, 0,...  11.7 us
    all_to_all x2, starting transfers between devices, plane_swap(): lax.all_to_all(blocks, 'fsdp', 0, 0, tiled=True, axis_index_groups=PLANES)  11.3 us
    ppermute x7, starting transfers between devices, to_core(): return lax.ppermute(value, 'fsdp', TO_CORE)  10.8 us
  transfers between devices with their start and end apart: 21, of which 17 were waited for; matrix products, arithmetic and copies ran while one was open for 11% of the time, Pallas kernels for 8%

profile of v4, /device:TPU:1, one launch (start us, length us, event | category | flops | bytes accessed | tf_op | source)
XLA Modules:
  0.0 310.4 jit_solution(6260866805907217001)
XLA Ops:
  8.0 1.5 reshape.132
  12.9 4.8 %all-to-all-start = ((bf16[4,16,3200]{2,1,0:T(8,128)(2,1)}), bf16[4,16,3200]{2,1,0:T(8,128)(2,1)S(1)}, u32[]{:S(2)}, u32[]{:S(2)}) async-start(bf16[4,16,3200]{2,1,0:T(8,128)(2,1)} %pad_maximum_fusion.4), calls=%async_computation | async-start | bytes 819200 | tf_op jit(solution)/shard_map/all_to_all | solution.py:87
  17.7 6.7 %all-to-all-done = bf16[4,16,3200]{2,1,0:T(8,128)(2,1)S(1)} async-done(((bf16[4,16,3200]{2,1,0:T(8,128)(2,1)}), bf16[4,16,3200]{2,1,0:T(8,128)(2,1)S(1)}, u32[]{:S(2)}, u32[]{:S(2)}) %all-to-all-start) | async-done | bytes 409632 | tf_op jit(solution)/shard_map/all_to_all | solution.py:87
  25.4 1.5 fusion.24
  27.4 1.7 broadcast_in_dim.10
  29.1 6.8 %all-to-all-start.1 = ((bf16[16,4,16,1152]{3,2,1,0:T(8,128)(2,1)}), bf16[16,4,16,1152]{3,2,1,0:T(8,128)(2,1)S(1)}, u32[]{:S(2)}, u32[]{:S(2)}) async-start(bf16[16,4,16,1152]{3,2,1,0:T(8,128)(2,1)} %broadcast_in_dim.10), calls=%async_computation.1 | async-start | bytes 4718592 | tf_op jit(solution)/shard_map/all_to_all | solution.py:91
  36.0 15.0 %collective-permute-done = bf16[2,256,1024]{2,1,0:T(8,128)(2,1)} collective-permute-done((bf16[2,256,1024]{2,1,0:T(8,128)(2,1)}, bf16[2,256,1024]{2,1,0:T(8,128)(2,1)}, u32[]{:S(2)}, u32[]{:S(2)}) %collective-permute-start) | collective-permute-done | bytes 1048608 | tf_op jit(solution)/shard_map/ppermute | solution.py:50
  51.0 3.1 pad_maximum_fusion.1.pair_ref.inputs_ref.outer_ref
  54.0 1.8 collective-permute-start.1
  55.8 17.6 %all-to-all-done.1 = bf16[16,4,16,1152]{3,2,1,0:T(8,128)(2,1)S(1)} async-done(((bf16[16,4,16,1152]{3,2,1,0:T(8,128)(2,1)}), bf16[16,4,16,1152]{3,2,1,0:T(8,128)(2,1)S(1)}, u32[]{:S(2)}, u32[]{:S(2)}) %all-to-all-start.1) | async-done | bytes 2359328 | tf_op jit(solution)/shard_map/all_to_all | solution.py:91
  73.4 4.8 %shard_map.177 = (bf16[4,256,1024]{2,1,0:T(8,128)(2,1)S(1)}, f32[4,256,768]{2,1,0:T(8,128)S(1)}, bf16[4,256,256]{2,1,0:T(8,128)(2,1)S(1)}, bf16[1024,768]{1,0:T(...) custom-call(bf16[2,2,256,1024]{3,2,1,0:T(8,128)(2,1)} %pad_maximum_fusion.1.pair_ref.inp, ...), custom_call_target="tpu_custom_call" | custom-call | flops 4600000000 | tf_op jit(solution)/shard_map/pallas_call | solution.py:142
  78.2 1.6 copy-done.6
  79.8 1.3 copy-done.16
  81.2 1.1 copy-done.18
  82.3 1.6 collective-permute-start.2
  83.9 4.3 %collective-permute-done.2 = bf16[2,2,256]{2,1,0:T(2,128)(2,1)S(1)} collective-permute-done((bf16[2,2,256]{2,1,0:T(2,128)(2,1)S(1)}, bf16[2,2,256]{2,1,0:T(2,128)(2,1)S(1)}, u32[]{:S(2)}, u32[]{:S(2)}) %collective-permute-start.2) | collective-permute-done | bytes 2080 | tf_op jit(solution)/shard_map/ppermute | solution.py:567
  88.3 1.9 copy-done.7
  90.2 1.7 shard_map.178
  92.0 1.0 copy-done.10
  93.7 5.3 %collective-permute-start.3 = (bf16[2,256,1024]{2,1,0:T(8,128)(2,1)S(1)}, bf16[2,256,1024]{2,1,0:T(8,128)(2,1)S(1)}, u32[]{:S(2)}, u32[]{:S(2)}) collective-permute-start(bf16[2,256,1024]{2,1,0:T(8,128)(2,1)S(1)} %get-tuple-element.56), channel_id=1, source_target_pairs={{0,1},{1,0},{2,3},{3,2},{4,5},{5,4},{6,7},{7,6},{8,9},{9,8},{10,11... | collective-permute-start | bytes 3145736 | tf_op jit(solution)/shard_map/ppermute | solution.py:46
  99.1 2.3 collective-permute-done.3
  101.3 1.4 fusion.26
  103.5 13.1 %all-gather.2.cloned.1.call-done = bf16[2,512,3456]{2,1,0:T(8,128)(2,1)} async-done(((bf16[2,32,3456]{2,1,0:T(8,128)(2,1)}), bf16[2,512,3456]{2,1,0:T(8,128)(2,1)}) %all-gather.2.cloned.1.call-update) | async-done | bytes 7077904 | tf_op jit(solution)/shard_map/all_gather | solution.py:96
  117.6 1.8 slice.222
  119.7 1.6 pad_maximum_fusion
  121.3 6.1 %collective-permute-done.4.crossed_ref = bf16[2,256,1024]{2,1,0:T(8,128)(2,1)} collective-permute-done((bf16[2,256,1024]{2,1,0:T(8,128)(2,1)}, bf16[2,256,1024]{2,1,0:T(8,128)(2,1)}, u32[]{:S(2)}, u32[]{:S(2)}) %collective-permute-start.4) | collective-permute-done | bytes 1048608 | tf_op jit(solution)/shard_map/ppermute | solution.py:50
  127.4 1.9 shard_map.179
  129.3 1.4 copy-done
  130.7 1.2 collective-permute-start.5
  131.9 2.3 collective-permute-done.5.swap_ref
  134.2 19.9 %shard_map.180 = (bf16[4,256,1152]{2,1,0:T(8,128)(2,1)S(1)}, bf16[4,256,1152]{2,1,0:T(8,128)(2,1)S(1)}, bf16[4,256,1152]{2,1,0:T(8,128)(2,1)}, f32[2,256,1024]{2,1,0:T(8,128)S(1)}, bf16[2,256,1024]{2,1,0:T(8,128)(2,1)S(1)}) custom-call(bf16[2,256,1024]{2,1,0:T(8,128)(2,1)S(1)} %get-tuple-element.60.own_ref, ...), custom_call_target="tpu_custom_call" | custom-call | flops 24149999616 | tf_op jit(solution)/shard_map/pallas_call | solution.py:142
  155.0 1.4 copy-done.20
  156.4 16.2 %shard_map.181 = bf16[1024,3456]{1,0:T(8,128)(2,1)} custom-call(bf16[2,256,1024]{2,1,0:T(8,128)(2,1)S(1)} %get-tuple-element.60.own_ref, bf16[2,256,1024]{2,1,0:T(8,128)(2,1)S(1)} %collective-permute-done.5.swap_ref, bf16[2,2,256,1024]{3,2,1,0:T(8,128)(2,1)} %pad_maximum_fusion.1.pair_ref.inputs_ref.outer_ref, ...), custom_call_target="tpu_custom_call" | custom-call | flops 18400000000 | tf_op jit(solution)/shard_map/pallas_call | solution.py:142
  173.1 2.5 collective-permute-done.6
  178.0 4.4 %fusion = f32[4,256,1024]{2,1,0:T(8,128)} fusion(bf16[4,256,1152]{2,1,0:T(8,128)(2,1)S(1)} %copy-done.13, bf16[1152,1024]{1,0:T(8,128)(2,1)S(1)} %bitcast.113), kind=kOutput, calls=%fused_computation.1 | convolution fusion | flops 2415919104 | bytes 8912896 | tf_op jit(solution)/shard_map/dot_general | solution.py:651
  182.4 18.2 %collective-permute-done.7.crossed_ref = bf16[2,256,1024]{2,1,0:T(8,128)(2,1)S(1)} collective-permute-done((bf16[2,256,1024]{2,1,0:T(8,128)(2,1)S(1)}, bf16[2,256,1024]{2,1,0:T(8,128)(2,1)S(1)}, u32[]{:S(2)}, u32[]{:S(2)}) %collective-permute-start.7) | collective-permute-done | bytes 1048608 | tf_op jit(solution)/shard_map/ppermute | solution.py:50
  200.6 2.7 shard_map.182
  203.3 1.3 copy-done.3
  204.6 1.1 collective-permute-start.8
  205.7 2.3 collective-permute-done.8.swap_ref
  208.0 1.9 copy-done.8
  209.9 1.3 copy-done.11
  211.2 1.5 shard_map.183
  213.1 2.0 shard_map.184
  216.1 9.1 %shard_map.185 = (bf16[16,64,1152]{2,1,0:T(8,128)(2,1)}, f32[2,256,1024]{2,1,0:T(8,128)S(1)}, bf16[2,256,1024]{2,1,0:T(8,128)(2,1)S(1)}) custom-call(f32[4,256,256]{2,1,0:T(8,128)S(1)} %get-tuple-element.71.grad_conv_ref, f32[4,8,256]{2,1,0:T(8,128)S(1)} %select_maximum_fusion.later_ref, f32[4,256,768]{2,1,0:T(8,128)S(1)} %copy-done.9, ...), custom_call_target="tpu_custom_call" | custom-call | flops 9200000000 | tf_op jit(solution)/shard_map/pallas_call | solution.py:142
  225.3 1.0 collective-permute-start.12
  226.6 1.0 slice.190
  227.7 4.5 %all-to-all-start.2 = ((bf16[16,4,16,1152]{3,2,1,0:T(8,128)(2,1)}), bf16[16,4,16,1152]{3,2,1,0:T(8,128)(2,1)}, u32[]{:S(2)}, u32[]{:S(2)}) async-start(bf16[16,4,16,1152]{3,2,1,0:T(8,128)(2,1)} %bitcast.34), calls=%async_computation.2 | async-start | bytes 4718592 | tf_op jit(solution)/shard_map/all_to_all | solution.py:91
  232.2 1.7 convert_add_fusion
  234.8 1.7 convert_add_fusion.1
  237.3 9.4 %collective-permute-done.13 = bf16[256,1024]{1,0:T(8,128)(2,1)S(1)} collective-permute-done((bf16[256,1024]{1,0:T(8,128)(2,1)S(1)}, bf16[256,1024]{1,0:T(8,128)(2,1)S(1)}, u32[]{:S(2)}, u32[]{:S(2)}) %collective-permute-start.13) | collective-permute-done | bytes 524320 | tf_op jit(solution)/shard_map/ppermute | solution.py:50
  247.2 10.8 %collective-permute-done.11 = bf16[256,1024]{1,0:T(8,128)(2,1)S(1)} collective-permute-done((bf16[256,1024]{1,0:T(8,128)(2,1)S(1)}, bf16[256,1024]{1,0:T(8,128)(2,1)S(1)}, u32[]{:S(2)}, u32[]{:S(2)}) %collective-permute-start.11) | collective-permute-done | bytes 524320 | tf_op jit(solution)/shard_map/ppermute | solution.py:50
  258.0 1.1 fusion.13
  259.1 1.3 fusion.7
  260.4 5.6 %all-to-all-done.2 = bf16[16,4,16,1152]{3,2,1,0:T(8,128)(2,1)} async-done(((bf16[16,4,16,1152]{3,2,1,0:T(8,128)(2,1)}), bf16[16,4,16,1152]{3,2,1,0:T(8,128)(2,1)}, u32[]{:S(2)}, u32[]{:S(2)}) %all-to-all-start.2) | async-done | bytes 2359328 | tf_op jit(solution)/shard_map/all_to_all | solution.py:91
  266.0 2.0 reduce_sum.32
  268.1 4.3 %reduce-scatter.2.cloned.1.call-done = bf16[2,32,3456]{2,1,0:T(8,128)(2,1)} async-done(((bf16[2,512,3456]{2,1,0:T(8,128)(2,1)}), bf16[2,32,3456]{2,1,0:T(8,128)(2,1)}) %reduce-scatter.2.cloned.1.call-update) | async-done | bytes 442384 | tf_op jit(solution)/shard_map/reduce_scatter | solution.py:107
  272.4 1.0 slice.236
  273.4 1.0 maximum_maximum_fusion
  274.3 6.9 %all-to-all-start.3 = ((bf16[8,16,3200]{2,1,0:T(8,128)(2,1)}), bf16[8,16,3200]{2,1,0:T(8,128)(2,1)S(1)}, u32[]{:S(2)}, u32[]{:S(2)}) async-start(bf16[8,16,3200]{2,1,0:T(8,128)(2,1)} %maximum_maximum_fusion), calls=%async_computation.4 | async-start | bytes 1638400 | tf_op jit(solution)/shard_map/all_to_all | solution.py:767
  282.2 11.7 %all-to-all-done.3.blocks_ref = bf16[8,16,3200]{2,1,0:T(8,128)(2,1)S(1)} async-done(((bf16[8,16,3200]{2,1,0:T(8,128)(2,1)}), bf16[8,16,3200]{2,1,0:T(8,128)(2,1)S(1)}, u32[]{:S(2)}, u32[]{:S(2)}) %all-to-all-start.3) | async-done | bytes 819232 | tf_op jit(solution)/shard_map/all_to_all | solution.py:767
  294.4 1.7 shard_map.186
  297.0 1.4 reshape.149
  299.3 1.4 reshape.151
  (141 shorter events, 22.1 us)
Async XLA Ops:
  7.2 3.1 %copy-start.27 = (bf16[16,4608]{1,0:T(8,128)(2,1)S(1)}, bf16[16,4608]{1,0:T(8,128)(2,1)}, u32[]{:S(2)}) copy-start(bf16[16,4608]{1,0:T(8,128)(2,1)} %param.17) | copy-start | bytes 442372
  9.5 1.7 copy-start.28
  10.9 13.6 %slice-start = ((bf16[72,1024]{1,0:T(8,128)(2,1)}), bf16[8,1024]{1,0:T(8,128)(2,1)S(1)}, s32[]{:S(2)}) async-start(bf16[72,1024]{1,0:T(8,128)(2,1)} %param.18), calls=%async_computation.7 | async-start | bytes 32768 | tf_op jit(solution)/shard_map/slice | solution.py:493
  10.9 13.6 %slice-start.1 = ((bf16[72,1024]{1,0:T(8,128)(2,1)}), bf16[64,1024]{1,0:T(8,128)(2,1)S(1)}, s32[]{:S(2)}) async-start(bf16[72,1024]{1,0:T(8,128)(2,1)} %param.18), calls=%async_computation.8 | async-start | bytes 262144 | tf_op jit(solution)/shard_map/slice | solution.py:492
  11.8 13.6 %copy-start.23 = (bf16[256,1024]{1,0:T(8,128)(2,1)S(1)}, bf16[256,1024]{1,0:T(8,128)(2,1)}, u32[]{:S(2)}) copy-start(bf16[256,1024]{1,0:T(8,128)(2,1)} %param.10) | copy-start | bytes 1572868
  11.8 13.6 %copy-start.26 = (bf16[256,1024]{1,0:T(8,128)(2,1)S(1)}, bf16[256,1024]{1,0:T(8,128)(2,1)}, u32[]{:S(2)}) copy-start(bf16[256,1024]{1,0:T(8,128)(2,1)} %param.19) | copy-start | bytes 1572868
  12.9 11.6 %all-to-all-start = ((bf16[4,16,3200]{2,1,0:T(8,128)(2,1)}), bf16[4,16,3200]{2,1,0:T(8,128)(2,1)S(1)}, u32[]{:S(2)}, u32[]{:S(2)}) async-start(bf16[4,16,3200]{2,1,0:T(8,128)(2,1)} %pad_maximum_fusion.4), calls=%async_computation | async-start | bytes 819200 | tf_op jit(solution)/shard_map/all_to_all | solution.py:87
  17.7 98.9 %all-gather.2.cloned.1.call-start = ((), (), s32[]{:S(2)}) async-start(), calls=%async_computation.5 | async-start | bytes 7520256 | tf_op jit(solution)/shard_map/all_gather | solution.py:96
  24.5 2.7 copy-start.30
  24.5 2.8 copy-start.29
  26.8 24.1 %collective-permute-start = (bf16[2,256,1024]{2,1,0:T(8,128)(2,1)}, bf16[2,256,1024]{2,1,0:T(8,128)(2,1)}, u32[]{:S(2)}, u32[]{:S(2)}) collective-permute-start(bf16[2,256,1024]{2,1,0:T(8,128)(2,1)} %get-tuple-element.103), channel_id=1, source_target_pairs={{0,32},{1,33},{2,34},{3,35},{4,36},{5,37},{6,38},{7,39},{8,40},{9,... | collective-permute-start | bytes 3145736 | tf_op jit(solution)/shard_map/ppermute | solution.py:50
  29.1 44.3 %all-to-all-start.1 = ((bf16[16,4,16,1152]{3,2,1,0:T(8,128)(2,1)}), bf16[16,4,16,1152]{3,2,1,0:T(8,128)(2,1)S(1)}, u32[]{:S(2)}, u32[]{:S(2)}) async-start(bf16[16,4,16,1152]{3,2,1,0:T(8,128)(2,1)} %broadcast_in_dim.10), calls=%async_computation.1 | async-start | bytes 4718592 | tf_op jit(solution)/shard_map/all_to_all | solution.py:91
  35.9 236.5 %reduce-scatter.2.cloned.1.call-start = ((), (), s32[]{:S(2)}) async-start(), calls=%async_computation.6 | async-start | bytes 7520256 | tf_op jit(solution)/shard_map/reduce_scatter | solution.py:107
  54.0 19.4 %collective-permute-start.1 = (bf16[2,2,256,1024]{3,2,1,0:T(8,128)(2,1)}, bf16[2,2,256,1024]{3,2,1,0:T(8,128)(2,1)}, u32[]{:S(2)}, u32[]{:S(2)}) collective-permute-start(bf16[2,2,256,1024]{3,2,1,0:T(8,128)(2,1)} %pad_maximum_fusion.1.pair_ref.inputs_ref.outer_ref), channel_id=1, source_target_pairs={{0,1},{1,0},{2,3},{3,2},{4,5},{5,4},{6,7},{7,6},{8,9},{9,8},{10,11... | collective-permute-start | bytes 6291464 | tf_op jit(solution)/shard_map/ppermute | solution.py:46
  78.2 1.6 copy-start.6
  79.8 1.3 copy-start.16
  81.1 1.2 copy-start.18
  82.3 5.9 %collective-permute-start.2 = (bf16[2,2,256]{2,1,0:T(2,128)(2,1)S(1)}, bf16[2,2,256]{2,1,0:T(2,128)(2,1)S(1)}, u32[]{:S(2)}, u32[]{:S(2)}) collective-permute-start(bf16[2,2,256]{2,1,0:T(2,128)(2,1)S(1)} %broadcast_select_fusion.7), channel_id=1, source_target_pairs={{0,2},{1,3},{2,4},{3,5},{4,6},{5,7},{6,8},{7,9},{8,10},{9,11},{10,... | collective-permute-start | bytes 6152 | tf_op jit(solution)/shard_map/ppermute | solution.py:567
  88.3 1.9 copy-start.7
  91.9 1.0 copy-start.10
  92.9 0.8 copy-start.14
  93.7 7.6 %collective-permute-start.3 = (bf16[2,256,1024]{2,1,0:T(8,128)(2,1)S(1)}, bf16[2,256,1024]{2,1,0:T(8,128)(2,1)S(1)}, u32[]{:S(2)}, u32[]{:S(2)}) collective-permute-start(bf16[2,256,1024]{2,1,0:T(8,128)(2,1)S(1)} %get-tuple-element.56), channel_id=1, source_target_pairs={{0,1},{1,0},{2,3},{3,2},{4,5},{5,4},{6,7},{7,6},{8,9},{9,8},{10,11... | collective-permute-start | bytes 3145736 | tf_op jit(solution)/shard_map/ppermute | solution.py:46
  102.7 24.7 %collective-permute-start.4 = (bf16[2,256,1024]{2,1,0:T(8,128)(2,1)}, bf16[2,256,1024]{2,1,0:T(8,128)(2,1)}, u32[]{:S(2)}, u32[]{:S(2)}) collective-permute-start(bf16[2,256,1024]{2,1,0:T(8,128)(2,1)} %get-tuple-element.98), channel_id=1, source_target_pairs={{0,32},{1,33},{2,34},{3,35},{4,36},{5,37},{6,38},{7,39},{8,40},{9,... | collective-permute-start | bytes 3145736 | tf_op jit(solution)/shard_map/ppermute | solution.py:50
  129.3 1.4 copy-start
  130.7 3.5 %collective-permute-start.5 = (bf16[2,256,1024]{2,1,0:T(8,128)(2,1)S(1)}, bf16[2,256,1024]{2,1,0:T(8,128)(2,1)S(1)}, u32[]{:S(2)}, u32[]{:S(2)}) collective-permute-start(bf16[2,256,1024]{2,1,0:T(8,128)(2,1)S(1)} %get-tuple-element.60.own_ref), channel_id=1, source_target_pairs={{0,1},{1,0},{2,3},{3,2},{4,5},{5,4},{6,7},{7,6},{8,9},{9,8},{10,11... | collective-permute-start | bytes 3145736 | tf_op jit(solution)/shard_map/ppermute | solution.py:46
  154.0 1.0 copy-start.5
  155.0 1.4 copy-start.20
  156.4 16.2 %copy-start.12 = (bf16[4,256,1152]{2,1,0:T(8,128)(2,1)}, bf16[4,256,1152]{2,1,0:T(8,128)(2,1)S(1)}, u32[]{:S(2)}) copy-start(bf16[4,256,1152]{2,1,0:T(8,128)(2,1)S(1)} %get-tuple-element.64.hidden_ref) | copy-start | bytes 7077892
  172.6 3.0 collective-permute-start.6
  175.6 1.7 copy-start.13
  175.6 2.4 copy-start.25
  176.0 24.6 %copy-start.1 = (f32[2,256,1024]{2,1,0:T(8,128)S(1)}, f32[2,256,1024]{2,1,0:T(8,128)}, u32[]{:S(2)}) copy-start(f32[2,256,1024]{2,1,0:T(8,128)} %copy-done) | copy-start | bytes 6291460
  176.0 24.6 %collective-permute-start.7 = (bf16[2,256,1024]{2,1,0:T(8,128)(2,1)S(1)}, bf16[2,256,1024]{2,1,0:T(8,128)(2,1)S(1)}, u32[]{:S(2)}, u32[]{:S(2)}) collective-permute-start(bf16[2,256,1024]{2,1,0:T(8,128)(2,1)S(1)} %get-tuple-element.96), channel_id=1, source_target_pairs={{0,32},{1,33},{2,34},{3,35},{4,36},{5,37},{6,38},{7,39},{8,40},{9,... | collective-permute-start | bytes 3145736 | tf_op jit(solution)/shard_map/ppermute | solution.py:50
  203.3 1.3 copy-start.3
  204.6 3.4 %collective-permute-start.8 = (bf16[2,256,1024]{2,1,0:T(8,128)(2,1)S(1)}, bf16[2,256,1024]{2,1,0:T(8,128)(2,1)S(1)}, u32[]{:S(2)}, u32[]{:S(2)}) collective-permute-start(bf16[2,256,1024]{2,1,0:T(8,128)(2,1)S(1)} %get-tuple-element.69.own_ref), channel_id=1, source_target_pairs={{0,1},{1,0},{2,3},{3,2},{4,5},{5,4},{6,7},{7,6},{8,9},{9,8},{10,11... | collective-permute-start | bytes 3145736 | tf_op jit(solution)/shard_map/ppermute | solution.py:46
  208.0 1.9 copy-start.8
  209.9 1.3 copy-start.11
  211.2 1.9 copy-start.15
  212.7 3.1 %collective-permute-start.9 = (f32[2,2,256]{2,1,0:T(2,128)S(1)}, f32[2,2,256]{2,1,0:T(2,128)S(1)}, u32[]{:S(2)}, u32[]{:S(2)}) collective-permute-start(f32[2,2,256]{2,1,0:T(2,128)S(1)} %broadcast_select_fusion.4), channel_id=1, source_target_pairs={{0,30},{1,31},{2,0},{3,1},{4,2},{5,3},{6,4},{7,5},{8,6},{9,7},{10,... | collective-permute-start | bytes 12296 | tf_op jit(solution)/shard_map/ppermute | solution.py:681
  213.0 2.9 copy-start.9
  213.0 2.9 copy-start.17
  213.0 3.1 copy-start.19
  216.1 10.1 %copy-start.21 = (f32[4,256,1024]{2,1,0:T(8,128)S(1)}, f32[4,256,1024]{2,1,0:T(8,128)}, u32[]{:S(2)}) copy-start(f32[4,256,1024]{2,1,0:T(8,128)} %fusion) | copy-start | bytes 12582916
  225.3 6.9 %collective-permute-start.12 = (bf16[2,256,1024]{2,1,0:T(8,128)(2,1)S(1)}, bf16[2,256,1024]{2,1,0:T(8,128)(2,1)}, u32[]{:S(2)}, u32[]{:S(2)}) collective-permute-start(bf16[2,256,1024]{2,1,0:T(8,128)(2,1)S(1)} %get-tuple-element.83), channel_id=1, source_target_pairs={{0,1},{1,0},{2,3},{3,2},{4,5},{5,4},{6,7},{7,6},{8,9},{9,8},{10,11... | collective-permute-start | bytes 3145736 | tf_op jit(solution)/shard_map/ppermute | solution.py:46
  227.7 7.1 %collective-permute-start.10 = (bf16[2,256,1024]{2,1,0:T(8,128)(2,1)}, bf16[2,256,1024]{2,1,0:T(8,128)(2,1)}, u32[]{:S(2)}, u32[]{:S(2)}) collective-permute-start(bf16[2,256,1024]{2,1,0:T(8,128)(2,1)} %slice.190), channel_id=1, source_target_pairs={{0,1},{1,0},{2,3},{3,2},{4,5},{5,4},{6,7},{7,6},{8,9},{9,8},{10,11... | collective-permute-start | bytes 3145736 | tf_op jit(solution)/shard_map/ppermute | solution.py:46
  227.7 38.4 %all-to-all-start.2 = ((bf16[16,4,16,1152]{3,2,1,0:T(8,128)(2,1)}), bf16[16,4,16,1152]{3,2,1,0:T(8,128)(2,1)}, u32[]{:S(2)}, u32[]{:S(2)}) async-start(bf16[16,4,16,1152]{3,2,1,0:T(8,128)(2,1)} %bitcast.34), calls=%async_computation.2 | async-start | bytes 4718592 | tf_op jit(solution)/shard_map/all_to_all | solution.py:91
  232.2 2.6 copy-start.22
  233.9 12.9 %copy-start.24 = (bf16[256,1024]{1,0:T(8,128)(2,1)S(1)}, bf16[256,1024]{1,0:T(8,128)(2,1)}, u32[]{:S(2)}) copy-start(bf16[256,1024]{1,0:T(8,128)(2,1)} %param.10) | copy-start | bytes 1572868
  233.9 12.9 %collective-permute-start.13 = (bf16[256,1024]{1,0:T(8,128)(2,1)S(1)}, bf16[256,1024]{1,0:T(8,128)(2,1)S(1)}, u32[]{:S(2)}, u32[]{:S(2)}) collective-permute-start(bf16[256,1024]{1,0:T(8,128)(2,1)S(1)} %fusion.15), channel_id=1, source_target_pairs={{0,32},{1,33},{2,34},{3,35},{4,36},{5,37},{6,38},{7,39},{8,40},{9,... | collective-permute-start | bytes 1572872 | tf_op jit(solution)/shard_map/ppermute | solution.py:50
  236.5 21.6 %copy-start.2 = (f32[2,256,1024]{2,1,0:T(8,128)S(1)}, f32[2,256,1024]{2,1,0:T(8,128)}, u32[]{:S(2)}) copy-start(f32[2,256,1024]{2,1,0:T(8,128)} %copy-done) | copy-start | bytes 6291460
  236.5 21.5 %collective-permute-start.11 = (bf16[256,1024]{1,0:T(8,128)(2,1)S(1)}, bf16[256,1024]{1,0:T(8,128)(2,1)S(1)}, u32[]{:S(2)}, u32[]{:S(2)}) collective-permute-start(bf16[256,1024]{1,0:T(8,128)(2,1)S(1)} %fusion.14), channel_id=1, source_target_pairs={{0,32},{1,33},{2,34},{3,35},{4,36},{5,37},{6,38},{7,39},{8,40},{9,... | collective-permute-start | bytes 1572872 | tf_op jit(solution)/shard_map/ppermute | solution.py:50
  247.2 11.9 %copy-start.4 = (f32[2,256,1024]{2,1,0:T(8,128)S(1)}, f32[2,256,1024]{2,1,0:T(8,128)}, u32[]{:S(2)}) copy-start(f32[2,256,1024]{2,1,0:T(8,128)} %copy-done.3) | copy-start | bytes 6291460
  274.3 19.5 %all-to-all-start.3 = ((bf16[8,16,3200]{2,1,0:T(8,128)(2,1)}), bf16[8,16,3200]{2,1,0:T(8,128)(2,1)S(1)}, u32[]{:S(2)}, u32[]{:S(2)}) async-start(bf16[8,16,3200]{2,1,0:T(8,128)(2,1)} %maximum_maximum_fusion), calls=%async_computation.4 | async-start | bytes 1638400 | tf_op jit(solution)/shard_map/all_to_all | solution.py:767
  293.9 7.5 %collective-permute-start.14 = (bf16[4,16,1536]{2,1,0:T(8,128)(2,1)S(1)}, bf16[4,16,1536]{2,1,0:T(8,128)(2,1)S(1)}, u32[]{:S(2)}, u32[]{:S(2)}) collective-permute-start(bf16[4,16,1536]{2,1,0:T(8,128)(2,1)S(1)} %pad_maximum_fusion.6), channel_id=1, source_target_pairs={{0,64},{64,0},{1,65},{65,1},{2,66},{66,2},{3,67},{67,3},{4,68},{68... | collective-permute-start | bytes 589832 | tf_op jit(solution)/shard_map/ppermute | solution.py:756
Sparse Core Ops, SparseCore 0:
  25.5 91.1 all-gather.1
  172.8 99.5 reduce-scatter.1

commit v5 on v4

--- a/solution.py
+++ b/solution.py
@@ -123,7 +123,7 @@
 
 
 def whole(*shape):
-    return pl.BlockSpec(shape, lambda *_: (0,) * len(shape))
+    return pl.BlockSpec(shape, lambda *_: (0,) * len(shape), pipeline_mode=pl.Buffered(1))
 
 
 def per_slot(length, width, column=0):
@@ -273,25 +273,29 @@
     own_ref, swap_ref, pair_ref, other_ref, weights_ref, down_ref,
     hidden_ref, grad_gate_ref, grad_up_ref, keep_ref, sent_ref,
 ):
-    slot = pl.program_id(0)
-    units = down_ref.shape[0]
-    normed = pick(slot, own_ref[0], swap_ref[0])
-    outer = pick(slot, pair_ref[0, 0], other_ref[0, 0])
+    units, width = down_ref.shape
+    length = own_ref.shape[1]
+    normed = jnp.concatenate([own_ref[0], swap_ref[0]], 0)
+    outer = jnp.concatenate([pair_ref[0, 0], other_ref[0, 0]], 0)
     for start in range(0, units, CHUNK):
         lanes = slice(start, min(start + CHUNK, units))
         up_lanes = slice(units + lanes.start, units + lanes.stop)
+        shape = (2, length, lanes.stop - lanes.start)
         gate = jnp.dot(normed, weights_ref[:, lanes], preferred_element_type=jnp.float32)
         up = jnp.dot(normed, weights_ref[:, up_lanes], preferred_element_type=jnp.float32)
         grad = contract_cols(outer, down_ref[lanes, :])
         sigmoid = jax.nn.sigmoid(gate)
         silu = gate * sigmoid
-        hidden_ref[0, :, lanes] = (silu * up).astype(jnp.bfloat16)
+        hidden_ref[:, :, lanes] = (silu * up).astype(jnp.bfloat16).reshape(shape)
         grad_gate = grad * up * sigmoid * (1.0 + gate * (1.0 - sigmoid))
-        grad_gate_ref[0, :, lanes] = grad_gate.astype(jnp.bfloat16)
-        grad_up_ref[0, :, lanes] = (grad * silu).astype(jnp.bfloat16)
-    term = contract_cols(grad_gate_ref[0], weights_ref[:, :units])
-    term += contract_cols(grad_up_ref[0], weights_ref[:, units : 2 * units])
-    store_pair(slot, term, keep_ref, sent_ref)
+        grad_gate_ref[:, :, lanes] = grad_gate.astype(jnp.bfloat16).reshape(shape)
+        grad_up_ref[:, :, lanes] = (grad * silu).astype(jnp.bfloat16).reshape(shape)
+    grad_gate = grad_gate_ref[...].reshape(2 * length, units)
+    grad_up = grad_up_ref[...].reshape(2 * length, units)
+    term = contract_cols(grad_gate, weights_ref[:, :units])
+    term += contract_cols(grad_up, weights_ref[:, units : 2 * units])
+    keep_ref[0] = term[:length]
+    sent_ref[0] = term[length:].astype(jnp.bfloat16)
 
 
 def ff_grads_kernel(
@@ -299,28 +303,35 @@
     pack_ref,
     gate_total, up_total, down_total,
 ):
-    slot = pl.program_id(0)
+    step = pl.program_id(0)
     width, units = gate_total.shape
     each = units // PLANE
     block = width // PLANE
     rest = each - block
-    normed = pick(slot, own_ref[0], swap_ref[0])
-    outer = pick(slot, pair_ref[0, 0], other_ref[0, 0])
-
-    @pl.when(slot == 0)
-    def _():
-        gate_total[...] = jnp.zeros_like(gate_total)
-        up_total[...] = jnp.zeros_like(up_total)
-        down_total[...] = jnp.zeros_like(down_total)
-
-    gate_total[...] += contract_rows(normed, grad_gate_ref[0])
-    up_total[...] += contract_rows(normed, grad_up_ref[0])
-    down_total[...] += contract_rows(hidden_ref[0], outer)
-
-    @pl.when(slot == 3)
-    def _():
-        pack_ref[:, :units] = gate_total[...].astype(jnp.bfloat16)
-        pack_ref[:, units : 2 * units] = up_total[...].astype(jnp.bfloat16)
+    tokens = 2 * own_ref.shape[1]
+    normed = jnp.concatenate([own_ref[0], swap_ref[0]], 0)
+    outer = jnp.concatenate([pair_ref[0, 0], other_ref[0, 0]], 0)
+
+    def gate_term():
+        return contract_rows(normed, grad_gate_ref[...].reshape(tokens, units))
+
+    def up_term():
+        return contract_rows(normed, grad_up_ref[...].reshape(tokens, units))
+
+    def down_term():
+        return contract_rows(hidden_ref[...].reshape(tokens, units), outer)
+
+    @pl.when(step == 0)
+    def _():
+        gate_total[...] = gate_term()
+        up_total[...] = up_term()
+        down_total[...] = down_term()
+
+    @pl.when(step == 1)
+    def _():
+        pack_ref[:, :units] = (gate_total[...] + gate_term()).astype(jnp.bfloat16)
+        pack_ref[:, units : 2 * units] = (up_total[...] + up_term()).astype(jnp.bfloat16)
+        down_total[...] += down_term()
         for plane in range(PLANE):
             start = plane * each
             for half in range(2):
@@ -521,7 +532,6 @@
     pair = jnp.stack([pair, to_z(pair)])
     other = to_core(pair)
     team_pairs = [pair_of_values(length, model_width, 0)] * 2
-    outer_pairs = [pair_of_values(length, model_width, 1)] * 2
     slot_wide, slot_narrow = (4, length, model_width), (4, length, channels)
     pair_wide = (2, length, model_width)
     pairs = [per_pair(length, model_width)] * 2
@@ -613,19 +623,19 @@
     )
     normed_swap = to_core(normed_two)
 
-    unit_slot = per_slot(length, units)
+    step_pairs = [pl.BlockSpec((1, length, model_width), lambda step: (step, 0, 0))] * 2
+    step_outer = [pl.BlockSpec((1, 1, length, model_width), lambda step: (step, 1, 0, 0))] * 2
+    unit_slot = pl.BlockSpec((2, length, units), lambda step: (step, 0, 0))
     unit_shape = array((4, length, units), low)
     hidden, grad_gate, grad_upper, grad_keep, grad_sent = run(
         ff_kernel,
-        (4,),
-        pairs
-        + outer_pairs
-        + [whole(*ff_all.shape), whole(units, model_width)],
-        [unit_slot] * 3 + pairs,
+        (2,),
+        step_pairs + step_outer + [whole(model_width, 2 * units), whole(units, model_width)],
+        [unit_slot] * 3 + step_pairs,
         [unit_shape] * 3 + [array(pair_wide, wide), array(pair_wide, low)],
         [],
-        40,
-        21,
+        44,
+        17,
         [normed_two, normed_swap, pair, other, ff_all, down_full],
     )
     grad_pair = core_sum(grad_keep, grad_sent)
@@ -634,8 +644,8 @@
 
     (ff_grads,) = run(
         ff_grads_kernel,
-        (4,),
-        pairs + outer_pairs + [unit_slot] * 3,
+        (2,),
+        step_pairs + step_outer + [unit_slot] * 3,
         [whole(*ff_all.shape)],
         [array(ff_all.shape, low)],
         [
@@ -643,8 +653,8 @@
             pltpu.VMEM((model_width, units), wide),
             pltpu.VMEM((units, model_width), wide),
         ],
-        44,
-        16,
+        54,
+        12,
         [normed_two, normed_swap, pair, other, hidden, grad_gate, grad_upper],
     )
     ff_share = scatter_rows(ff_grads)

time: 311 us -> 307 us (0.987)
  no operation moved by 1% of the time
where the time goes in v5:
time: 307 us
  waiting for transfers between devices  133 us (43%)
  Pallas kernels  59.2 us (19%)
  starting transfers between devices  39.6 us (13%)
  local copies, waits for them, and re-layouts  34.7 us (11%)
  other arithmetic  20.8 us (7%)
  between operations  14.8 us (5%)
  matrix products  4.41 us (1%)
    ppermute x5, waiting for transfers between devices, to_z(): return lax.ppermute(value, 'fsdp', TO_Z)  59.6 us
    pallas_call x10, Pallas kernels, run(): pl.pallas_call(kernel, grid=grid, in_specs=in_specs, out_specs=out_specs,...  59.2 us
    all_to_all x2, waiting for transfers between devices, plane_swap(): lax.all_to_all(blocks, 'fsdp', 0, 0, tiled=True, axis_index_groups=PLANES)  23.2 us
    unnamed x65, local copies, waits for them, and re-layouts  16.2 us
    all_gather x1, waiting for transfers between devices, gather_rows(): lax.all_gather(blocks.reshape(2, 2 * rows, columns), 'fsdp', axis=1, tile...  13.1 us
    all_to_all x1, waiting for transfers between devices, body(): lax.all_to_all(jnp.concatenate([blocks, blocks]), ('rep', 'fsdp'), 0, 0,...  11.7 us
    all_to_all x2, starting transfers between devices, plane_swap(): lax.all_to_all(blocks, 'fsdp', 0, 0, tiled=True, axis_index_groups=PLANES)  11.3 us
    ppermute x7, starting transfers between devices, to_core(): return lax.ppermute(value, 'fsdp', TO_CORE)  11 us
  transfers between devices with their start and end apart: 21, of which 17 were waited for; matrix products, arithmetic and copies ran while one was open for 11% of the time, Pallas kernels for 8%

profile of v5, /device:TPU:1, one launch (start us, length us, event | category | flops | bytes accessed | tf_op | source)
XLA Modules:
  0.0 306.6 jit_solution(5419676661666788669)
XLA Ops:
  8.0 1.5 reshape.132
  12.9 4.8 %all-to-all-start = ((bf16[4,16,3200]{2,1,0:T(8,128)(2,1)}), bf16[4,16,3200]{2,1,0:T(8,128)(2,1)S(1)}, u32[]{:S(2)}, u32[]{:S(2)}) async-start(bf16[4,16,3200]{2,1,0:T(8,128)(2,1)} %pad_maximum_fusion.4), calls=%async_computation | async-start | bytes 819200 | tf_op jit(solution)/shard_map/all_to_all | solution.py:87
  17.7 6.7 %all-to-all-done = bf16[4,16,3200]{2,1,0:T(8,128)(2,1)S(1)} async-done(((bf16[4,16,3200]{2,1,0:T(8,128)(2,1)}), bf16[4,16,3200]{2,1,0:T(8,128)(2,1)S(1)}, u32[]{:S(2)}, u32[]{:S(2)}) %all-to-all-start) | async-done | bytes 409632 | tf_op jit(solution)/shard_map/all_to_all | solution.py:87
  25.4 1.5 fusion.24
  27.4 1.6 broadcast_in_dim.10
  29.1 6.8 %all-to-all-start.1 = ((bf16[16,4,16,1152]{3,2,1,0:T(8,128)(2,1)}), bf16[16,4,16,1152]{3,2,1,0:T(8,128)(2,1)S(1)}, u32[]{:S(2)}, u32[]{:S(2)}) async-start(bf16[16,4,16,1152]{3,2,1,0:T(8,128)(2,1)} %broadcast_in_dim.10), calls=%async_computation.1 | async-start | bytes 4718592 | tf_op jit(solution)/shard_map/all_to_all | solution.py:91
  35.9 15.0 %collective-permute-done = bf16[2,256,1024]{2,1,0:T(8,128)(2,1)} collective-permute-done((bf16[2,256,1024]{2,1,0:T(8,128)(2,1)}, bf16[2,256,1024]{2,1,0:T(8,128)(2,1)}, u32[]{:S(2)}, u32[]{:S(2)}) %collective-permute-start) | collective-permute-done | bytes 1048608 | tf_op jit(solution)/shard_map/ppermute | solution.py:50
  51.0 3.1 pad_maximum_fusion.1.pair_ref.inputs_ref.outer_ref
  54.0 1.8 collective-permute-start.1
  55.8 17.6 %all-to-all-done.1 = bf16[16,4,16,1152]{3,2,1,0:T(8,128)(2,1)S(1)} async-done(((bf16[16,4,16,1152]{3,2,1,0:T(8,128)(2,1)}), bf16[16,4,16,1152]{3,2,1,0:T(8,128)(2,1)S(1)}, u32[]{:S(2)}, u32[]{:S(2)}) %all-to-all-start.1) | async-done | bytes 2359328 | tf_op jit(solution)/shard_map/all_to_all | solution.py:91
  73.4 4.8 %shard_map.177 = (bf16[4,256,1024]{2,1,0:T(8,128)(2,1)S(1)}, f32[4,256,768]{2,1,0:T(8,128)S(1)}, bf16[4,256,256]{2,1,0:T(8,128)(2,1)S(1)}, bf16[1024,768]{1,0:T(...) custom-call(bf16[2,2,256,1024]{3,2,1,0:T(8,128)(2,1)} %pad_maximum_fusion.1.pair_ref.inp, ...), custom_call_target="tpu_custom_call" | custom-call | flops 4600000000 | tf_op jit(solution)/shard_map/pallas_call | solution.py:142
  78.2 1.6 copy-done.8
  79.8 1.3 copy-done.16
  81.1 1.2 copy-done.18
  82.3 1.6 collective-permute-start.2
  83.9 4.3 %collective-permute-done.2 = bf16[2,2,256]{2,1,0:T(2,128)(2,1)S(1)} collective-permute-done((bf16[2,2,256]{2,1,0:T(2,128)(2,1)S(1)}, bf16[2,2,256]{2,1,0:T(2,128)(2,1)S(1)}, u32[]{:S(2)}, u32[]{:S(2)}) %collective-permute-start.2) | collective-permute-done | bytes 2080 | tf_op jit(solution)/shard_map/ppermute | solution.py:577
  88.3 1.9 copy-done.9
  90.2 1.7 shard_map.178
  91.9 1.0 copy-done.12
  93.7 5.3 %collective-permute-start.3 = (bf16[2,256,1024]{2,1,0:T(8,128)(2,1)S(1)}, bf16[2,256,1024]{2,1,0:T(8,128)(2,1)S(1)}, u32[]{:S(2)}, u32[]{:S(2)}) collective-permute-start(bf16[2,256,1024]{2,1,0:T(8,128)(2,1)S(1)} %get-tuple-element.56), channel_id=1, source_target_pairs={{0,1},{1,0},{2,3},{3,2},{4,5},{5,4},{6,7},{7,6},{8,9},{9,8},{10,11... | collective-permute-start | bytes 3145736 | tf_op jit(solution)/shard_map/ppermute | solution.py:46
  99.1 2.3 collective-permute-done.3
  101.3 1.4 fusion.26
  103.5 13.1 %all-gather.2.cloned.1.call-done = bf16[2,512,3456]{2,1,0:T(8,128)(2,1)} async-done(((bf16[2,32,3456]{2,1,0:T(8,128)(2,1)}), bf16[2,512,3456]{2,1,0:T(8,128)(2,1)}) %all-gather.2.cloned.1.call-update) | async-done | bytes 7077904 | tf_op jit(solution)/shard_map/all_gather | solution.py:96
  116.6 1.0 slice.223
  117.6 1.8 slice.222
  119.7 1.6 pad_maximum_fusion
  121.3 6.1 %collective-permute-done.4.crossed_ref = bf16[2,256,1024]{2,1,0:T(8,128)(2,1)} collective-permute-done((bf16[2,256,1024]{2,1,0:T(8,128)(2,1)}, bf16[2,256,1024]{2,1,0:T(8,128)(2,1)}, u32[]{:S(2)}, u32[]{:S(2)}) %collective-permute-start.4) | collective-permute-done | bytes 1048608 | tf_op jit(solution)/shard_map/ppermute | solution.py:50
  127.4 1.9 shard_map.179
  129.3 1.4 copy-done
  130.7 1.2 collective-permute-start.5
  131.9 2.3 collective-permute-done.5.swap_ref
  134.2 19.6 %shard_map.180 = (bf16[4,256,1152]{2,1,0:T(8,128)(2,1)}, bf16[4,256,1152]{2,1,0:T(8,128)(2,1)}, bf16[4,256,1152]{2,1,0:T(8,128)(2,1)}, f32[2,256,1024]{2,1,0:T(8,128)S(1)}, bf16[2,256,1024]{2,1,0:T(8,128)(2,1)S(1)}) custom-call(bf16[2,256,1024]{2,1,0:T(8,128)(2,1)S(1)} %get-tuple-element.60.own_ref, ...), custom_call_target="tpu_custom_call" | custom-call | flops 19549999104 | tf_op jit(solution)/shard_map/pallas_call | solution.py:142
  153.8 1.0 copy-done.5
  154.7 14.2 %shard_map.181 = bf16[1024,3456]{1,0:T(8,128)(2,1)} custom-call(bf16[2,256,1024]{2,1,0:T(8,128)(2,1)} %copy-done.6, bf16[2,256,1024]{2,1,0:T(8,128)(2,1)} %copy-done.7, bf16[2,2,256,1024]{3,2,1,0:T(8,128)(2,1)} %pad_maximum_fusion.1.pair_ref.inputs_ref.outer_ref, bf16[2,2,256,1024]{3,2,1,0:T(8,128)(2,1)} %collective-permute-done.1.other_ref, ...), custom_call_target="tpu_custom_call" | custom-call | flops 13799999488 | tf_op jit(solution)/shard_map/pallas_call | solution.py:142
  169.6 2.5 collective-permute-done.6
  174.5 4.4 %fusion = f32[4,256,1024]{2,1,0:T(8,128)} fusion(bf16[4,256,1152]{2,1,0:T(8,128)(2,1)S(1)} %copy-done.30, bf16[1152,1024]{1,0:T(8,128)(2,1)S(1)} %bitcast.113), kind=kOutput, calls=%fused_computation.1 | convolution fusion | flops 2415919104 | bytes 8912896 | tf_op jit(solution)/shard_map/dot_general | solution.py:661
  178.9 18.2 %collective-permute-done.7.crossed_ref = bf16[2,256,1024]{2,1,0:T(8,128)(2,1)S(1)} collective-permute-done((bf16[2,256,1024]{2,1,0:T(8,128)(2,1)S(1)}, bf16[2,256,1024]{2,1,0:T(8,128)(2,1)S(1)}, u32[]{:S(2)}, u32[]{:S(2)}) %collective-permute-start.7) | collective-permute-done | bytes 1048608 | tf_op jit(solution)/shard_map/ppermute | solution.py:50
  197.1 2.7 shard_map.182
  199.9 1.3 copy-done.3
  201.2 1.1 collective-permute-start.8
  202.2 2.3 collective-permute-done.8.swap_ref
  204.5 1.9 copy-done.10
  206.4 1.2 copy-done.13
  207.7 1.5 shard_map.183
  209.4 2.0 shard_map.184
  212.5 9.1 %shard_map.185 = (bf16[16,64,1152]{2,1,0:T(8,128)(2,1)}, f32[2,256,1024]{2,1,0:T(8,128)S(1)}, bf16[2,256,1024]{2,1,0:T(8,128)(2,1)S(1)}) custom-call(f32[4,256,256]{2,1,0:T(8,128)S(1)} %get-tuple-element.71.grad_conv_ref, f32[4,8,256]{2,1,0:T(8,128)S(1)} %select_maximum_fusion.later_ref, f32[4,256,768]{2,1,0:T(8,128)S(1)} %copy-done.11, ...), custom_call_target="tpu_custom_call" | custom-call | flops 9200000000 | tf_op jit(solution)/shard_map/pallas_call | solution.py:142
  222.9 1.0 slice.190
  224.0 4.5 %all-to-all-start.2 = ((bf16[16,4,16,1152]{3,2,1,0:T(8,128)(2,1)}), bf16[16,4,16,1152]{3,2,1,0:T(8,128)(2,1)}, u32[]{:S(2)}, u32[]{:S(2)}) async-start(bf16[16,4,16,1152]{3,2,1,0:T(8,128)(2,1)} %bitcast.34), calls=%async_computation.2 | async-start | bytes 4718592 | tf_op jit(solution)/shard_map/all_to_all | solution.py:91
  228.4 1.7 convert_add_fusion
  231.2 1.7 convert_add_fusion.1
  233.7 9.4 %collective-permute-done.13 = bf16[256,1024]{1,0:T(8,128)(2,1)S(1)} collective-permute-done((bf16[256,1024]{1,0:T(8,128)(2,1)S(1)}, bf16[256,1024]{1,0:T(8,128)(2,1)S(1)}, u32[]{:S(2)}, u32[]{:S(2)}) %collective-permute-start.13) | collective-permute-done | bytes 524320 | tf_op jit(solution)/shard_map/ppermute | solution.py:50
  243.5 10.8 %collective-permute-done.11 = bf16[256,1024]{1,0:T(8,128)(2,1)S(1)} collective-permute-done((bf16[256,1024]{1,0:T(8,128)(2,1)S(1)}, bf16[256,1024]{1,0:T(8,128)(2,1)S(1)}, u32[]{:S(2)}, u32[]{:S(2)}) %collective-permute-start.11) | collective-permute-done | bytes 524320 | tf_op jit(solution)/shard_map/ppermute | solution.py:50
  254.3 1.1 fusion.13
  255.4 1.3 fusion.7
  256.7 5.6 %all-to-all-done.2 = bf16[16,4,16,1152]{3,2,1,0:T(8,128)(2,1)} async-done(((bf16[16,4,16,1152]{3,2,1,0:T(8,128)(2,1)}), bf16[16,4,16,1152]{3,2,1,0:T(8,128)(2,1)}, u32[]{:S(2)}, u32[]{:S(2)}) %all-to-all-start.2) | async-done | bytes 2359328 | tf_op jit(solution)/shard_map/all_to_all | solution.py:91
  262.3 2.0 reduce_sum.32
  264.3 4.3 %reduce-scatter.2.cloned.1.call-done = bf16[2,32,3456]{2,1,0:T(8,128)(2,1)} async-done(((bf16[2,512,3456]{2,1,0:T(8,128)(2,1)}), bf16[2,32,3456]{2,1,0:T(8,128)(2,1)}) %reduce-scatter.2.cloned.1.call-update) | async-done | bytes 442384 | tf_op jit(solution)/shard_map/reduce_scatter | solution.py:107
  268.6 1.0 slice.236
  269.6 1.0 maximum_maximum_fusion
  270.6 6.8 %all-to-all-start.3 = ((bf16[8,16,3200]{2,1,0:T(8,128)(2,1)}), bf16[8,16,3200]{2,1,0:T(8,128)(2,1)S(1)}, u32[]{:S(2)}, u32[]{:S(2)}) async-start(bf16[8,16,3200]{2,1,0:T(8,128)(2,1)} %maximum_maximum_fusion), calls=%async_computation.4 | async-start | bytes 1638400 | tf_op jit(solution)/shard_map/all_to_all | solution.py:777
  278.3 11.7 %all-to-all-done.3.blocks_ref = bf16[8,16,3200]{2,1,0:T(8,128)(2,1)S(1)} async-done(((bf16[8,16,3200]{2,1,0:T(8,128)(2,1)}), bf16[8,16,3200]{2,1,0:T(8,128)(2,1)S(1)}, u32[]{:S(2)}, u32[]{:S(2)}) %all-to-all-start.3) | async-done | bytes 819232 | tf_op jit(solution)/shard_map/all_to_all | solution.py:777
  290.6 1.7 shard_map.186
  293.1 1.4 reshape.149
  295.4 1.4 reshape.151
  (141 shorter events, 21.2 us)
Async XLA Ops:
  7.2 3.1 %copy-start.26 = (bf16[16,4608]{1,0:T(8,128)(2,1)S(1)}, bf16[16,4608]{1,0:T(8,128)(2,1)}, u32[]{:S(2)}) copy-start(bf16[16,4608]{1,0:T(8,128)(2,1)} %param.17) | copy-start | bytes 442372
  9.5 1.7 copy-start.27
  10.9 13.6 %slice-start = ((bf16[72,1024]{1,0:T(8,128)(2,1)}), bf16[8,1024]{1,0:T(8,128)(2,1)S(1)}, s32[]{:S(2)}) async-start(bf16[72,1024]{1,0:T(8,128)(2,1)} %param.18), calls=%async_computation.7 | async-start | bytes 32768 | tf_op jit(solution)/shard_map/slice | solution.py:504
  10.9 13.6 %slice-start.1 = ((bf16[72,1024]{1,0:T(8,128)(2,1)}), bf16[64,1024]{1,0:T(8,128)(2,1)S(1)}, s32[]{:S(2)}) async-start(bf16[72,1024]{1,0:T(8,128)(2,1)} %param.18), calls=%async_computation.8 | async-start | bytes 262144 | tf_op jit(solution)/shard_map/slice | solution.py:503
  11.8 13.6 %copy-start.22 = (bf16[256,1024]{1,0:T(8,128)(2,1)S(1)}, bf16[256,1024]{1,0:T(8,128)(2,1)}, u32[]{:S(2)}) copy-start(bf16[256,1024]{1,0:T(8,128)(2,1)} %param.10) | copy-start | bytes 1572868
  11.8 13.6 %copy-start.25 = (bf16[256,1024]{1,0:T(8,128)(2,1)S(1)}, bf16[256,1024]{1,0:T(8,128)(2,1)}, u32[]{:S(2)}) copy-start(bf16[256,1024]{1,0:T(8,128)(2,1)} %param.19) | copy-start | bytes 1572868
  12.9 11.6 %all-to-all-start = ((bf16[4,16,3200]{2,1,0:T(8,128)(2,1)}), bf16[4,16,3200]{2,1,0:T(8,128)(2,1)S(1)}, u32[]{:S(2)}, u32[]{:S(2)}) async-start(bf16[4,16,3200]{2,1,0:T(8,128)(2,1)} %pad_maximum_fusion.4), calls=%async_computation | async-start | bytes 819200 | tf_op jit(solution)/shard_map/all_to_all | solution.py:87
  17.7 98.9 %all-gather.2.cloned.1.call-start = ((), (), s32[]{:S(2)}) async-start(), calls=%async_computation.5 | async-start | bytes 7520256 | tf_op jit(solution)/shard_map/all_gather | solution.py:96
  24.5 2.7 copy-start.29
  24.5 2.8 copy-start.28
  26.8 24.1 %collective-permute-start = (bf16[2,256,1024]{2,1,0:T(8,128)(2,1)}, bf16[2,256,1024]{2,1,0:T(8,128)(2,1)}, u32[]{:S(2)}, u32[]{:S(2)}) collective-permute-start(bf16[2,256,1024]{2,1,0:T(8,128)(2,1)} %get-tuple-element.103), channel_id=1, source_target_pairs={{0,32},{1,33},{2,34},{3,35},{4,36},{5,37},{6,38},{7,39},{8,40},{9,... | collective-permute-start | bytes 3145736 | tf_op jit(solution)/shard_map/ppermute | solution.py:50
  29.1 44.3 %all-to-all-start.1 = ((bf16[16,4,16,1152]{3,2,1,0:T(8,128)(2,1)}), bf16[16,4,16,1152]{3,2,1,0:T(8,128)(2,1)S(1)}, u32[]{:S(2)}, u32[]{:S(2)}) async-start(bf16[16,4,16,1152]{3,2,1,0:T(8,128)(2,1)} %broadcast_in_dim.10), calls=%async_computation.1 | async-start | bytes 4718592 | tf_op jit(solution)/shard_map/all_to_all | solution.py:91
  35.9 232.7 %reduce-scatter.2.cloned.1.call-start = ((), (), s32[]{:S(2)}) async-start(), calls=%async_computation.6 | async-start | bytes 7520256 | tf_op jit(solution)/shard_map/reduce_scatter | solution.py:107
  54.0 19.4 %collective-permute-start.1 = (bf16[2,2,256,1024]{3,2,1,0:T(8,128)(2,1)}, bf16[2,2,256,1024]{3,2,1,0:T(8,128)(2,1)}, u32[]{:S(2)}, u32[]{:S(2)}) collective-permute-start(bf16[2,2,256,1024]{3,2,1,0:T(8,128)(2,1)} %pad_maximum_fusion.1.pair_ref.inputs_ref.outer_ref), channel_id=1, source_target_pairs={{0,1},{1,0},{2,3},{3,2},{4,5},{5,4},{6,7},{7,6},{8,9},{9,8},{10,11... | collective-permute-start | bytes 6291464 | tf_op jit(solution)/shard_map/ppermute | solution.py:46
  78.2 1.6 copy-start.8
  79.8 1.3 copy-start.16
  81.1 1.2 copy-start.18
  82.3 5.9 %collective-permute-start.2 = (bf16[2,2,256]{2,1,0:T(2,128)(2,1)S(1)}, bf16[2,2,256]{2,1,0:T(2,128)(2,1)S(1)}, u32[]{:S(2)}, u32[]{:S(2)}) collective-permute-start(bf16[2,2,256]{2,1,0:T(2,128)(2,1)S(1)} %broadcast_select_fusion.7), channel_id=1, source_target_pairs={{0,2},{1,3},{2,4},{3,5},{4,6},{5,7},{6,8},{7,9},{8,10},{9,11},{10,... | collective-permute-start | bytes 6152 | tf_op jit(solution)/shard_map/ppermute | solution.py:577
  88.3 1.9 copy-start.9
  91.9 1.0 copy-start.12
  92.9 0.8 copy-start.14
  93.7 7.6 %collective-permute-start.3 = (bf16[2,256,1024]{2,1,0:T(8,128)(2,1)S(1)}, bf16[2,256,1024]{2,1,0:T(8,128)(2,1)S(1)}, u32[]{:S(2)}, u32[]{:S(2)}) collective-permute-start(bf16[2,256,1024]{2,1,0:T(8,128)(2,1)S(1)} %get-tuple-element.56), channel_id=1, source_target_pairs={{0,1},{1,0},{2,3},{3,2},{4,5},{5,4},{6,7},{7,6},{8,9},{9,8},{10,11... | collective-permute-start | bytes 3145736 | tf_op jit(solution)/shard_map/ppermute | solution.py:46
  102.8 24.7 %collective-permute-start.4 = (bf16[2,256,1024]{2,1,0:T(8,128)(2,1)}, bf16[2,256,1024]{2,1,0:T(8,128)(2,1)}, u32[]{:S(2)}, u32[]{:S(2)}) collective-permute-start(bf16[2,256,1024]{2,1,0:T(8,128)(2,1)} %get-tuple-element.98), channel_id=1, source_target_pairs={{0,32},{1,33},{2,34},{3,35},{4,36},{5,37},{6,38},{7,39},{8,40},{9,... | collective-permute-start | bytes 3145736 | tf_op jit(solution)/shard_map/ppermute | solution.py:50
  129.3 1.4 copy-start
  130.7 23.1 %copy-start.6 = (bf16[2,256,1024]{2,1,0:T(8,128)(2,1)}, bf16[2,256,1024]{2,1,0:T(8,128)(2,1)S(1)}, u32[]{:S(2)}) copy-start(bf16[2,256,1024]{2,1,0:T(8,128)(2,1)S(1)} %get-tuple-element.60.own_ref) | copy-start | bytes 3145732
  130.7 3.5 %collective-permute-start.5 = (bf16[2,256,1024]{2,1,0:T(8,128)(2,1)S(1)}, bf16[2,256,1024]{2,1,0:T(8,128)(2,1)S(1)}, u32[]{:S(2)}, u32[]{:S(2)}) collective-permute-start(bf16[2,256,1024]{2,1,0:T(8,128)(2,1)S(1)} %get-tuple-element.60.own_ref), channel_id=1, source_target_pairs={{0,1},{1,0},{2,3},{3,2},{4,5},{5,4},{6,7},{7,6},{8,9},{9,8},{10,11... | collective-permute-start | bytes 3145736 | tf_op jit(solution)/shard_map/ppermute | solution.py:46
  134.2 19.6 %copy-start.7 = (bf16[2,256,1024]{2,1,0:T(8,128)(2,1)}, bf16[2,256,1024]{2,1,0:T(8,128)(2,1)S(1)}, u32[]{:S(2)}) copy-start(bf16[2,256,1024]{2,1,0:T(8,128)(2,1)S(1)} %collective-permute-done.5.swap_ref) | copy-start | bytes 3145732
  153.8 1.0 copy-start.5
  168.9 3.2 %collective-permute-start.6 = (bf16[2,256,1024]{2,1,0:T(8,128)(2,1)}, bf16[2,256,1024]{2,1,0:T(8,128)(2,1)S(1)}, u32[]{:S(2)}, u32[]{:S(2)}) collective-permute-start(bf16[2,256,1024]{2,1,0:T(8,128)(2,1)} %copy-done.5), channel_id=1, source_target_pairs={{0,1},{1,0},{2,3},{3,2},{4,5},{5,4},{6,7},{7,6},{8,9},{9,8},{10,11... | collective-permute-start | bytes 3145736 | tf_op jit(solution)/shard_map/ppermute | solution.py:46
  172.1 1.7 copy-start.24
  172.1 2.4 copy-start.30
  172.6 24.6 %copy-start.1 = (f32[2,256,1024]{2,1,0:T(8,128)S(1)}, f32[2,256,1024]{2,1,0:T(8,128)}, u32[]{:S(2)}) copy-start(f32[2,256,1024]{2,1,0:T(8,128)} %copy-done) | copy-start | bytes 6291460
  172.6 24.6 %collective-permute-start.7 = (bf16[2,256,1024]{2,1,0:T(8,128)(2,1)S(1)}, bf16[2,256,1024]{2,1,0:T(8,128)(2,1)S(1)}, u32[]{:S(2)}, u32[]{:S(2)}) collective-permute-start(bf16[2,256,1024]{2,1,0:T(8,128)(2,1)S(1)} %get-tuple-element.96), channel_id=1, source_target_pairs={{0,32},{1,33},{2,34},{3,35},{4,36},{5,37},{6,38},{7,39},{8,40},{9,... | collective-permute-start | bytes 3145736 | tf_op jit(solution)/shard_map/ppermute | solution.py:50
  199.8 1.3 copy-start.3
  201.2 3.4 %collective-permute-start.8 = (bf16[2,256,1024]{2,1,0:T(8,128)(2,1)S(1)}, bf16[2,256,1024]{2,1,0:T(8,128)(2,1)S(1)}, u32[]{:S(2)}, u32[]{:S(2)}) collective-permute-start(bf16[2,256,1024]{2,1,0:T(8,128)(2,1)S(1)} %get-tuple-element.69.own_ref), channel_id=1, source_target_pairs={{0,1},{1,0},{2,3},{3,2},{4,5},{5,4},{6,7},{7,6},{8,9},{9,8},{10,11... | collective-permute-start | bytes 3145736 | tf_op jit(solution)/shard_map/ppermute | solution.py:46
  204.5 1.9 copy-start.10
  206.4 1.2 copy-start.13
  207.7 1.6 copy-start.15
  209.2 2.9 collective-permute-start.9
  209.3 2.9 copy-start.11
  209.3 2.9 copy-start.17
  209.4 3.2 %copy-start.19 = (bf16[1024,768]{1,0:T(8,128)(2,1)S(1)}, bf16[1024,768]{1,0:T(8,128)(2,1)}, u32[]{:S(2)}) copy-start(bf16[1024,768]{1,0:T(8,128)(2,1)} %copy-done.18) | copy-start | bytes 4718596
  212.5 10.0 %copy-start.20 = (f32[4,256,1024]{2,1,0:T(8,128)S(1)}, f32[4,256,1024]{2,1,0:T(8,128)}, u32[]{:S(2)}) copy-start(f32[4,256,1024]{2,1,0:T(8,128)} %fusion) | copy-start | bytes 12582916
  221.7 6.8 %collective-permute-start.12 = (bf16[2,256,1024]{2,1,0:T(8,128)(2,1)S(1)}, bf16[2,256,1024]{2,1,0:T(8,128)(2,1)}, u32[]{:S(2)}, u32[]{:S(2)}) collective-permute-start(bf16[2,256,1024]{2,1,0:T(8,128)(2,1)S(1)} %get-tuple-element.83), channel_id=1, source_target_pairs={{0,1},{1,0},{2,3},{3,2},{4,5},{5,4},{6,7},{7,6},{8,9},{9,8},{10,11... | collective-permute-start | bytes 3145736 | tf_op jit(solution)/shard_map/ppermute | solution.py:46
  223.9 7.2 %collective-permute-start.10 = (bf16[2,256,1024]{2,1,0:T(8,128)(2,1)}, bf16[2,256,1024]{2,1,0:T(8,128)(2,1)}, u32[]{:S(2)}, u32[]{:S(2)}) collective-permute-start(bf16[2,256,1024]{2,1,0:T(8,128)(2,1)} %slice.190), channel_id=1, source_target_pairs={{0,1},{1,0},{2,3},{3,2},{4,5},{5,4},{6,7},{7,6},{8,9},{9,8},{10,11... | collective-permute-start | bytes 3145736 | tf_op jit(solution)/shard_map/ppermute | solution.py:46
  224.0 38.3 %all-to-all-start.2 = ((bf16[16,4,16,1152]{3,2,1,0:T(8,128)(2,1)}), bf16[16,4,16,1152]{3,2,1,0:T(8,128)(2,1)}, u32[]{:S(2)}, u32[]{:S(2)}) async-start(bf16[16,4,16,1152]{3,2,1,0:T(8,128)(2,1)} %bitcast.34), calls=%async_computation.2 | async-start | bytes 4718592 | tf_op jit(solution)/shard_map/all_to_all | solution.py:91
  228.4 2.7 copy-start.21
  230.2 12.9 %copy-start.23 = (bf16[256,1024]{1,0:T(8,128)(2,1)S(1)}, bf16[256,1024]{1,0:T(8,128)(2,1)}, u32[]{:S(2)}) copy-start(bf16[256,1024]{1,0:T(8,128)(2,1)} %param.10) | copy-start | bytes 1572868
  230.2 12.9 %collective-permute-start.13 = (bf16[256,1024]{1,0:T(8,128)(2,1)S(1)}, bf16[256,1024]{1,0:T(8,128)(2,1)S(1)}, u32[]{:S(2)}, u32[]{:S(2)}) collective-permute-start(bf16[256,1024]{1,0:T(8,128)(2,1)S(1)} %fusion.15), channel_id=1, source_target_pairs={{0,32},{1,33},{2,34},{3,35},{4,36},{5,37},{6,38},{7,39},{8,40},{9,... | collective-permute-start | bytes 1572872 | tf_op jit(solution)/shard_map/ppermute | solution.py:50
  232.9 21.4 %copy-start.2 = (f32[2,256,1024]{2,1,0:T(8,128)S(1)}, f32[2,256,1024]{2,1,0:T(8,128)}, u32[]{:S(2)}) copy-start(f32[2,256,1024]{2,1,0:T(8,128)} %copy-done) | copy-start | bytes 6291460
  232.9 21.4 %collective-permute-start.11 = (bf16[256,1024]{1,0:T(8,128)(2,1)S(1)}, bf16[256,1024]{1,0:T(8,128)(2,1)S(1)}, u32[]{:S(2)}, u32[]{:S(2)}) collective-permute-start(bf16[256,1024]{1,0:T(8,128)(2,1)S(1)} %fusion.14), channel_id=1, source_target_pairs={{0,32},{1,33},{2,34},{3,35},{4,36},{5,37},{6,38},{7,39},{8,40},{9,... | collective-permute-start | bytes 1572872 | tf_op jit(solution)/shard_map/ppermute | solution.py:50
  243.5 11.9 %copy-start.4 = (f32[2,256,1024]{2,1,0:T(8,128)S(1)}, f32[2,256,1024]{2,1,0:T(8,128)}, u32[]{:S(2)}) copy-start(f32[2,256,1024]{2,1,0:T(8,128)} %copy-done.3) | copy-start | bytes 6291460
  270.6 19.4 %all-to-all-start.3 = ((bf16[8,16,3200]{2,1,0:T(8,128)(2,1)}), bf16[8,16,3200]{2,1,0:T(8,128)(2,1)S(1)}, u32[]{:S(2)}, u32[]{:S(2)}) async-start(bf16[8,16,3200]{2,1,0:T(8,128)(2,1)} %maximum_maximum_fusion), calls=%async_computation.4 | async-start | bytes 1638400 | tf_op jit(solution)/shard_map/all_to_all | solution.py:777
  290.0 7.5 %collective-permute-start.14 = (bf16[4,16,1536]{2,1,0:T(8,128)(2,1)S(1)}, bf16[4,16,1536]{2,1,0:T(8,128)(2,1)S(1)}, u32[]{:S(2)}, u32[]{:S(2)}) collective-permute-start(bf16[4,16,1536]{2,1,0:T(8,128)(2,1)S(1)} %pad_maximum_fusion.6), channel_id=1, source_target_pairs={{0,64},{64,0},{1,65},{65,1},{2,66},{66,2},{3,67},{67,3},{4,68},{68... | collective-permute-start | bytes 589832 | tf_op jit(solution)/shard_map/ppermute | solution.py:766
Sparse Core Ops, SparseCore 0:
  25.5 91.1 all-gather.1
  169.1 99.5 reduce-scatter.1

commit v6 on v5

--- a/solution.py
+++ b/solution.py
@@ -564,7 +564,7 @@
             array((8, channels), wide),
         ],
         [pltpu.VMEM((model_width, SPARE), wide), pltpu.VMEM((channels, SPARE), wide)],
-        24,
+        20,
         4,
         [pair, other, first_all],
     )
@@ -596,7 +596,7 @@
             array(pair_wide, low),
         ],
         [],
-        16,
+        12,
         2,
         [mixed, earlier, projected, kernel, out_full],
     )
@@ -617,7 +617,7 @@
         [one, one],
         [array(pair_wide, wide), array(pair_wide, low)],
         [],
-        20,
+        16,
         3,
         [pair, branch_pair, branch_other, gains],
     )
@@ -634,7 +634,7 @@
         [unit_slot] * 3 + step_pairs,
         [unit_shape] * 3 + [array(pair_wide, wide), array(pair_wide, low)],
         [],
-        44,
+        36,
         17,
         [normed_two, normed_swap, pair, other, ff_all, down_full],
     )
@@ -653,7 +653,7 @@
             pltpu.VMEM((model_width, units), wide),
             pltpu.VMEM((units, model_width), wide),
         ],
-        54,
+        48,
         12,
         [normed_two, normed_swap, pair, other, hidden, grad_gate, grad_upper],
     )
@@ -669,7 +669,7 @@
         [one, one, whole(1, model_width)],
         [array(pair_wide, wide), array(pair_wide, low), array((1, model_width), wide)],
         [],
-        24,
+        18,
         4,
         [grad_pair, grad_other, middle, pair, gains],
     )
@@ -682,7 +682,7 @@
         [narrow, narrow],
         [array(slot_narrow, low), array(slot_narrow, wide)],
         [],
-        16,
+        12,
         2,
         [grad_branch, grad_swap, out_full, convolved, projected],
     )
@@ -710,7 +710,7 @@
             pltpu.VMEM((SPARE, channels), wide),
             pltpu.VMEM((SPARE, model_width), wide),
         ],
-        20,
+        14,
         2.5,
         [grad_branch, grad_swap, gated, grad_conv, mixed, earlier, grad_gain_two],
     )
@@ -731,7 +731,7 @@
         [whole(*first_all.shape)] + pairs,
         [array(first_all.shape, low), array(pair_wide, wide), array(pair_wide, low)],
         [pltpu.VMEM((model_width, in_width), wide), pltpu.VMEM((SPARE, model_width), wide)],
-        32,
+        26,
         8,
         [
             grad_conv,

time: 307 us -> 310 us (level)
  local copies, waits for them, and re-layouts: 34.7 us -> 39 us
    unnamed x65 -> x67, local copies, waits for them, and re-layouts: 16.2 us -> 20.5 us
where the time goes in v6:
time: 310 us; the launch traced here: 309 us
  waiting for transfers between devices  133 us (43%)
  Pallas kernels  57.1 us (18%)
  starting transfers between devices  39.8 us (13%)
  local copies, waits for them, and re-layouts  39 us (13%)
  other arithmetic  20.8 us (7%)
  between operations  14.8 us (5%)
  matrix products  4.43 us (1%)
    ppermute x5, waiting for transfers between devices, to_z(): return lax.ppermute(value, 'fsdp', TO_Z)  59.6 us
    pallas_call x10, Pallas kernels, run(): pl.pallas_call(kernel, grid=grid, in_specs=in_specs, out_specs=out_specs,...  57.1 us
    all_to_all x2, waiting for transfers between devices, plane_swap(): lax.all_to_all(blocks, 'fsdp', 0, 0, tiled=True, axis_index_groups=PLANES)  23.6 us
    unnamed x67, local copies, waits for them, and re-layouts  20.5 us
    all_gather x1, waiting for transfers between devices, gather_rows(): lax.all_gather(blocks.reshape(2, 2 * rows, columns), 'fsdp', axis=1, tile...  13.1 us
    all_to_all x1, waiting for transfers between devices, body(): lax.all_to_all(jnp.concatenate([blocks, blocks]), ('rep', 'fsdp'), 0, 0,...  11.7 us
    all_to_all x2, starting transfers between devices, plane_swap(): lax.all_to_all(blocks, 'fsdp', 0, 0, tiled=True, axis_index_groups=PLANES)  11.3 us
    ppermute x7, starting transfers between devices, to_core(): return lax.ppermute(value, 'fsdp', TO_CORE)  10.9 us
  transfers between devices with their start and end apart: 21, of which 17 were waited for; matrix products, arithmetic and copies ran while one was open for 11% of the time, Pallas kernels for 8%

profile of v6, /device:TPU:1, one launch (start us, length us, event | category | flops | bytes accessed | tf_op | source)
XLA Modules:
  0.0 309.0 jit_solution(3130247458873937215)
XLA Ops:
  8.0 1.5 reshape.132
  12.9 4.8 %all-to-all-start = ((bf16[4,16,3200]{2,1,0:T(8,128)(2,1)}), bf16[4,16,3200]{2,1,0:T(8,128)(2,1)S(1)}, u32[]{:S(2)}, u32[]{:S(2)}) async-start(bf16[4,16,3200]{2,1,0:T(8,128)(2,1)} %pad_maximum_fusion.4), calls=%async_computation | async-start | bytes 819200 | tf_op jit(solution)/shard_map/all_to_all | solution.py:87
  17.7 6.7 %all-to-all-done = bf16[4,16,3200]{2,1,0:T(8,128)(2,1)S(1)} async-done(((bf16[4,16,3200]{2,1,0:T(8,128)(2,1)}), bf16[4,16,3200]{2,1,0:T(8,128)(2,1)S(1)}, u32[]{:S(2)}, u32[]{:S(2)}) %all-to-all-start) | async-done | bytes 409632 | tf_op jit(solution)/shard_map/all_to_all | solution.py:87
  25.4 1.5 fusion.24
  27.4 1.6 broadcast_in_dim.10
  29.1 6.8 %all-to-all-start.1 = ((bf16[16,4,16,1152]{3,2,1,0:T(8,128)(2,1)}), bf16[16,4,16,1152]{3,2,1,0:T(8,128)(2,1)S(1)}, u32[]{:S(2)}, u32[]{:S(2)}) async-start(bf16[16,4,16,1152]{3,2,1,0:T(8,128)(2,1)} %broadcast_in_dim.10), calls=%async_computation.1 | async-start | bytes 4718592 | tf_op jit(solution)/shard_map/all_to_all | solution.py:91
  36.0 15.0 %collective-permute-done = bf16[2,256,1024]{2,1,0:T(8,128)(2,1)} collective-permute-done((bf16[2,256,1024]{2,1,0:T(8,128)(2,1)}, bf16[2,256,1024]{2,1,0:T(8,128)(2,1)}, u32[]{:S(2)}, u32[]{:S(2)}) %collective-permute-start) | collective-permute-done | bytes 1048608 | tf_op jit(solution)/shard_map/ppermute | solution.py:50
  50.9 3.1 pad_maximum_fusion.1.pair_ref.inputs_ref.outer_ref
  54.0 1.8 collective-permute-start.1
  55.8 17.6 %all-to-all-done.1 = bf16[16,4,16,1152]{3,2,1,0:T(8,128)(2,1)S(1)} async-done(((bf16[16,4,16,1152]{3,2,1,0:T(8,128)(2,1)}), bf16[16,4,16,1152]{3,2,1,0:T(8,128)(2,1)S(1)}, u32[]{:S(2)}, u32[]{:S(2)}) %all-to-all-start.1) | async-done | bytes 2359328 | tf_op jit(solution)/shard_map/all_to_all | solution.py:91
  73.4 4.8 %shard_map.177 = (bf16[4,256,1024]{2,1,0:T(8,128)(2,1)S(1)}, f32[4,256,768]{2,1,0:T(8,128)S(1)}, bf16[4,256,256]{2,1,0:T(8,128)(2,1)S(1)}, bf16[1024,768]{1,0:T(...) custom-call(bf16[2,2,256,1024]{3,2,1,0:T(8,128)(2,1)} %pad_maximum_fusion.1.pair_ref.inp, ...), custom_call_target="tpu_custom_call" | custom-call | flops 4600000000 | tf_op jit(solution)/shard_map/pallas_call | solution.py:142
  78.2 1.6 copy-done.6
  79.8 1.3 copy-done.16
  81.2 1.2 copy-done.18
  82.3 1.6 collective-permute-start.2
  83.9 4.3 %collective-permute-done.2 = bf16[2,2,256]{2,1,0:T(2,128)(2,1)S(1)} collective-permute-done((bf16[2,2,256]{2,1,0:T(2,128)(2,1)S(1)}, bf16[2,2,256]{2,1,0:T(2,128)(2,1)S(1)}, u32[]{:S(2)}, u32[]{:S(2)}) %collective-permute-start.2) | collective-permute-done | bytes 2080 | tf_op jit(solution)/shard_map/ppermute | solution.py:577
  88.4 1.9 copy-done.7
  90.2 1.7 shard_map.178
  92.0 1.0 copy-done.10
  93.7 5.3 %collective-permute-start.3 = (bf16[2,256,1024]{2,1,0:T(8,128)(2,1)S(1)}, bf16[2,256,1024]{2,1,0:T(8,128)(2,1)S(1)}, u32[]{:S(2)}, u32[]{:S(2)}) collective-permute-start(bf16[2,256,1024]{2,1,0:T(8,128)(2,1)S(1)} %get-tuple-element.56), channel_id=1, source_target_pairs={{0,1},{1,0},{2,3},{3,2},{4,5},{5,4},{6,7},{7,6},{8,9},{9,8},{10,11... | collective-permute-start | bytes 3145736 | tf_op jit(solution)/shard_map/ppermute | solution.py:46
  99.1 2.3 collective-permute-done.3
  101.4 1.4 fusion.26
  103.6 13.1 %all-gather.2.cloned.1.call-done = bf16[2,512,3456]{2,1,0:T(8,128)(2,1)} async-done(((bf16[2,32,3456]{2,1,0:T(8,128)(2,1)}), bf16[2,512,3456]{2,1,0:T(8,128)(2,1)}) %all-gather.2.cloned.1.call-update) | async-done | bytes 7077904 | tf_op jit(solution)/shard_map/all_gather | solution.py:96
  117.6 1.8 slice.222
  119.7 1.6 pad_maximum_fusion
  121.3 6.2 %collective-permute-done.4.crossed_ref = bf16[2,256,1024]{2,1,0:T(8,128)(2,1)} collective-permute-done((bf16[2,256,1024]{2,1,0:T(8,128)(2,1)}, bf16[2,256,1024]{2,1,0:T(8,128)(2,1)}, u32[]{:S(2)}, u32[]{:S(2)}) %collective-permute-start.4) | collective-permute-done | bytes 1048608 | tf_op jit(solution)/shard_map/ppermute | solution.py:50
  127.5 1.9 shard_map.179
  129.3 1.4 copy-done
  130.7 1.2 collective-permute-start.5
  131.9 2.3 collective-permute-done.5.swap_ref
  134.2 17.8 %shard_map.180 = (bf16[4,256,1152]{2,1,0:T(8,128)(2,1)S(1)}, bf16[4,256,1152]{2,1,0:T(8,128)(2,1)S(1)}, bf16[4,256,1152]{2,1,0:T(8,128)(2,1)S(1)}, f32[2,256,1024]{2,1,0:T(8,128)S(1)}, bf16[2,256,1024]{2,1,0:T(8,128)(2,1)S(1)}) custom-call(bf16[2,256,1024]{2,1,0:T(8,128)(2,1)S(1)} %get-tuple-element.60.own_ref, ...), custom_call_target="tpu_custom_call" | custom-call | flops 19549999104 | tf_op jit(solution)/shard_map/pallas_call | solution.py:142
  152.9 1.5 copy-done.12
  154.4 1.4 copy-done.20
  155.8 1.4 copy-done.21
  157.2 13.9 %shard_map.181 = bf16[1024,3456]{1,0:T(8,128)(2,1)} custom-call(bf16[2,256,1024]{2,1,0:T(8,128)(2,1)S(1)} %get-tuple-element.60.own_ref, bf16[2,256,1024]{2,1,0:T(8,128)(2,1)S(1)} %collective-permute-done.5.swap_ref, bf16[2,2,256,1024]{3,2,1,0:T(8,128)(2,1)} %pad_maximum_fusion.1.pair_ref.inputs_ref.outer_ref, ...), custom_call_target="tpu_custom_call" | custom-call | flops 13799999488 | tf_op jit(solution)/shard_map/pallas_call | solution.py:142
  171.8 2.5 collective-permute-done.6
  176.7 4.4 %fusion = f32[4,256,1024]{2,1,0:T(8,128)} fusion(bf16[4,256,1152]{2,1,0:T(8,128)(2,1)S(1)} %copy-done.13, bf16[1152,1024]{1,0:T(8,128)(2,1)S(1)} %bitcast.113), kind=kOutput, calls=%fused_computation.1 | convolution fusion | flops 2415919104 | bytes 8912896 | tf_op jit(solution)/shard_map/dot_general | solution.py:661
  181.1 18.2 %collective-permute-done.7.crossed_ref = bf16[2,256,1024]{2,1,0:T(8,128)(2,1)S(1)} collective-permute-done((bf16[2,256,1024]{2,1,0:T(8,128)(2,1)S(1)}, bf16[2,256,1024]{2,1,0:T(8,128)(2,1)S(1)}, u32[]{:S(2)}, u32[]{:S(2)}) %collective-permute-start.7) | collective-permute-done | bytes 1048608 | tf_op jit(solution)/shard_map/ppermute | solution.py:50
  199.3 2.7 shard_map.182
  202.1 1.3 copy-done.3
  203.4 1.1 collective-permute-start.8
  204.4 2.3 collective-permute-done.8.swap_ref
  206.7 2.0 copy-done.8
  208.7 1.3 copy-done.11
  209.9 1.5 shard_map.183
  211.6 2.0 shard_map.184
  214.8 9.1 %shard_map.185 = (bf16[16,64,1152]{2,1,0:T(8,128)(2,1)}, f32[2,256,1024]{2,1,0:T(8,128)S(1)}, bf16[2,256,1024]{2,1,0:T(8,128)(2,1)S(1)}) custom-call(f32[4,256,256]{2,1,0:T(8,128)S(1)} %get-tuple-element.71.grad_conv_ref, f32[4,8,256]{2,1,0:T(8,128)S(1)} %select_maximum_fusion.later_ref, f32[4,256,768]{2,1,0:T(8,128)S(1)} %copy-done.9, ...), custom_call_target="tpu_custom_call" | custom-call | flops 9200000000 | tf_op jit(solution)/shard_map/pallas_call | solution.py:142
  225.1 1.0 slice.190
  226.2 4.5 %all-to-all-start.2 = ((bf16[16,4,16,1152]{3,2,1,0:T(8,128)(2,1)}), bf16[16,4,16,1152]{3,2,1,0:T(8,128)(2,1)}, u32[]{:S(2)}, u32[]{:S(2)}) async-start(bf16[16,4,16,1152]{3,2,1,0:T(8,128)(2,1)} %bitcast.34), calls=%async_computation.2 | async-start | bytes 4718592 | tf_op jit(solution)/shard_map/all_to_all | solution.py:91
  230.7 1.7 convert_add_fusion
  233.4 1.7 convert_add_fusion.1
  235.9 9.4 %collective-permute-done.13 = bf16[256,1024]{1,0:T(8,128)(2,1)S(1)} collective-permute-done((bf16[256,1024]{1,0:T(8,128)(2,1)S(1)}, bf16[256,1024]{1,0:T(8,128)(2,1)S(1)}, u32[]{:S(2)}, u32[]{:S(2)}) %collective-permute-start.13) | collective-permute-done | bytes 524320 | tf_op jit(solution)/shard_map/ppermute | solution.py:50
  245.8 10.8 %collective-permute-done.11 = bf16[256,1024]{1,0:T(8,128)(2,1)S(1)} collective-permute-done((bf16[256,1024]{1,0:T(8,128)(2,1)S(1)}, bf16[256,1024]{1,0:T(8,128)(2,1)S(1)}, u32[]{:S(2)}, u32[]{:S(2)}) %collective-permute-start.11) | collective-permute-done | bytes 524320 | tf_op jit(solution)/shard_map/ppermute | solution.py:50
  256.6 1.1 fusion.13
  257.6 1.3 fusion.7
  259.0 6.0 %all-to-all-done.2 = bf16[16,4,16,1152]{3,2,1,0:T(8,128)(2,1)} async-done(((bf16[16,4,16,1152]{3,2,1,0:T(8,128)(2,1)}), bf16[16,4,16,1152]{3,2,1,0:T(8,128)(2,1)}, u32[]{:S(2)}, u32[]{:S(2)}) %all-to-all-start.2) | async-done | bytes 2359328 | tf_op jit(solution)/shard_map/all_to_all | solution.py:91
  265.0 2.0 reduce_sum.32
  267.0 4.0 %reduce-scatter.2.cloned.1.call-done = bf16[2,32,3456]{2,1,0:T(8,128)(2,1)} async-done(((bf16[2,512,3456]{2,1,0:T(8,128)(2,1)}), bf16[2,32,3456]{2,1,0:T(8,128)(2,1)}) %reduce-scatter.2.cloned.1.call-update) | async-done | bytes 442384 | tf_op jit(solution)/shard_map/reduce_scatter | solution.py:107
  271.9 1.0 maximum_maximum_fusion
  272.9 6.9 %all-to-all-start.3 = ((bf16[8,16,3200]{2,1,0:T(8,128)(2,1)}), bf16[8,16,3200]{2,1,0:T(8,128)(2,1)S(1)}, u32[]{:S(2)}, u32[]{:S(2)}) async-start(bf16[8,16,3200]{2,1,0:T(8,128)(2,1)} %maximum_maximum_fusion), calls=%async_computation.4 | async-start | bytes 1638400 | tf_op jit(solution)/shard_map/all_to_all | solution.py:777
  280.8 11.7 %all-to-all-done.3.blocks_ref = bf16[8,16,3200]{2,1,0:T(8,128)(2,1)S(1)} async-done(((bf16[8,16,3200]{2,1,0:T(8,128)(2,1)}), bf16[8,16,3200]{2,1,0:T(8,128)(2,1)S(1)}, u32[]{:S(2)}, u32[]{:S(2)}) %all-to-all-start.3) | async-done | bytes 819232 | tf_op jit(solution)/shard_map/all_to_all | solution.py:777
  293.1 1.7 shard_map.186
  295.6 1.4 reshape.149
  297.9 1.4 reshape.151
  (143 shorter events, 24.1 us)
Async XLA Ops:
  7.2 3.1 %copy-start.28 = (bf16[16,4608]{1,0:T(8,128)(2,1)S(1)}, bf16[16,4608]{1,0:T(8,128)(2,1)}, u32[]{:S(2)}) copy-start(bf16[16,4608]{1,0:T(8,128)(2,1)} %param.17) | copy-start | bytes 442372
  9.5 1.7 copy-start.29
  10.9 13.6 %slice-start = ((bf16[72,1024]{1,0:T(8,128)(2,1)}), bf16[8,1024]{1,0:T(8,128)(2,1)S(1)}, s32[]{:S(2)}) async-start(bf16[72,1024]{1,0:T(8,128)(2,1)} %param.18), calls=%async_computation.7 | async-start | bytes 32768 | tf_op jit(solution)/shard_map/slice | solution.py:504
  10.9 13.6 %slice-start.1 = ((bf16[72,1024]{1,0:T(8,128)(2,1)}), bf16[64,1024]{1,0:T(8,128)(2,1)S(1)}, s32[]{:S(2)}) async-start(bf16[72,1024]{1,0:T(8,128)(2,1)} %param.18), calls=%async_computation.8 | async-start | bytes 262144 | tf_op jit(solution)/shard_map/slice | solution.py:503
  11.8 13.6 %copy-start.24 = (bf16[256,1024]{1,0:T(8,128)(2,1)S(1)}, bf16[256,1024]{1,0:T(8,128)(2,1)}, u32[]{:S(2)}) copy-start(bf16[256,1024]{1,0:T(8,128)(2,1)} %param.10) | copy-start | bytes 1572868
  11.8 13.6 %copy-start.27 = (bf16[256,1024]{1,0:T(8,128)(2,1)S(1)}, bf16[256,1024]{1,0:T(8,128)(2,1)}, u32[]{:S(2)}) copy-start(bf16[256,1024]{1,0:T(8,128)(2,1)} %param.19) | copy-start | bytes 1572868
  12.9 11.6 %all-to-all-start = ((bf16[4,16,3200]{2,1,0:T(8,128)(2,1)}), bf16[4,16,3200]{2,1,0:T(8,128)(2,1)S(1)}, u32[]{:S(2)}, u32[]{:S(2)}) async-start(bf16[4,16,3200]{2,1,0:T(8,128)(2,1)} %pad_maximum_fusion.4), calls=%async_computation | async-start | bytes 819200 | tf_op jit(solution)/shard_map/all_to_all | solution.py:87
  17.7 98.9 %all-gather.2.cloned.1.call-start = ((), (), s32[]{:S(2)}) async-start(), calls=%async_computation.5 | async-start | bytes 7520256 | tf_op jit(solution)/shard_map/all_gather | solution.py:96
  24.5 2.7 copy-start.31
  24.5 2.8 copy-start.30
  26.8 24.1 %collective-permute-start = (bf16[2,256,1024]{2,1,0:T(8,128)(2,1)}, bf16[2,256,1024]{2,1,0:T(8,128)(2,1)}, u32[]{:S(2)}, u32[]{:S(2)}) collective-permute-start(bf16[2,256,1024]{2,1,0:T(8,128)(2,1)} %get-tuple-element.103), channel_id=1, source_target_pairs={{0,32},{1,33},{2,34},{3,35},{4,36},{5,37},{6,38},{7,39},{8,40},{9,... | collective-permute-start | bytes 3145736 | tf_op jit(solution)/shard_map/ppermute | solution.py:50
  29.1 44.3 %all-to-all-start.1 = ((bf16[16,4,16,1152]{3,2,1,0:T(8,128)(2,1)}), bf16[16,4,16,1152]{3,2,1,0:T(8,128)(2,1)S(1)}, u32[]{:S(2)}, u32[]{:S(2)}) async-start(bf16[16,4,16,1152]{3,2,1,0:T(8,128)(2,1)} %broadcast_in_dim.10), calls=%async_computation.1 | async-start | bytes 4718592 | tf_op jit(solution)/shard_map/all_to_all | solution.py:91
  35.9 235.0 %reduce-scatter.2.cloned.1.call-start = ((), (), s32[]{:S(2)}) async-start(), calls=%async_computation.6 | async-start | bytes 7520256 | tf_op jit(solution)/shard_map/reduce_scatter | solution.py:107
  54.0 19.4 %collective-permute-start.1 = (bf16[2,2,256,1024]{3,2,1,0:T(8,128)(2,1)}, bf16[2,2,256,1024]{3,2,1,0:T(8,128)(2,1)}, u32[]{:S(2)}, u32[]{:S(2)}) collective-permute-start(bf16[2,2,256,1024]{3,2,1,0:T(8,128)(2,1)} %pad_maximum_fusion.1.pair_ref.inputs_ref.outer_ref), channel_id=1, source_target_pairs={{0,1},{1,0},{2,3},{3,2},{4,5},{5,4},{6,7},{7,6},{8,9},{9,8},{10,11... | collective-permute-start | bytes 6291464 | tf_op jit(solution)/shard_map/ppermute | solution.py:46
  78.2 1.7 copy-start.6
  79.8 1.3 copy-start.16
  81.2 1.2 copy-start.18
  82.3 5.9 %collective-permute-start.2 = (bf16[2,2,256]{2,1,0:T(2,128)(2,1)S(1)}, bf16[2,2,256]{2,1,0:T(2,128)(2,1)S(1)}, u32[]{:S(2)}, u32[]{:S(2)}) collective-permute-start(bf16[2,2,256]{2,1,0:T(2,128)(2,1)S(1)} %broadcast_select_fusion.7), channel_id=1, source_target_pairs={{0,2},{1,3},{2,4},{3,5},{4,6},{5,7},{6,8},{7,9},{8,10},{9,11},{10,... | collective-permute-start | bytes 6152 | tf_op jit(solution)/shard_map/ppermute | solution.py:577
  88.4 1.9 copy-start.7
  91.9 1.0 copy-start.10
  92.9 0.8 copy-start.14
  93.7 7.6 %collective-permute-start.3 = (bf16[2,256,1024]{2,1,0:T(8,128)(2,1)S(1)}, bf16[2,256,1024]{2,1,0:T(8,128)(2,1)S(1)}, u32[]{:S(2)}, u32[]{:S(2)}) collective-permute-start(bf16[2,256,1024]{2,1,0:T(8,128)(2,1)S(1)} %get-tuple-element.56), channel_id=1, source_target_pairs={{0,1},{1,0},{2,3},{3,2},{4,5},{5,4},{6,7},{7,6},{8,9},{9,8},{10,11... | collective-permute-start | bytes 3145736 | tf_op jit(solution)/shard_map/ppermute | solution.py:46
  102.8 24.7 %collective-permute-start.4 = (bf16[2,256,1024]{2,1,0:T(8,128)(2,1)}, bf16[2,256,1024]{2,1,0:T(8,128)(2,1)}, u32[]{:S(2)}, u32[]{:S(2)}) collective-permute-start(bf16[2,256,1024]{2,1,0:T(8,128)(2,1)} %get-tuple-element.98), channel_id=1, source_target_pairs={{0,32},{1,33},{2,34},{3,35},{4,36},{5,37},{6,38},{7,39},{8,40},{9,... | collective-permute-start | bytes 3145736 | tf_op jit(solution)/shard_map/ppermute | solution.py:50
  129.3 1.4 copy-start
  130.7 3.5 %collective-permute-start.5 = (bf16[2,256,1024]{2,1,0:T(8,128)(2,1)S(1)}, bf16[2,256,1024]{2,1,0:T(8,128)(2,1)S(1)}, u32[]{:S(2)}, u32[]{:S(2)}) collective-permute-start(bf16[2,256,1024]{2,1,0:T(8,128)(2,1)S(1)} %get-tuple-element.60.own_ref), channel_id=1, source_target_pairs={{0,1},{1,0},{2,3},{3,2},{4,5},{5,4},{6,7},{7,6},{8,9},{9,8},{10,11... | collective-permute-start | bytes 3145736 | tf_op jit(solution)/shard_map/ppermute | solution.py:46
  152.0 1.0 copy-start.5
  152.9 1.5 copy-start.12
  154.4 1.4 copy-start.20
  155.8 1.4 copy-start.21
  171.1 3.2 %collective-permute-start.6 = (bf16[2,256,1024]{2,1,0:T(8,128)(2,1)}, bf16[2,256,1024]{2,1,0:T(8,128)(2,1)S(1)}, u32[]{:S(2)}, u32[]{:S(2)}) collective-permute-start(bf16[2,256,1024]{2,1,0:T(8,128)(2,1)} %copy-done.5), channel_id=1, source_target_pairs={{0,1},{1,0},{2,3},{3,2},{4,5},{5,4},{6,7},{7,6},{8,9},{9,8},{10,11... | collective-permute-start | bytes 3145736 | tf_op jit(solution)/shard_map/ppermute | solution.py:46
  174.3 1.7 copy-start.13
  174.3 2.4 copy-start.26
  174.7 24.6 %copy-start.1 = (f32[2,256,1024]{2,1,0:T(8,128)S(1)}, f32[2,256,1024]{2,1,0:T(8,128)}, u32[]{:S(2)}) copy-start(f32[2,256,1024]{2,1,0:T(8,128)} %copy-done) | copy-start | bytes 6291460
  174.8 24.6 %collective-permute-start.7 = (bf16[2,256,1024]{2,1,0:T(8,128)(2,1)S(1)}, bf16[2,256,1024]{2,1,0:T(8,128)(2,1)S(1)}, u32[]{:S(2)}, u32[]{:S(2)}) collective-permute-start(bf16[2,256,1024]{2,1,0:T(8,128)(2,1)S(1)} %get-tuple-element.96), channel_id=1, source_target_pairs={{0,32},{1,33},{2,34},{3,35},{4,36},{5,37},{6,38},{7,39},{8,40},{9,... | collective-permute-start | bytes 3145736 | tf_op jit(solution)/shard_map/ppermute | solution.py:50
  202.1 1.3 copy-start.3
  203.4 3.4 %collective-permute-start.8 = (bf16[2,256,1024]{2,1,0:T(8,128)(2,1)S(1)}, bf16[2,256,1024]{2,1,0:T(8,128)(2,1)S(1)}, u32[]{:S(2)}, u32[]{:S(2)}) collective-permute-start(bf16[2,256,1024]{2,1,0:T(8,128)(2,1)S(1)} %get-tuple-element.69.own_ref), channel_id=1, source_target_pairs={{0,1},{1,0},{2,3},{3,2},{4,5},{5,4},{6,7},{7,6},{8,9},{9,8},{10,11... | collective-permute-start | bytes 3145736 | tf_op jit(solution)/shard_map/ppermute | solution.py:46
  206.7 2.0 copy-start.8
  208.7 1.3 copy-start.11
  209.9 1.6 copy-start.15
  211.5 2.9 collective-permute-start.9
  211.6 2.9 copy-start.9
  211.6 2.9 copy-start.17
  211.6 3.2 %copy-start.19 = (bf16[1024,768]{1,0:T(8,128)(2,1)S(1)}, bf16[1024,768]{1,0:T(8,128)(2,1)}, u32[]{:S(2)}) copy-start(bf16[1024,768]{1,0:T(8,128)(2,1)} %copy-done.18) | copy-start | bytes 4718596
  214.8 10.0 %copy-start.22 = (f32[4,256,1024]{2,1,0:T(8,128)S(1)}, f32[4,256,1024]{2,1,0:T(8,128)}, u32[]{:S(2)}) copy-start(f32[4,256,1024]{2,1,0:T(8,128)} %fusion) | copy-start | bytes 12582916
  223.9 6.8 %collective-permute-start.12 = (bf16[2,256,1024]{2,1,0:T(8,128)(2,1)S(1)}, bf16[2,256,1024]{2,1,0:T(8,128)(2,1)}, u32[]{:S(2)}, u32[]{:S(2)}) collective-permute-start(bf16[2,256,1024]{2,1,0:T(8,128)(2,1)S(1)} %get-tuple-element.83), channel_id=1, source_target_pairs={{0,1},{1,0},{2,3},{3,2},{4,5},{5,4},{6,7},{7,6},{8,9},{9,8},{10,11... | collective-permute-start | bytes 3145736 | tf_op jit(solution)/shard_map/ppermute | solution.py:46
  226.2 7.3 %collective-permute-start.10 = (bf16[2,256,1024]{2,1,0:T(8,128)(2,1)}, bf16[2,256,1024]{2,1,0:T(8,128)(2,1)}, u32[]{:S(2)}, u32[]{:S(2)}) collective-permute-start(bf16[2,256,1024]{2,1,0:T(8,128)(2,1)} %slice.190), channel_id=1, source_target_pairs={{0,1},{1,0},{2,3},{3,2},{4,5},{5,4},{6,7},{7,6},{8,9},{9,8},{10,11... | collective-permute-start | bytes 3145736 | tf_op jit(solution)/shard_map/ppermute | solution.py:46
  226.2 38.8 %all-to-all-start.2 = ((bf16[16,4,16,1152]{3,2,1,0:T(8,128)(2,1)}), bf16[16,4,16,1152]{3,2,1,0:T(8,128)(2,1)}, u32[]{:S(2)}, u32[]{:S(2)}) async-start(bf16[16,4,16,1152]{3,2,1,0:T(8,128)(2,1)} %bitcast.34), calls=%async_computation.2 | async-start | bytes 4718592 | tf_op jit(solution)/shard_map/all_to_all | solution.py:91
  230.7 2.7 copy-start.23
  232.5 12.9 %copy-start.25 = (bf16[256,1024]{1,0:T(8,128)(2,1)S(1)}, bf16[256,1024]{1,0:T(8,128)(2,1)}, u32[]{:S(2)}) copy-start(bf16[256,1024]{1,0:T(8,128)(2,1)} %param.10) | copy-start | bytes 1572868
  232.5 12.8 %collective-permute-start.13 = (bf16[256,1024]{1,0:T(8,128)(2,1)S(1)}, bf16[256,1024]{1,0:T(8,128)(2,1)S(1)}, u32[]{:S(2)}, u32[]{:S(2)}) collective-permute-start(bf16[256,1024]{1,0:T(8,128)(2,1)S(1)} %fusion.15), channel_id=1, source_target_pairs={{0,32},{1,33},{2,34},{3,35},{4,36},{5,37},{6,38},{7,39},{8,40},{9,... | collective-permute-start | bytes 1572872 | tf_op jit(solution)/shard_map/ppermute | solution.py:50
  235.1 21.5 %copy-start.2 = (f32[2,256,1024]{2,1,0:T(8,128)S(1)}, f32[2,256,1024]{2,1,0:T(8,128)}, u32[]{:S(2)}) copy-start(f32[2,256,1024]{2,1,0:T(8,128)} %copy-done) | copy-start | bytes 6291460
  235.2 21.4 %collective-permute-start.11 = (bf16[256,1024]{1,0:T(8,128)(2,1)S(1)}, bf16[256,1024]{1,0:T(8,128)(2,1)S(1)}, u32[]{:S(2)}, u32[]{:S(2)}) collective-permute-start(bf16[256,1024]{1,0:T(8,128)(2,1)S(1)} %fusion.14), channel_id=1, source_target_pairs={{0,32},{1,33},{2,34},{3,35},{4,36},{5,37},{6,38},{7,39},{8,40},{9,... | collective-permute-start | bytes 1572872 | tf_op jit(solution)/shard_map/ppermute | solution.py:50
  245.7 11.9 %copy-start.4 = (f32[2,256,1024]{2,1,0:T(8,128)S(1)}, f32[2,256,1024]{2,1,0:T(8,128)}, u32[]{:S(2)}) copy-start(f32[2,256,1024]{2,1,0:T(8,128)} %copy-done.3) | copy-start | bytes 6291460
  272.9 19.6 %all-to-all-start.3 = ((bf16[8,16,3200]{2,1,0:T(8,128)(2,1)}), bf16[8,16,3200]{2,1,0:T(8,128)(2,1)S(1)}, u32[]{:S(2)}, u32[]{:S(2)}) async-start(bf16[8,16,3200]{2,1,0:T(8,128)(2,1)} %maximum_maximum_fusion), calls=%async_computation.4 | async-start | bytes 1638400 | tf_op jit(solution)/shard_map/all_to_all | solution.py:777
  292.5 7.5 %collective-permute-start.14 = (bf16[4,16,1536]{2,1,0:T(8,128)(2,1)S(1)}, bf16[4,16,1536]{2,1,0:T(8,128)(2,1)S(1)}, u32[]{:S(2)}, u32[]{:S(2)}) collective-permute-start(bf16[4,16,1536]{2,1,0:T(8,128)(2,1)S(1)} %pad_maximum_fusion.6), channel_id=1, source_target_pairs={{0,64},{64,0},{1,65},{65,1},{2,66},{66,2},{3,67},{67,3},{4,68},{68... | collective-permute-start | bytes 589832 | tf_op jit(solution)/shard_map/ppermute | solution.py:766
Sparse Core Ops, SparseCore 0:
  25.5 91.1 all-gather.1
  171.2 99.6 reduce-scatter.1
